TPU v7x, 512 devices: a whole 4x8x8 slice. The times are simulated.
512 devices in a mesh: tower: 16 (over z, core), seq: 8 (over y), mp: 4 (over x).
Axes of the slice: x: 4, y: 8, z: 8, core: 2. Of those that a mesh axis runs over, the one named last changes fastest.
Arguments:
- tiles: bfloat16 [256, 8, 8, 3072], P(('tower', 'mp'), None, None, 'seq'), may hold values from -6 to 6
- dw_weight: float32 [7, 7, 3072], P(None, None, 'seq'), may hold values from -0.875 to 0.875
- dw_bias: float32 [3072], P('seq'), may hold values from -3 to 3
- block_gain: float32 [3072], P('seq'), may hold values from 0.5 to 1.5
- block_bias: float32 [3072], P('seq'), may hold values from -3 to 3
- proj_weight: bfloat16 [3072, 8192], P('seq', 'mp'), may hold values from -0.109375 to 0.109375
- proj_bias: float32 [8192], P('mp'), may hold values from -3 to 3
- directions: float32 [16, 8192], replicated, may hold values from 0.001 to 30
- dir_index: int32 [16], P('tower'), may hold values from 0 to 15
- tile_counts: int32 [16], P('tower'), may hold values from 1 to 16
- positions: int32 [16, 1024], P('tower', 'seq'), may hold values from 0 to 5118, as said below
- rms_gain: float32 [8192], P('mp'), may hold values from 0.5 to 1.5
- kv_weight: bfloat16 [2, 8192, 1024], P(None, 'tower', 'mp'), may hold values from -0.0625 to 0.0625
- kv_bias: float32 [2, 1024], P(None, 'mp'), may hold values from -3 to 3
Outputs:
- cache: bfloat16 [16, 2, 1024, 1024], P('tower', None, 'seq', 'mp')
Inputs may be any that keep to these rules, and one draw needn't show every extreme that they name: Each request's visual token slots take 1024 consecutive increasing positions.
All inputs are finite; a program needn't handle non-finite values.
Results may differ from a plain program's by a relative error of at most 0.02.
Values may be sent and summed in bfloat16 or wider, within the bound.
No kernel may reach another device: no remote copies, remote signals or barrier semaphores. Data moves between devices by JAX's collectives and lax.ppermute only.
A program may use at most 64 MiB of HBM per device.

v0:
```python
import jax
import jax.numpy as jnp
from jax import lax
from jax.sharding import PartitionSpec as P

C = 3072
D = 8192
HEAD = 128
SIDE = 8


epsilon = 1e-06


def depthwise(inputs, kernel, shift):
    reach = kernel.shape[0] // 2
    cells = inputs.shape[1]
    padded = jnp.pad(inputs, ((0, 0), (reach, reach), (reach, reach), (0, 0)))
    running = jnp.zeros_like(inputs) + shift
    for row_off in range(kernel.shape[0]):
        for col_off in range(kernel.shape[1]):
            running = (
                running
                + padded[:, row_off : row_off + cells, col_off : col_off + cells, :]
                * kernel[row_off, col_off]
            )
    return running


def rotate(key_rows, position):
    count_rows = key_rows.shape[0]
    heads = key_rows.reshape(count_rows, -1, HEAD)
    half_head = HEAD // 2
    inverse = jnp.power(
        jnp.float32(1000000.0), -(jnp.arange(half_head, dtype=jnp.float32) * 2.0 / HEAD)
    )
    angles = position.astype(jnp.float32)[:, None] * inverse[None, :]
    cosine = jnp.cos(angles)[:, None, :]
    sine_part = jnp.sin(angles)[:, None, :]
    leading = heads[..., :half_head]
    trailing = heads[..., half_head:]
    turned = jnp.concatenate(
        [leading * cosine - trailing * sine_part, trailing * cosine + leading * sine_part], axis=-1
    )
    return turned.reshape(count_rows, -1)


def local(
    tiles,
    dw_weight,
    dw_bias,
    block_gain,
    block_bias,
    proj_weight,
    proj_bias,
    directions,
    dir_index,
    tile_counts,
    positions,
    rms_gain,
    kv_weight,
    kv_bias,
):
    inputs = tiles.astype(jnp.float32)
    filtered = depthwise(inputs, dw_weight, dw_bias)
    row_sums, row_squares = lax.psum(
        (jnp.sum(filtered, -1), jnp.sum(filtered * filtered, -1)), "seq"
    )
    average = row_sums[..., None] / C
    variance = row_squares[..., None] / C - average * average
    normalized = (filtered - average) * lax.rsqrt(variance + epsilon) * block_gain + block_bias
    block_rows = normalized.astype(jnp.bfloat16).reshape(-1, inputs.shape[3])
    gathered = lax.all_gather(block_rows, "mp", axis=0, tiled=True)
    projected = lax.psum_scatter(
        jnp.dot(gathered, proj_weight, preferred_element_type=jnp.float32).astype(jnp.bfloat16),
        "seq",
        scatter_dimension=0,
        tiled=True,
    ).astype(jnp.float32)
    hidden = jax.nn.gelu(projected + proj_bias, approximate=False)
    column_count = hidden.shape[1]
    picked = jnp.arange(directions.shape[0], dtype=jnp.int32)[:, None] == dir_index[0]
    chosen = jnp.sum(jnp.where(picked, directions, 0.0), 0)
    unit_dir = chosen / jnp.sqrt(jnp.sum(chosen * chosen))
    local_unit = lax.dynamic_slice_in_dim(
        unit_dir, lax.axis_index("mp") * column_count, column_count, 0
    )
    along_unit = jnp.sum(hidden * local_unit, -1)
    coefficient = lax.psum(along_unit, "mp")
    ablated = hidden - coefficient[:, None] * local_unit
    mean_square = lax.psum(jnp.sum(ablated * ablated, -1), "mp") / D
    normed = (ablated * lax.rsqrt(mean_square + epsilon)[:, None] * rms_gain).astype(jnp.bfloat16)
    features = lax.all_gather(normed, "mp", axis=1, tiled=True)
    kv_pair = jnp.einsum(
        "td,kdh->kth",
        features,
        lax.all_gather(kv_weight, "tower", axis=1, tiled=True),
        preferred_element_type=jnp.float32,
    )
    key_rows = rotate(kv_pair[0] + kv_bias[0], positions[0])
    values = kv_pair[1] + kv_bias[1]
    rows_here = key_rows.shape[0]
    row_ids = lax.axis_index("seq") * rows_here + jnp.arange(rows_here, dtype=jnp.int32)
    row_valid = (row_ids // (SIDE * SIDE) < tile_counts[0]).astype(jnp.float32)[:, None]
    return (jnp.stack([key_rows, values]) * row_valid)[None].astype(jnp.bfloat16)


def solution(mesh):
    return jax.shard_map(
        local,
        mesh=mesh,
        in_specs=(
            P(("tower", "mp"), None, None, "seq"),
            P(None, None, "seq"),
            P("seq"),
            P("seq"),
            P("seq"),
            P("seq", "mp"),
            P("mp"),
            P(),
            P("tower"),
            P("tower"),
            P("tower", "seq"),
            P("mp"),
            P(None, "tower", "mp"),
            P(None, "mp"),
        ),
        out_specs=P("tower", None, "seq", "mp"),
        check_vma=False,
    )
```

profile of v0, /device:TPU:1, one launch (start us, length us, event | category | flops | bytes accessed | tf_op | source)
XLA Modules:
  0.0 256.3 jit_solution(10522788164269468827)
XLA Ops:
  6.5 1.2 slice_reduce_fusion.48
  7.8 1.1 slice_reduce_fusion.47
  8.9 1.0 slice_reduce_fusion.46
  9.8 1.0 convert_element_type.45
  10.8 3.5 %fusion.116 = (f32[4,8,8]{2,1,0:T(8,128)S(1)}, f32[4,8,8]{2,1,0:T(8,128)S(1)}, f32[4,8,8,384]{3,2,1,0:T(8,128)S(1)}) fusion(f32[384]{0:T(512)S(1)} %get-tuple-element.54, f32[384]{0:T(512)S(1)} %get-tuple-element.55, f32[384]{0:T(512)S(1)} %get-tuple-element.8, f32[384]{0:T(512)S(1)} %get-tuple-element.9, f32[384]{0:T(512)S(1)} %get-tuple-element.10, ...), kind=kLoop, calls=%fused_computation.249 | loop fusion | flops 9928192 | bytes 865280 | tf_op jit(solution)/shard_map/reduce_sum | solution.py:67
  14.3 24.2 %all-reduce.1 = (f32[4,8,8]{2,1,0:T(8,128)S(1)}, f32[4,8,8]{2,1,0:T(8,128)S(1)}) all-reduce(f32[4,8,8]{2,1,0:T(8,128)S(1)} %get-tuple-element.6, f32[4,8,8]{2,1,0:T(8,128)S(1)} %get-tuple-element.5), channel_id=1, replica_groups=mesh['tower'=16,'seq'=8,'mp'=4] {'seq'}, use_global_device_ids=true, to_apply=%region_3.4 | all-reduce | flops 512 | bytes 4096 | tf_op jit(solution)/shard_map/psum | solution.py:66
  38.5 0.8 add_convert_fusion
  39.4 10.9 %all_gather.9 = bf16[1024,384]{1,0:T(8,128)(2,1)S(1)} all-gather(bf16[256,384]{1,0:T(8,128)(2,1)S(1)} %bitcast.25), channel_id=1, replica_groups=mesh['tower'=16,'seq'=8,'mp'=4] {'mp'}, dimensions={0}, use_global_device_ids=true | all-gather | bytes 983040 | tf_op jit(solution)/shard_map/all_gather | solution.py:73
  50.3 4.3 %convolution_convert_fusion = bf16[1024,2048]{1,0:T(8,128)(2,1)} fusion(bf16[1024,384]{1,0:T(8,128)(2,1)S(1)} %all_gather.9, bf16[384,2048]{1,0:T(8,128)(2,1)S(1)} %copy-done), kind=kOutput, calls=%fused_computation.48 | convolution fusion | flops 1612709888 | bytes 6553600 | tf_op jit(solution)/shard_map/dot_general | solution.py:75
  54.6 0.0 reduce-scatter.2.cloned.1.call-update
  54.6 0.0 all-gather.3.cloned.1.call-start
  55.4 0.3 copy-done.1
  55.6 0.2 select_reduce_fusion
  55.8 0.6 multiply_reduce_fusion.3
  57.1 66.3 %reduce-scatter.2.cloned.1.call-done = bf16[128,2048]{1,0:T(8,128)(2,1)} async-done(((bf16[1024,2048]{1,0:T(8,128)(2,1)}), bf16[128,2048]{1,0:T(8,128)(2,1)}) %reduce-scatter.2.cloned.1.call-update) | async-done | bytes 524304 | tf_op jit(solution)/shard_map/reduce_scatter | solution.py:74
  123.4 3.5 %multiply_reduce_fusion.1 = (f32[128]{0:T(128)S(1)}, f32[128,2048]{1,0:T(8,128)S(1)}) fusion(f32[2048]{0:T(1024)S(1)} %dynamic-slice_divide_fusion, f32[2048]{0:T(1024)S(1)} %copy-done.2, bf16[128,2048]{1,0:T(8,128)(2,1)} %reduce-scatter.2.cloned.1.call-done), kind=kLoop, calls=%fused_computation.58 | loop fusion | flops 17825664 | bytes 1589760 | tf_op jit(solution)/shard_map/reduce_sum | solution.py:88
  126.9 8.4 %psum.30 = f32[128]{0:T(128)S(1)} all-reduce(f32[128]{0:T(128)S(1)} %get-tuple-element.58), channel_id=1, replica_groups=mesh['tower'=16,'seq'=8,'mp'=4] {'mp'}, use_global_device_ids=true, to_apply=%region_8.9 | all-reduce | flops 128 | bytes 1024 | tf_op jit(solution)/shard_map/psum | solution.py:89
  135.3 0.3 multiply_reduce_fusion
  135.6 6.0 %psum.31 = f32[128]{0:T(128)S(1)} all-reduce(f32[128]{0:T(128)S(1)} %multiply_reduce_fusion), channel_id=1, replica_groups=mesh['tower'=16,'seq'=8,'mp'=4] {'mp'}, use_global_device_ids=true, to_apply=%region_10.11 | all-reduce | flops 128 | bytes 1024 | tf_op jit(solution)/shard_map/psum | solution.py:91
  141.6 1.2 multiply_convert_fusion
  142.8 0.0 all-gather.3.cloned.1.call-update
  142.8 0.0 all-gather.5.cloned.1.call-start
  142.9 0.7 all-gather.5.cloned.1.call-update
  144.3 0.3 multiply_cosine_fusion
  144.6 36.4 %all-gather.3.cloned.1.call-done = bf16[128,8192]{1,0:T(8,128)(2,1)} async-done(((bf16[128,2048]{1,0:T(8,128)(2,1)}), bf16[128,8192]{1,0:T(8,128)(2,1)}) %all-gather.3.cloned.1.call-update) | async-done | bytes 2097168 | tf_op jit(solution)/shard_map/all_gather | solution.py:93
  181.0 62.0 %all-gather.5.cloned.1.call-done = bf16[2,8192,256]{2,1,0:T(8,128)(2,1)} async-done(((bf16[2,512,256]{2,1,0:T(8,128)(2,1)}), bf16[2,8192,256]{2,1,0:T(8,128)(2,1)}) %all-gather.5.cloned.1.call-update) | async-done | bytes 8388624 | tf_op jit(solution)/shard_map/all_gather | solution.py:97
  243.0 5.3 %fusion.2 = f32[2,128,256]{2,1,0:T(8,128)S(1)} fusion(bf16[2,8192,256]{2,1,0:T(8,128)(2,1)} %all-gather.5.cloned.1.call-done, bf16[128,8192]{1,0:T(8,128)(2,1)} %all-gather.3.cloned.1.call-done), kind=kOutput, calls=%fused_computation.52 | convolution fusion | flops 1073741824 | bytes 10747904 | tf_op jit(solution)/shard_map/td,kdh->kth/dot_general | solution.py:94
  248.3 0.1 squeeze.12
  248.4 0.3 multiply_subtract_fusion.1
  248.7 0.2 pad_maximum_fusion
  249.0 0.1 stack.8
  249.1 0.7 fusion.114
  (23 shorter events, 0.1 us)
Async XLA Ops:
  6.5 43.8 %copy-start = (bf16[384,2048]{1,0:T(8,128)(2,1)S(1)}, bf16[384,2048]{1,0:T(8,128)(2,1)}, u32[]{:S(2)}) copy-start(bf16[384,2048]{1,0:T(8,128)(2,1)} %param.19) | copy-start | bytes 4718596
  6.5 116.8 %reduce-scatter.2.cloned.1.call-start = ((), (), s32[]{:S(2)}) async-start(), calls=%async_computation.1 | async-start | bytes 4718592 | tf_op jit(solution)/shard_map/reduce_scatter | solution.py:74
  54.6 1.1 copy-start.1
  54.6 68.8 %copy-start.2 = (f32[2048]{0:T(1024)S(1)}, f32[2048]{0:T(1024)}, u32[]{:S(2)}) copy-start(f32[2048]{0:T(1024)} %param.20) | copy-start | bytes 24580
  54.6 87.0 %copy-start.3 = (f32[2048]{0:T(1024)S(1)}, f32[2048]{0:T(1024)}, u32[]{:S(2)}) copy-start(f32[2048]{0:T(1024)} %param.25) | copy-start | bytes 24580
  54.6 126.4 %all-gather.3.cloned.1.call-start = ((), (), s32[]{:S(2)}) async-start(), calls=%async_computation.2 | async-start | bytes 2621440 | tf_op jit(solution)/shard_map/all_gather | solution.py:93
  126.9 17.4 %copy-start.5 = (s32[1,128]{1,0:T(1,128)S(1)}, s32[1,128]{1,0:T(1,128)}, u32[]{:S(2)}) copy-start(s32[1,128]{1,0:T(1,128)} %param.24) | copy-start | bytes 1540
  126.9 17.4 %copy-start.4 = (f32[2,256]{1,0:T(2,128)S(1)}, f32[2,256]{1,0:T(2,128)}, u32[]{:S(2)}) copy-start(f32[2,256]{1,0:T(2,128)} %param.27) | copy-start | bytes 6148
  142.8 100.2 %all-gather.5.cloned.1.call-start = ((), (), s32[]{:S(2)}) async-start(), calls=%async_computation.3 | async-start | bytes 8912896 | tf_op jit(solution)/shard_map/all_gather | solution.py:97
Sparse Core Ops, SparseCore 0:
  54.7 68.6 reduce-scatter.1
  143.0 38.0 all-gather.2
  183.2 59.8 all-gather.4
where the time goes:
time: 257 us; the launch traced here: 256 us
  waiting for transfers between devices  165 us (64%)
  blocking collectives  49.6 us (19%)
  between operations  15.3 us (6%)
  other arithmetic  12.6 us (5%)
  matrix products  9.54 us (4%)
  local copies, waits for them, and re-layouts  3.76 us (1%)
    reduce_scatter x1, waiting for transfers between devices, local(): lax.psum_scatter(jnp.dot(gathered, proj_weight, preferred_element_type=jn...  66.3 us
    all_gather x1, waiting for transfers between devices, local(): lax.all_gather(kv_weight, 'tower', axis=1, tiled=True)  62 us
    all_gather x1, waiting for transfers between devices, local(): features = lax.all_gather(normed, 'mp', axis=1, tiled=True)  36.4 us
    psum x1, blocking collectives, local(): lax.psum((jnp.sum(filtered, -1), jnp.sum(filtered * filtered, -1)), 'seq')  24.2 us
    all_gather x1, blocking collectives, local(): gathered = lax.all_gather(block_rows, 'mp', axis=0, tiled=True)  10.9 us
    psum x1, blocking collectives, local(): coefficient = lax.psum(along_unit, 'mp')  8.42 us
    psum x1, blocking collectives, local(): mean_square = lax.psum(jnp.sum(ablated * ablated, -1), 'mp') / D  6 us
    dot_general x1, matrix products, local(): jnp.einsum('td,kdh->kth', features, lax.all_gather(kv_weight, 'tower', ax...  5.26 us
  transfers between devices with their start and end apart: 3, of which 3 were waited for; matrix products, arithmetic and copies ran while one was open for 0% of the time, Pallas kernels for 0%

commit v1 on v0

--- a/solution.py
+++ b/solution.py
@@ -1,6 +1,8 @@
 import jax
 import jax.numpy as jnp
 from jax import lax
+from jax.experimental import pallas as pl
+from jax.experimental.pallas import tpu as pltpu
 from jax.sharding import PartitionSpec as P
 
 C = 3072
@@ -43,6 +45,50 @@
         [leading * cosine - trailing * sine_part, trailing * cosine + leading * sine_part], axis=-1
     )
     return turned.reshape(count_rows, -1)
+
+
+def split_dot(rows, weight):
+    parts = []
+    rest = rows
+    for _ in range(3):
+        part = lax.reduce_precision(rest, 8, 7)
+        parts.append(part)
+        rest = rest - part
+    stacked = jnp.concatenate(parts, 0).astype(jnp.bfloat16)
+    out = jnp.dot(stacked, weight, preferred_element_type=jnp.float32)
+    count = rows.shape[0]
+    return out[:count] + out[count : 2 * count] + out[2 * count :]
+
+
+def kv_kernel(rows_ref, weight_ref, out_ref):
+    blocks, _, depth, width = weight_ref.shape
+    for pair in range(2):
+        total = jnp.zeros((rows_ref.shape[0], width), jnp.float32)
+        for block in range(blocks):
+            total = total + jnp.dot(
+                rows_ref[:, block * depth : (block + 1) * depth],
+                weight_ref[block, pair],
+                preferred_element_type=jnp.float32,
+            )
+        out_ref[0, :, pair * width : (pair + 1) * width] = total.astype(out_ref.dtype)
+
+
+def kv_partial(rows, weight):
+    count = rows.shape[0]
+    _, pairs, depth, width = weight.shape
+    blocks = rows.shape[1] // depth
+    groups = weight.shape[0] // blocks
+    return pl.pallas_call(
+        kv_kernel,
+        grid=(groups,),
+        in_specs=[
+            pl.BlockSpec((count, rows.shape[1]), lambda g: (0, 0)),
+            pl.BlockSpec((blocks, pairs, depth, width), lambda g: (g, 0, 0, 0)),
+        ],
+        out_specs=pl.BlockSpec((1, count, pairs * width), lambda g: (g, 0, 0)),
+        out_shape=jax.ShapeDtypeStruct((groups, count, pairs * width), jnp.bfloat16),
+        compiler_params=pltpu.CompilerParams(vmem_limit_bytes=56 * 2**20),
+    )(rows, weight)
 
 
 def local(
@@ -61,45 +107,91 @@
     kv_weight,
     kv_bias,
 ):
+    n_seq = lax.axis_size("seq")
+    n_mp = lax.axis_size("mp")
+    n_tower = lax.axis_size("tower")
+    inner = n_tower // n_mp
+    swap = [
+        ((a * inner + b) * n_mp + x, (x * inner + b) * n_mp + a)
+        for a in range(n_mp)
+        for b in range(inner)
+        for x in range(n_mp)
+    ]
+    swapped = lax.ppermute(kv_weight, ("tower", "mp"), swap)
+
     inputs = tiles.astype(jnp.float32)
     filtered = depthwise(inputs, dw_weight, dw_bias)
-    row_sums, row_squares = lax.psum(
-        (jnp.sum(filtered, -1), jnp.sum(filtered * filtered, -1)), "seq"
-    )
-    average = row_sums[..., None] / C
-    variance = row_squares[..., None] / C - average * average
-    normalized = (filtered - average) * lax.rsqrt(variance + epsilon) * block_gain + block_bias
-    block_rows = normalized.astype(jnp.bfloat16).reshape(-1, inputs.shape[3])
+    channels = inputs.shape[3]
+    mean_here = jnp.sum(filtered, -1) / channels
+    centered = filtered - mean_here[..., None]
+    square_here = jnp.sum(centered * centered, -1)
+    block_rows = (centered * block_gain).astype(jnp.bfloat16).reshape(-1, channels)
     gathered = lax.all_gather(block_rows, "mp", axis=0, tiled=True)
-    projected = lax.psum_scatter(
-        jnp.dot(gathered, proj_weight, preferred_element_type=jnp.float32).astype(jnp.bfloat16),
-        "seq",
-        scatter_dimension=0,
-        tiled=True,
-    ).astype(jnp.float32)
-    hidden = jax.nn.gelu(projected + proj_bias, approximate=False)
-    column_count = hidden.shape[1]
+    gathered, swapped = lax.optimization_barrier((gathered, swapped))
+    kv_rows = lax.all_gather(swapped, "tower", axis=0, tiled=False)
+    partial = jnp.dot(gathered, proj_weight, preferred_element_type=jnp.float32).astype(
+        jnp.bfloat16
+    )
+    vectors = split_dot(jnp.stack([block_gain, block_bias]), proj_weight)
+    partial, mean_here, square_here, vectors = lax.optimization_barrier(
+        (partial, mean_here, square_here, vectors)
+    )
+    summed = lax.psum_scatter(partial, "seq", scatter_dimension=0, tiled=True)
+
+    stats = jnp.stack([mean_here.reshape(-1), square_here.reshape(-1)])
+    stats = lax.all_gather(stats, "mp", axis=1, tiled=True)
+    rows_here = stats.shape[1] // n_seq
+    stats = stats.reshape(2, n_seq, rows_here).swapaxes(0, 1).reshape(n_seq, -1)
+    payload = jnp.concatenate(
+        [stats, jnp.broadcast_to(vectors.reshape(1, -1), (n_seq, vectors.size))], 1
+    )
+    payload = lax.all_to_all(payload, "seq", 0, 0, tiled=True)
+    means = payload[:, :rows_here]
+    squares = payload[:, rows_here : 2 * rows_here]
+    column_count = vectors.shape[1]
+    gain_rows = payload[:, 2 * rows_here : 2 * rows_here + column_count]
+    bias_row = jnp.sum(payload[:, 2 * rows_here + column_count :], 0) + proj_bias
+    average = jnp.sum(means, 0) / n_seq
+    offsets = means - average
+    variance = (jnp.sum(squares, 0) + channels * jnp.sum(offsets * offsets, 0)) / C
+    inverse_std = lax.rsqrt(variance + epsilon)
+    shift = jnp.dot(offsets.T, gain_rows, precision=lax.Precision.HIGHEST)
+
     picked = jnp.arange(directions.shape[0], dtype=jnp.int32)[:, None] == dir_index[0]
     chosen = jnp.sum(jnp.where(picked, directions, 0.0), 0)
     unit_dir = chosen / jnp.sqrt(jnp.sum(chosen * chosen))
     local_unit = lax.dynamic_slice_in_dim(
         unit_dir, lax.axis_index("mp") * column_count, column_count, 0
     )
+    unit_square = jnp.sum(local_unit * local_unit)
+
+    projected = (summed.astype(jnp.float32) + shift) * inverse_std[:, None]
+    hidden = jax.nn.gelu(projected + bias_row, approximate=False)
     along_unit = jnp.sum(hidden * local_unit, -1)
-    coefficient = lax.psum(along_unit, "mp")
-    ablated = hidden - coefficient[:, None] * local_unit
-    mean_square = lax.psum(jnp.sum(ablated * ablated, -1), "mp") / D
+    part = along_unit / unit_square
+    across = hidden - part[:, None] * local_unit
+    across_square = jnp.sum(across * across, -1)
+    norms = lax.all_gather(
+        jnp.concatenate([along_unit, across_square, jnp.broadcast_to(unit_square, (128,))]),
+        "mp",
+        axis=0,
+        tiled=False,
+    )
+    along_all = norms[:, :rows_here]
+    across_all = norms[:, rows_here : 2 * rows_here]
+    unit_all = norms[:, 2 * rows_here : 2 * rows_here + 1]
+    coefficient = jnp.sum(along_all, 0)
+    left = along_all / unit_all - coefficient
+    mean_square = (jnp.sum(across_all, 0) + jnp.sum(left * left * unit_all, 0)) / D
+    ablated = across + (part - coefficient)[:, None] * local_unit
     normed = (ablated * lax.rsqrt(mean_square + epsilon)[:, None] * rms_gain).astype(jnp.bfloat16)
-    features = lax.all_gather(normed, "mp", axis=1, tiled=True)
-    kv_pair = jnp.einsum(
-        "td,kdh->kth",
-        features,
-        lax.all_gather(kv_weight, "tower", axis=1, tiled=True),
-        preferred_element_type=jnp.float32,
-    )
-    key_rows = rotate(kv_pair[0] + kv_bias[0], positions[0])
-    values = kv_pair[1] + kv_bias[1]
-    rows_here = key_rows.shape[0]
+
+    pieces = kv_partial(normed, kv_rows)
+    pieces = lax.all_to_all(pieces, "mp", 0, 0, tiled=True)
+    kv_pair = jnp.sum(pieces.astype(jnp.float32), 0)
+    width = kv_bias.shape[1]
+    key_rows = rotate(kv_pair[:, :width] + kv_bias[0], positions[0])
+    values = kv_pair[:, width:] + kv_bias[1]
     row_ids = lax.axis_index("seq") * rows_here + jnp.arange(rows_here, dtype=jnp.int32)
     row_valid = (row_ids // (SIDE * SIDE) < tile_counts[0]).astype(jnp.float32)[:, None]
     return (jnp.stack([key_rows, values]) * row_valid)[None].astype(jnp.bfloat16)

time: 257 us -> 166 us (0.65); the launches traced: 256 us -> 163 us
  waiting for transfers between devices: 165 us -> 51.1 us
  starting transfers between devices: 0.09 us -> 12.2 us
  Pallas kernels: 0 us -> 5.72 us
    all_gather x2 -> x1, waiting for transfers between devices: 98.4 us -> 0.01 us  [local(): kv_rows = lax.all_gather(swapped, 'tower', axis=0, tiled=False)]
    psum x3 -> x0, blocking collectives: 38.7 us -> none  [the longest x1 24.2 us: local(): lax.psum((jnp.sum(filtered, -1), jnp.sum(filtered * filtered, -1)), 'seq')]
    reduce_scatter x1, waiting for transfers between devices: 66.3 us -> 35.8 us  [local(): summed = lax.psum_scatter(partial, 'seq', scatter_dimension=0, tiled=True)]
    all_gather x1, blocking collectives: 10.9 us -> 33.1 us  [local(): gathered = lax.all_gather(block_rows, 'mp', axis=0, tiled=True)]
    all_gather x0 -> x2, blocking collectives: none -> 18 us  [the longest x1 9.54 us: local(): stats = lax.all_gather(stats, 'mp', axis=1, tiled=True)]
    all_to_all x0 -> x2, waiting for transfers between devices: none -> 14.7 us  [the longest x1 8.84 us: local(): payload = lax.all_to_all(payload, 'seq', 0, 0, tiled=True)]
    all_to_all x0 -> x2, starting transfers between devices: none -> 10.3 us  [the longest x1 6.83 us: local(): payload = lax.all_to_all(payload, 'seq', 0, 0, tiled=True)]
    pallas_call x0 -> x1, Pallas kernels: none -> 5.72 us  [kv_partial(): pl.pallas_call(kv_kernel, grid=(groups,), in_specs=[pl.BlockSpec((count,...]
  transfers between devices with their start and end apart: 3 -> 5, of which waited for: 3 -> 3; matrix products, arithmetic and copies ran while one was open for 0% -> 12% of each run, Pallas kernels for 0% -> 0%
where the time goes in v1:
time: 166 us; the launch traced here: 163 us
  blocking collectives  51.1 us (31%)
  waiting for transfers between devices  51.1 us (31%)
  between operations  17.1 us (10%)
  starting transfers between devices  12.2 us (7%)
  other arithmetic  10.8 us (7%)
  matrix products  9.23 us (6%)
  Pallas kernels  5.72 us (3%)
  local copies, waits for them, and re-layouts  5.33 us (3%)
    reduce_scatter x1, waiting for transfers between devices, local(): summed = lax.psum_scatter(partial, 'seq', scatter_dimension=0, tiled=True)  35.8 us
    all_gather x1, blocking collectives, local(): gathered = lax.all_gather(block_rows, 'mp', axis=0, tiled=True)  33.1 us
    all_gather x1, blocking collectives, local(): stats = lax.all_gather(stats, 'mp', axis=1, tiled=True)  9.54 us
    all_to_all x1, waiting for transfers between devices, local(): payload = lax.all_to_all(payload, 'seq', 0, 0, tiled=True)  8.84 us
    all_gather x1, blocking collectives, local(): lax.all_gather(jnp.concatenate([along_unit, across_square, jnp.broadcast_...  8.41 us
    all_to_all x1, starting transfers between devices, local(): payload = lax.all_to_all(payload, 'seq', 0, 0, tiled=True)  6.83 us
    all_to_all x1, waiting for transfers between devices, local(): pieces = lax.all_to_all(pieces, 'mp', 0, 0, tiled=True)  5.9 us
    pallas_call x1, Pallas kernels, kv_partial(): pl.pallas_call(kv_kernel, grid=(groups,), in_specs=[pl.BlockSpec((count,...  5.72 us
  transfers between devices with their start and end apart: 5, of which 3 were waited for; matrix products, arithmetic and copies ran while one was open for 12% of the time, Pallas kernels for 0%

profile of v1, /device:TPU:1, one launch (start us, length us, event | category | flops | bytes accessed | tf_op | source)
XLA Modules:
  0.0 162.6 jit_solution(17259567259311665848)
XLA Ops:
  7.4 1.8 %collective-permute-start = (bf16[2,512,256]{2,1,0:T(8,128)(2,1)}, bf16[2,512,256]{2,1,0:T(8,128)(2,1)S(1)}, u32[]{:S(2)}, u32[]{:S(2)}) collective-permute-start(bf16[2,512,256]{2,1,0:T(8,128)(2,1)} %param.26), channel_id=1, source_target_pairs={{0,0},{1,128},{2,256},{3,384},{32,32},{33,160},{34,288},{35,416},{... | collective-permute-start | bytes 1572872 | tf_op jit(solution)/shard_map/ppermute | solution.py:120
  9.2 1.2 slice_reduce_fusion.54
  10.4 1.2 slice_reduce_fusion.53
  11.6 1.0 slice_reduce_fusion.52
  12.6 1.0 convert_element_type.49
  13.6 3.4 %fusion.121 = (f32[4,8,8]{2,1,0:T(8,128)S(1)}, f32[4,8,8,384]{3,2,1,0:T(8,128)S(1)}) fusion(f32[384]{0:T(512)S(1)} %get-tuple-element.66, f32[384]{0:T(512)S(1)} %get-tuple-element.67, f32[384]{0:T(512)S(1)} %get-tuple-element.20, f32[384]{0:T(512)S(1)} %get-tuple-element.21, f32[384]{0:T(512)S(1)} %get-tuple-element.22, f32[384]{0:T(512)S(1)} %get-tuple-element.23, ...), kind=kLoop, calls=%fused_computation.283 | loop fusion | flops 9731840 | bytes 864256 | tf_op jit(solution)/shard_map/reduce_sum | solution.py:125
  17.0 0.2 multiply_reduce_fusion.2
  17.2 33.1 %all_gather.18 = bf16[1024,384]{1,0:T(8,128)(2,1)S(1)} all-gather(bf16[256,384]{1,0:T(8,128)(2,1)S(1)} %bitcast.33), channel_id=1, replica_groups=mesh['tower'=16,'seq'=8,'mp'=4] {'mp'}, dimensions={0}, use_global_device_ids=true | all-gather | bytes 983040 | tf_op jit(solution)/shard_map/all_gather | solution.py:129
  50.4 0.3 fusion.111
  50.7 4.3 %convolution_convert_fusion = bf16[1024,2048]{1,0:T(8,128)(2,1)} fusion(bf16[1024,384]{1,0:T(8,128)(2,1)S(1)} %all_gather.18, bf16[384,2048]{1,0:T(8,128)(2,1)S(1)} %copy-done), kind=kOutput, calls=%fused_computation.48 | convolution fusion | flops 1612709888 | bytes 6553600 | tf_op jit(solution)/shard_map/dot_general | solution.py:132
  55.2 0.5 all-gather.5.cloned.1.call-update
  56.5 0.6 multiply_reduce_fusion.3
  58.0 9.5 %all_gather.19 = f32[2,1024]{1,0:T(2,128)S(1)} all-gather(f32[2,256]{1,0:T(2,128)S(1)} %pad_maximum_fusion.3), channel_id=1, replica_groups=mesh['tower'=16,'seq'=8,'mp'=4] {'mp'}, dimensions={1}, use_global_device_ids=true | all-gather | bytes 10240 | tf_op jit(solution)/shard_map/all_gather | solution.py:142
  67.6 0.8 all_to_all.11
  68.4 6.8 %all-to-all-start = ((f32[8,1,4352]{2,1,0:T(1,128)}), f32[8,1,4352]{2,1,0:T(1,128)S(1)}, u32[]{:S(2)}, u32[]{:S(2)}) async-start(f32[8,1,4352]{2,1,0:T(1,128)} %all_to_all.11), calls=%async_computation.1 | async-start | bytes 278528 | tf_op jit(solution)/shard_map/all_to_all | solution.py:148
  75.2 0.6 multiply_reduce_fusion.4
  75.8 8.8 %all-to-all-done = f32[8,1,4352]{2,1,0:T(1,128)S(1)} async-done(((f32[8,1,4352]{2,1,0:T(1,128)}), f32[8,1,4352]{2,1,0:T(1,128)S(1)}, u32[]{:S(2)}, u32[]{:S(2)}) %all-to-all-start) | async-done | bytes 139296 | tf_op jit(solution)/shard_map/all_to_all | solution.py:148
  84.8 35.8 %reduce-scatter.2.cloned.1.call-done = bf16[128,2048]{1,0:T(8,128)(2,1)} async-done(((bf16[1024,2048]{1,0:T(8,128)(2,1)}), bf16[128,2048]{1,0:T(8,128)(2,1)}) %reduce-scatter.2.cloned.1.call-update) | async-done | bytes 524304 | tf_op jit(solution)/shard_map/reduce_scatter | solution.py:139
  120.6 4.6 %multiply_reduce_fusion.1 = (f32[128]{0:T(128)S(1)}, f32[128,2048]{1,0:T(8,128)S(1)}) fusion(f32[2048]{0:T(1024)S(1)} %get-tuple-element.71, f32[2048]{0:T(1024)S(1)} %add.303, f32[128]{0:T(128)S(1)} %add_rsqrt_fusion.1, f32[8,4352]{1,0:T(8,128)S(1)} %bitcast.37, f32[128]{0:T(128)S(1)} %broadcast_multiply_fusion.1, ...), kind=kOutput, calls=%fused_computation.59 | convolution fusion | flops 43516800 | bytes 1660416 | tf_op jit(solution)/shard_map/dot_general | solution.py:158
  125.2 0.7 broadcast_divide_fusion
  125.9 0.3 multiply_reduce_fusion
  126.2 0.7 div.79
  126.9 8.4 %all-gather.2 = f32[4,1,384]{2,1,0:T(1,128)S(1)} all-gather(f32[1,1,384]{2,1,0:T(1,128)S(1)} %reshape.228), channel_id=2, replica_groups=mesh['tower'=16,'seq'=8,'mp'=4] {'mp'}, dimensions={0}, use_global_device_ids=true | all-gather | bytes 7680 | tf_op jit(solution)/shard_map/all_gather | solution.py:174
  135.5 0.7 fusion.127
  136.2 1.3 multiply_convert_fusion.rows_ref
  137.5 5.7 %shard_map.136 = bf16[4,128,512]{2,1,0:T(8,128)(2,1)} custom-call(bf16[128,2048]{1,0:T(8,128)(2,1)} %multiply_convert_fusion.rows_ref, bf16[16,2,512,256]{3,2,1,0:T(8,128)(2,1)} %bitcast.32), custom_call_target="tpu_custom_call" | custom-call | tf_op jit(solution)/shard_map/pallas_call | solution.py:81
  143.3 3.5 %all-to-all-start.1 = ((bf16[4,128,512]{2,1,0:T(8,128)(2,1)}), bf16[4,128,512]{2,1,0:T(8,128)(2,1)S(1)}, u32[]{:S(2)}, u32[]{:S(2)}) async-start(bf16[4,128,512]{2,1,0:T(8,128)(2,1)} %shard_map.136), calls=%async_computation.2 | async-start | bytes 1048576 | tf_op jit(solution)/shard_map/all_to_all | solution.py:190
  147.4 0.3 multiply_cosine_fusion
  147.7 5.9 %all-to-all-done.1 = bf16[4,128,512]{2,1,0:T(8,128)(2,1)S(1)} async-done(((bf16[4,128,512]{2,1,0:T(8,128)(2,1)}), bf16[4,128,512]{2,1,0:T(8,128)(2,1)S(1)}, u32[]{:S(2)}, u32[]{:S(2)}) %all-to-all-start.1) | async-done | bytes 524320 | tf_op jit(solution)/shard_map/all_to_all | solution.py:190
  153.8 0.3 multiply_subtract_fusion.1
  154.1 0.2 pad_maximum_fusion.1
  154.4 0.7 fusion.108
  (59 shorter events, 1.2 us)
Async XLA Ops:
  7.4 43.0 %copy-start = (bf16[384,2048]{1,0:T(8,128)(2,1)S(1)}, bf16[384,2048]{1,0:T(8,128)(2,1)}, u32[]{:S(2)}) copy-start(bf16[384,2048]{1,0:T(8,128)(2,1)} %param.19) | copy-start | bytes 4718596
  7.4 9.6 %copy-start.4 = (f32[384]{0:T(512)S(1)}, f32[384]{0:T(512)}, u32[]{:S(2)}) copy-start(f32[384]{0:T(512)} %param.17) | copy-start | bytes 4612
  7.4 113.2 %reduce-scatter.2.cloned.1.call-start = ((), (), s32[]{:S(2)}) async-start(), calls=%async_computation.3 | async-start | bytes 4718592 | tf_op jit(solution)/shard_map/reduce_scatter | solution.py:139
  7.4 43.3 %collective-permute-start = (bf16[2,512,256]{2,1,0:T(8,128)(2,1)}, bf16[2,512,256]{2,1,0:T(8,128)(2,1)S(1)}, u32[]{:S(2)}, u32[]{:S(2)}) collective-permute-start(bf16[2,512,256]{2,1,0:T(8,128)(2,1)} %param.26), channel_id=1, source_target_pairs={{0,0},{1,128},{2,256},{3,384},{32,32},{33,160},{34,288},{35,416},{... | collective-permute-start | bytes 1572872 | tf_op jit(solution)/shard_map/ppermute | solution.py:120
  12.6 37.8 %copy-start.6 = (f32[384]{0:T(512)S(1)}, f32[384]{0:T(512)}, u32[]{:S(2)}) copy-start(f32[384]{0:T(512)} %param.18) | copy-start | bytes 4612
  50.7 4.3 %copy-start.2 = (bf16[2,512,256]{2,1,0:T(8,128)(2,1)}, bf16[2,512,256]{2,1,0:T(8,128)(2,1)S(1)}, u32[]{:S(2)}) copy-start(bf16[2,512,256]{2,1,0:T(8,128)(2,1)S(1)} %collective-permute-done) | copy-start | bytes 1572868
  55.0 1.3 copy-start.1
  55.0 2.8 %copy-start.8 = (s32[1,128]{1,0:T(1,128)S(1)}, s32[1,128]{1,0:T(1,128)}, u32[]{:S(2)}) copy-start(s32[1,128]{1,0:T(1,128)} %param.24) | copy-start | bytes 1540
  55.1 20.7 %copy-start.7 = (f32[2,256]{1,0:T(2,128)S(1)}, f32[2,256]{1,0:T(2,128)}, u32[]{:S(2)}) copy-start(f32[2,256]{1,0:T(2,128)} %param.27) | copy-start | bytes 6148
  55.1 29.6 %copy-start.5 = (f32[2048]{0:T(1024)S(1)}, f32[2048]{0:T(1024)}, u32[]{:S(2)}) copy-start(f32[2048]{0:T(1024)} %param.20) | copy-start | bytes 24580
  55.1 82.4 %all-gather.5.cloned.1.call-start = ((), (), s32[]{:S(2)}) async-start(), calls=%async_computation.4 | async-start | bytes 8912896 | tf_op jit(solution)/shard_map/all_gather | solution.py:131
  68.4 16.3 %all-to-all-start = ((f32[8,1,4352]{2,1,0:T(1,128)}), f32[8,1,4352]{2,1,0:T(1,128)S(1)}, u32[]{:S(2)}, u32[]{:S(2)}) async-start(f32[8,1,4352]{2,1,0:T(1,128)} %all_to_all.11), calls=%async_computation.1 | async-start | bytes 278528 | tf_op jit(solution)/shard_map/all_to_all | solution.py:148
  120.6 15.6 %copy-start.3 = (f32[2048]{0:T(1024)S(1)}, f32[2048]{0:T(1024)}, u32[]{:S(2)}) copy-start(f32[2048]{0:T(1024)} %param.25) | copy-start | bytes 24580
  143.3 10.4 %all-to-all-start.1 = ((bf16[4,128,512]{2,1,0:T(8,128)(2,1)}), bf16[4,128,512]{2,1,0:T(8,128)(2,1)S(1)}, u32[]{:S(2)}, u32[]{:S(2)}) async-start(bf16[4,128,512]{2,1,0:T(8,128)(2,1)} %shard_map.136), calls=%async_computation.2 | async-start | bytes 1048576 | tf_op jit(solution)/shard_map/all_to_all | solution.py:190
Sparse Core Ops, SparseCore 0:
  55.2 65.3 reduce-scatter.1
Sparse Core Ops, SparseCore 1:
  57.7 64.7 all-gather.4

commit v2 on v0

v2 whole, which is shorter than its diff:
```python
import jax
import jax.numpy as jnp
from jax import lax
from jax.experimental import pallas as pl
from jax.experimental.pallas import tpu as pltpu
from jax.sharding import PartitionSpec as P

C = 3072
D = 8192
HEAD = 128
SIDE = 8


epsilon = 1e-06


def conv_kernel(tile_ref, weight_ref, shift_ref, gain_ref, rows_ref, stats_ref, held):
    _, cells, width, channels = tile_ref.shape
    side = weight_ref.shape[0]
    reach = side // 2
    lanes = 128
    total = jnp.zeros((cells, width, 1), jnp.float32)
    column = lax.broadcasted_iota(jnp.int32, (cells, width, lanes), 1)
    for group in range(channels // lanes):
        part = slice(group * lanes, (group + 1) * lanes)
        cell = tile_ref[0, :, :, part].astype(jnp.float32)
        sums = [
            jnp.broadcast_to(shift_ref[:, part], (width, lanes)) for _ in range(cells)
        ]
        for col_off in range(side):
            move = col_off - reach
            moved = cell
            if move:
                inside = (column + move >= 0) & (column + move < width)
                moved = jnp.where(inside, pltpu.roll(cell, (-move) % width, 1), 0.0)
            for row_off in range(side):
                scale = jnp.broadcast_to(
                    weight_ref[row_off, col_off : col_off + 1, part], (width, lanes)
                )
                for row in range(cells):
                    source = row + row_off - reach
                    if 0 <= source < cells:
                        sums[row] = sums[row] + moved[source] * scale
        out = jnp.stack(sums)
        held[:, :, part] = out
        total = total + jnp.sum(out, -1, keepdims=True)
    average = total / channels
    square = jnp.zeros((cells, width, 1), jnp.float32)
    for group in range(channels // lanes):
        part = slice(group * lanes, (group + 1) * lanes)
        centered = held[:, :, part] - average
        square = square + jnp.sum(centered * centered, -1, keepdims=True)
        rows_ref[0, :, :, part] = (centered * gain_ref[0, part]).astype(rows_ref.dtype)
    stats_ref[0, 0] = jnp.broadcast_to(average, (cells, width, lanes))
    stats_ref[1, 0] = jnp.broadcast_to(square, (cells, width, lanes))


def conv_rows(tiles, kernel, shift, gain):
    count, cells, width, channels = tiles.shape
    whole = pl.BlockSpec((1, channels), lambda t: (0, 0))
    return pl.pallas_call(
        conv_kernel,
        grid=(count,),
        in_specs=[
            pl.BlockSpec((1, cells, width, channels), lambda t: (t, 0, 0, 0)),
            pl.BlockSpec(kernel.shape, lambda t: (0, 0, 0)),
            whole,
            whole,
        ],
        out_specs=[
            pl.BlockSpec((1, cells, width, channels), lambda t: (t, 0, 0, 0)),
            pl.BlockSpec((2, 1, cells, width, 128), lambda t: (0, t, 0, 0, 0)),
        ],
        out_shape=[
            jax.ShapeDtypeStruct(tiles.shape, jnp.bfloat16),
            jax.ShapeDtypeStruct((2, count, cells, width, 128), jnp.float32),
        ],
        scratch_shapes=[pltpu.VMEM((cells, width, channels), jnp.float32)],
        compiler_params=pltpu.CompilerParams(vmem_limit_bytes=32 * 2**20),
    )(tiles, kernel, shift[None], gain[None])


def split_dot(rows, weight):
    parts = []
    rest = rows
    for _ in range(3):
        part = lax.reduce_precision(rest, 8, 7)
        parts.append(part)
        rest = rest - part
    stacked = jnp.concatenate(parts, 0).astype(jnp.bfloat16)
    out = jnp.dot(stacked, weight, preferred_element_type=jnp.float32)
    count = rows.shape[0]
    return out[:count] + out[count : 2 * count] + out[2 * count :]


def three_parts(value):
    first = value.astype(jnp.bfloat16).astype(jnp.float32)
    rest = value - first
    second = rest.astype(jnp.bfloat16).astype(jnp.float32)
    return first, second, rest - second


EXTRA = 16
STEP = 16


def kv_kernel(
    summed_ref, means_ref, squares_ref, gains_ref, bias_ref, unit_ref, scale_ref, weight_ref,
    out_ref, rows, stats,
):
    count, features = summed_ref.shape
    towers, _, _, depth, width = weight_ref.shape
    n_seq = means_ref.shape[0]
    inner = features // depth // 4

    @pl.when(pl.program_id(0) == 0)
    def _():
        means = means_ref[...]
        average = jnp.sum(means, 0, keepdims=True) / n_seq
        offsets = means - average
        block = C // n_seq
        variance = (
            jnp.sum(squares_ref[...], 0, keepdims=True)
            + block * jnp.sum(offsets * offsets, 0, keepdims=True)
        ) / C
        inverse = lax.rsqrt(variance + epsilon)
        columns = jnp.transpose(
            jnp.concatenate([offsets, jnp.broadcast_to(inverse, (n_seq, count))], 0)
        )
        unit = unit_ref[...]
        gain = scale_ref[...]
        unit_square = jnp.sum(unit * unit)
        for begin in range(0, count, STEP):
            here = slice(begin, begin + STEP)
            value = summed_ref[here, :].astype(jnp.float32)
            for source in range(n_seq):
                value = value + columns[here, source : source + 1] * gains_ref[source : source + 1, :]
            value = value * columns[here, n_seq : n_seq + 1] + bias_ref[...]
            hidden = 0.5 * value * (1.0 + lax.erf(value * 0.7071067811865476))
            along = jnp.sum(hidden * unit, -1, keepdims=True)
            across = hidden - (along / unit_square) * unit
            square = jnp.sum(across * across, -1, keepdims=True)
            lane = lax.broadcasted_iota(jnp.int32, (STEP, count), 1)
            stats[here, :] = jnp.where(lane == 0, along, jnp.where(lane == 1, square, unit_square))
            scaled = (across * gain).astype(jnp.bfloat16)
            for place in range(features // depth):
                first, second = place // inner, place % inner
                source = second * 4 + first
                rows[here, place * depth : (place + 1) * depth] = scaled[
                    :, source * depth : (source + 1) * depth
                ]
        parts = jnp.concatenate(
            [*three_parts(unit * gain), jnp.zeros((EXTRA - 3, features), jnp.float32)], 0
        ).astype(jnp.bfloat16)
        for place in range(features // depth):
            first, second = place // inner, place % inner
            source = second * 4 + first
            rows[count:, place * depth : (place + 1) * depth] = parts[
                :, source * depth : (source + 1) * depth
            ]

    turned = jnp.transpose(stats[...])[:8]
    for pair in range(2):
        there = slice(pair * width, (pair + 1) * width)
        weight = weight_ref[:, 0, pair].reshape(towers * depth, width)
        total = jnp.dot(rows[...], weight, preferred_element_type=jnp.float32)
        out_ref[0, :count, there] = total[:count].astype(out_ref.dtype)
        vector = total[count : count + 1] + total[count + 1 : count + 2] + total[count + 2 : count + 3]
        line = jnp.concatenate([turned[pair : pair + 1], turned[2:3]], 1)
        extra = jnp.concatenate(
            [
                *three_parts(vector),
                *three_parts(line),
                jnp.zeros((EXTRA - 6, width), jnp.float32),
            ],
            0,
        )
        out_ref[0, count:, there] = extra.astype(out_ref.dtype)


def kv_partial(summed, means, squares, gains, bias, unit, scale, weight):
    count, features = summed.shape
    towers, groups, pairs, depth, width = weight.shape

    def whole(array):
        return pl.BlockSpec(array.shape, lambda g: (0,) * array.ndim)

    return pl.pallas_call(
        kv_kernel,
        grid=(groups,),
        in_specs=[
            *(whole(a) for a in (summed, means, squares, gains, bias, unit, scale)),
            pl.BlockSpec((towers, 1, pairs, depth, width), lambda g: (0, g, 0, 0, 0)),
        ],
        out_specs=pl.BlockSpec((1, count + EXTRA, pairs * width), lambda g: (g, 0, 0)),
        out_shape=jax.ShapeDtypeStruct((groups, count + EXTRA, pairs * width), jnp.bfloat16),
        scratch_shapes=[
            pltpu.VMEM((count + EXTRA, features), jnp.bfloat16),
            pltpu.VMEM((count, count), jnp.float32),
        ],
        compiler_params=pltpu.CompilerParams(vmem_limit_bytes=56 * 2**20),
    )(summed, means, squares, gains, bias, unit, scale, weight)


def end_kernel(pieces_ref, bias_ref, cosine_ref, sine_ref, valid_ref, out_ref):
    groups, rows, both = pieces_ref.shape
    count = rows - EXTRA
    width = both // 2
    extra = pieces_ref[:, count:, :].astype(jnp.float32)
    vectors = extra[:, 0] + extra[:, 1] + extra[:, 2]
    lines = extra[:, 3] + extra[:, 4] + extra[:, 5]
    along = lines[:, :count]
    unit_square = lines[:, count : 2 * count]
    across = lines[:, width : width + count]
    coefficient = jnp.sum(along, 0, keepdims=True)
    left = along / unit_square - coefficient
    mean_square = jnp.sum(across + left * left * unit_square, 0, keepdims=True) / D
    inverse = lax.rsqrt(mean_square + epsilon)
    columns = jnp.transpose(
        jnp.concatenate([left, jnp.broadcast_to(inverse, (8 - groups, count))], 0)
    )
    total = jnp.zeros((count, both), jnp.float32)
    for group in range(groups):
        total = total + pieces_ref[group, :count].astype(jnp.float32)
        total = total + columns[:, group : group + 1] * vectors[group : group + 1, :]
    total = total * columns[:, groups : groups + 1]
    valid = valid_ref[...]
    for head in range(width // HEAD):
        there = slice(head * HEAD, (head + 1) * HEAD)
        key = total[:, there] + bias_ref[0:1, there]
        turned = key * cosine_ref[...] + pltpu.roll(key, HEAD // 2, 1) * sine_ref[...]
        out_ref[0, 0, :, there] = (turned * valid).astype(out_ref.dtype)
    value = total[:, width:] + bias_ref[1:2, :]
    out_ref[0, 1] = (value * valid[:, :1]).astype(out_ref.dtype)


def end_rows(pieces, bias, cosine, sine, valid):
    _, rows, both = pieces.shape
    return pl.pallas_call(
        end_kernel,
        out_shape=jax.ShapeDtypeStruct((1, 2, rows - EXTRA, both // 2), jnp.bfloat16),
        compiler_params=pltpu.CompilerParams(vmem_limit_bytes=32 * 2**20),
    )(pieces, bias, cosine, sine, valid)


def local(
    tiles,
    dw_weight,
    dw_bias,
    block_gain,
    block_bias,
    proj_weight,
    proj_bias,
    directions,
    dir_index,
    tile_counts,
    positions,
    rms_gain,
    kv_weight,
    kv_bias,
):
    n_seq = lax.axis_size("seq")
    n_mp = lax.axis_size("mp")
    n_tower = lax.axis_size("tower")
    pairs, depth, width = kv_weight.shape
    inner = n_tower // n_mp
    cut = kv_weight.reshape(pairs, n_mp, depth // n_mp, width).swapaxes(0, 1)
    cut = lax.all_to_all(
        cut,
        "tower",
        0,
        0,
        tiled=True,
        axis_index_groups=[[a * inner + b for a in range(n_mp)] for b in range(inner)],
    )

    block_rows, stats = conv_rows(tiles, dw_weight, dw_bias, block_gain)
    channels = tiles.shape[3]
    gathered = lax.all_gather(block_rows.reshape(-1, channels), "mp", axis=0, tiled=True)
    gathered, cut = lax.optimization_barrier((gathered, cut))
    kv_rows = lax.all_gather(
        lax.all_to_all(cut, "mp", 0, 0, tiled=True), "tower", axis=0, tiled=False
    )
    partial = jnp.dot(gathered, proj_weight, preferred_element_type=jnp.float32).astype(
        jnp.bfloat16
    )
    partial, stats, block_gain, block_bias = lax.optimization_barrier(
        (partial, stats, block_gain, block_bias)
    )
    summed = lax.psum_scatter(partial, "seq", scatter_dimension=0, tiled=True)

    vectors = split_dot(jnp.stack([block_gain, block_bias]), proj_weight)
    stats = stats[..., 0].reshape(2, -1)
    stats = lax.all_gather(stats, "mp", axis=1, tiled=True)
    rows_here = stats.shape[1] // n_seq
    stats = stats.reshape(2, n_seq, rows_here).swapaxes(0, 1).reshape(n_seq, -1)
    payload = jnp.concatenate(
        [stats, jnp.broadcast_to(vectors.reshape(1, -1), (n_seq, vectors.size))], 1
    )
    payload = lax.all_to_all(payload, "seq", 0, 0, tiled=True)
    means = payload[:, :rows_here]
    squares = payload[:, rows_here : 2 * rows_here]
    column_count = vectors.shape[1]
    gain_rows = payload[:, 2 * rows_here : 2 * rows_here + column_count]
    bias_row = jnp.sum(payload[:, 2 * rows_here + column_count :], 0) + proj_bias

    picked = jnp.arange(directions.shape[0], dtype=jnp.int32)[:, None] == dir_index[0]
    chosen = jnp.sum(jnp.where(picked, directions, 0.0), 0)
    unit_dir = chosen / jnp.sqrt(jnp.sum(chosen * chosen))
    local_unit = lax.dynamic_slice_in_dim(
        unit_dir, lax.axis_index("mp") * column_count, column_count, 0
    )

    half_head = HEAD // 2
    inverse = jnp.power(
        jnp.float32(1000000.0), -(jnp.arange(half_head, dtype=jnp.float32) * 2.0 / HEAD)
    )
    angles = positions[0].astype(jnp.float32)[:, None] * inverse[None, :]
    cosine = jnp.tile(jnp.cos(angles), (1, 2))
    sine_part = jnp.sin(angles)
    sine = jnp.concatenate([-sine_part, sine_part], 1)
    row_ids = lax.axis_index("seq") * rows_here + jnp.arange(rows_here, dtype=jnp.int32)
    row_valid = (row_ids // (SIDE * SIDE) < tile_counts[0]).astype(jnp.float32)[:, None]
    row_valid = jnp.broadcast_to(row_valid, cosine.shape)

    pieces = kv_partial(
        summed,
        means,
        squares,
        gain_rows,
        bias_row[None],
        local_unit[None],
        rms_gain[None],
        kv_rows,
    )
    pieces = lax.all_to_all(pieces, "mp", 0, 0, tiled=True)
    return end_rows(pieces, kv_bias, cosine, sine, row_valid)


def solution(mesh):
    return jax.shard_map(
        local,
        mesh=mesh,
        in_specs=(
            P(("tower", "mp"), None, None, "seq"),
            P(None, None, "seq"),
            P("seq"),
            P("seq"),
            P("seq"),
            P("seq", "mp"),
            P("mp"),
            P(),
            P("tower"),
            P("tower"),
            P("tower", "seq"),
            P("mp"),
            P(None, "tower", "mp"),
            P(None, "mp"),
        ),
        out_specs=P("tower", None, "seq", "mp"),
        check_vma=False,
    )
```

time: 257 us -> 144 us (0.56)
  waiting for transfers between devices: 165 us -> 50.7 us
  starting transfers between devices: 0.09 us -> 21.8 us
  blocking collectives: 49.6 us -> 31.2 us
  Pallas kernels: 0 us -> 11 us
  other arithmetic: 12.6 us -> 3.08 us
  matrix products: 9.54 us -> 4.63 us
    all_gather x2 -> x1, waiting for transfers between devices: 98.4 us -> 9.73 us  [local(): lax.all_gather(lax.all_to_all(cut, 'mp', 0, 0, tiled=True), 'tower', axis...]
    reduce_scatter x1, waiting for transfers between devices: 66.3 us -> 22.8 us  [local(): summed = lax.psum_scatter(partial, 'seq', scatter_dimension=0, tiled=True)]
    psum x3 -> x0, blocking collectives: 38.7 us -> none  [the longest x1 24.2 us: local(): lax.psum((jnp.sum(filtered, -1), jnp.sum(filtered * filtered, -1)), 'seq')]
    all_to_all x0 -> x3, starting transfers between devices: none -> 21.8 us  [the longest x1 10.8 us: local(): lax.all_to_all(cut, 'tower', 0, 0, tiled=True, axis_index_groups=[[a * in...]
    all_to_all x0 -> x3, waiting for transfers between devices: none -> 18.1 us  [the longest x1 9.65 us: local(): payload = lax.all_to_all(payload, 'seq', 0, 0, tiled=True)]
    pallas_call x0 -> x3, Pallas kernels: none -> 11 us  [the longest x1 7.77 us: kv_partial(): pl.pallas_call(kv_kernel, grid=(groups,), in_specs=[*(whole(a) for a in (...]
    all_to_all x0 -> x1, blocking collectives: none -> 10.2 us  [local(): lax.all_to_all(cut, 'mp', 0, 0, tiled=True)]
    all_gather x1 -> x2, blocking collectives: 10.9 us -> 21 us  [the longest x1 12.6 us: local(): lax.all_gather(block_rows.reshape(-1, channels), 'mp', axis=0, tiled=True)]
  transfers between devices with their start and end apart: 3 -> 5, of which waited for: 3 -> 4; matrix products, arithmetic and copies ran while one was open for 0% -> 3% of each run, Pallas kernels for 0% -> 1%
where the time goes in v2:
time: 144 us; the launch traced here: 143 us
  waiting for transfers between devices  50.7 us (35%)
  blocking collectives  31.2 us (22%)
  starting transfers between devices  21.8 us (15%)
  between operations  17.1 us (12%)
  Pallas kernels  11 us (8%)
  matrix products  4.63 us (3%)
  local copies, waits for them, and re-layouts  3.91 us (3%)
  other arithmetic  3.08 us (2%)
    reduce_scatter x1, waiting for transfers between devices, local(): summed = lax.psum_scatter(partial, 'seq', scatter_dimension=0, tiled=True)  22.8 us
    all_gather x1, blocking collectives, local(): lax.all_gather(block_rows.reshape(-1, channels), 'mp', axis=0, tiled=True)  12.6 us
    all_to_all x1, starting transfers between devices, local(): lax.all_to_all(cut, 'tower', 0, 0, tiled=True, axis_index_groups=[[a * in...  10.8 us
    all_to_all x1, blocking collectives, local(): lax.all_to_all(cut, 'mp', 0, 0, tiled=True)  10.2 us
    all_gather x1, waiting for transfers between devices, local(): lax.all_gather(lax.all_to_all(cut, 'mp', 0, 0, tiled=True), 'tower', axis...  9.73 us
    all_to_all x1, waiting for transfers between devices, local(): payload = lax.all_to_all(payload, 'seq', 0, 0, tiled=True)  9.65 us
    all_to_all x1, waiting for transfers between devices, local(): pieces = lax.all_to_all(pieces, 'mp', 0, 0, tiled=True)  8.46 us
    all_gather x1, blocking collectives, local(): stats = lax.all_gather(stats, 'mp', axis=1, tiled=True)  8.4 us
  transfers between devices with their start and end apart: 5, of which 4 were waited for; matrix products, arithmetic and copies ran while one was open for 3% of the time, Pallas kernels for 1%

profile of v2, /device:TPU:1, one launch (start us, length us, event | category | flops | bytes accessed | tf_op | source)
XLA Modules:
  0.0 143.4 jit_solution(245260566335405108)
XLA Ops:
  7.4 2.0 %copy.27 = bf16[4,2,128,256]{3,2,1,0:T(8,128)(2,1)} copy(bf16[4,2,128,256]{3,2,0,1:T(8,128)(2,1)} %bitcast.39) | data formatting | bytes 1048576 | tf_op jit(solution)/shard_map/transpose | solution.py:267
  9.4 10.8 %all-to-all-start = ((bf16[4,2,128,256]{3,2,1,0:T(8,128)(2,1)}), bf16[4,2,128,256]{3,2,1,0:T(8,128)(2,1)S(1)}, u32[]{:S(2)}, u32[]{:S(2)}) async-start(bf16[4,2,128,256]{3,2,1,0:T(8,128)(2,1)} %copy.27), calls=%async_computation | async-start | bytes 1048576 | tf_op jit(solution)/shard_map/all_to_all | solution.py:268
  20.3 2.1 %shard_map.136 = (bf16[4,8,8,384]{3,2,1,0:T(8,128)(2,1)S(1)}, f32[2,4,8,8,128]{4,3,2,1,0:T(8,128)S(1)}) custom-call(bf16[4,8,8,384]{3,2,1,0:T(8,128)(2,1)S(1)} %copy-done.1, f32[7,7,384]{2,1,0:T(8,128)S(1)} %copy-done.2, f32[1,384]{1,0:T(1,128)S(1)} %broadcast_in_dim.43.shift_ref, f32[1,384]{1,0:T(1,128)S(1)} %broadcast_in_dim.44.gain_ref), custom_call_target="tpu_custom_call" | custom-call | tf_op jit(solution)/shard_map/pallas_call | solution.py:61
  22.4 12.6 %all_gather.12 = bf16[1024,384]{1,0:T(8,128)(2,1)S(1)} all-gather(bf16[256,384]{1,0:T(8,128)(2,1)S(1)} %bitcast.35), channel_id=1, replica_groups=mesh['tower'=16,'seq'=8,'mp'=4] {'mp'}, dimensions={0}, use_global_device_ids=true | all-gather | bytes 983040 | tf_op jit(solution)/shard_map/all_gather | solution.py:279
  35.1 4.3 %convolution_convert_fusion = bf16[1024,2048]{1,0:T(8,128)(2,1)} fusion(bf16[1024,384]{1,0:T(8,128)(2,1)S(1)} %all_gather.12, bf16[384,2048]{1,0:T(8,128)(2,1)S(1)} %copy-done), kind=kOutput, calls=%fused_computation | convolution fusion | flops 1612709888 | bytes 6553600 | tf_op jit(solution)/shard_map/dot_general | solution.py:284
  39.4 0.0 all-gather.3.cloned.1.call-start
  39.5 10.2 %all_to_all.27 = bf16[4,2,128,256]{3,2,1,0:T(8,128)(2,1)} all-to-all(bf16[4,2,128,256]{3,2,1,0:T(8,128)(2,1)S(1)} %all-to-all-done), channel_id=1, replica_groups=mesh['tower'=16,'seq'=8,'mp'=4] {'mp'}, dimensions={0} | all-to-all | bytes 1048576 | tf_op jit(solution)/shard_map/all_to_all | solution.py:282
  49.7 0.0 all-gather.3.cloned.1.call-update
  50.4 0.2 select_reduce_fusion
  50.5 0.6 multiply_reduce_fusion
  51.8 0.6 dynamic-slice_divide_fusion
  52.5 0.3 fusion.2
  52.8 0.1 slice_reduce_fusion
  53.0 0.1 reshape_squeeze.3
  53.1 8.4 %all_gather.13 = f32[2,1024]{1,0:T(2,128)S(1)} all-gather(f32[2,256]{1,0:T(2,128)S(1)} %reshape_squeeze.3), channel_id=1, replica_groups=mesh['tower'=16,'seq'=8,'mp'=4] {'mp'}, dimensions={1}, use_global_device_ids=true | all-gather | bytes 10240 | tf_op jit(solution)/shard_map/all_gather | solution.py:294
  61.5 0.7 all_to_all.18
  62.2 6.8 %all-to-all-start.1 = ((f32[8,1,4352]{2,1,0:T(1,128)}), f32[8,1,4352]{2,1,0:T(1,128)S(1)}, u32[]{:S(2)}, u32[]{:S(2)}) async-start(f32[8,1,4352]{2,1,0:T(1,128)} %all_to_all.18), calls=%async_computation.2 | async-start | bytes 278528 | tf_op jit(solution)/shard_map/all_to_all | solution.py:300
  69.1 9.6 %all-to-all-done.1 = f32[8,1,4352]{2,1,0:T(1,128)S(1)} async-done(((f32[8,1,4352]{2,1,0:T(1,128)}), f32[8,1,4352]{2,1,0:T(1,128)S(1)}, u32[]{:S(2)}, u32[]{:S(2)}) %all-to-all-start.1) | async-done | bytes 139296 | tf_op jit(solution)/shard_map/all_to_all | solution.py:300
  78.8 0.6 slice_reduce_fusion.1
  79.4 0.6 add.31
  80.0 0.6 fusion.11
  80.6 22.8 %reduce-scatter.2.cloned.1.call-done.summed_ref = bf16[128,2048]{1,0:T(8,128)(2,1)} async-done(((bf16[1024,2048]{1,0:T(8,128)(2,1)}), bf16[128,2048]{1,0:T(8,128)(2,1)}) %reduce-scatter.2.cloned.1.call-update) | async-done | bytes 524304 | tf_op jit(solution)/shard_map/reduce_scatter | solution.py:290
  103.4 9.7 %all-gather.3.cloned.1.call-done = bf16[64,2,128,256]{3,2,1,0:T(8,128)(2,1)} async-done(((bf16[4,2,128,256]{3,2,1,0:T(8,128)(2,1)}), bf16[64,2,128,256]{3,2,1,0:T(8,128)(2,1)}) %all-gather.3.cloned.1.call-update) | async-done | bytes 8388624 | tf_op jit(solution)/shard_map/all_gather | solution.py:281
  113.2 7.8 %shard_map.137 = bf16[4,144,512]{2,1,0:T(8,128)(2,1)} custom-call(bf16[128,2048]{1,0:T(8,128)(2,1)} %reduce-scatter.2.cloned.1.call-done.summed_ref, f32[8,128]{1,0:T(8,128)} %get-tuple-element.24.means_ref, f32[8,128]{1,0:T(8,128)} %get-tuple-element.23.squares_ref, f32[8,2048]{1,0:T(8,128)} %get-tuple-element.22.gains_ref, f32[1,2048]{1,0:T(1,128)} %bitcast.42, ...), custom_call_target="tpu_custom_call" | custom-call | tf_op jit(solution)/shard_map/pallas_call | solution.py:188
  120.9 4.1 %all-to-all-start.3 = ((bf16[4,144,512]{2,1,0:T(8,128)(2,1)}), bf16[4,144,512]{2,1,0:T(8,128)(2,1)S(1)}, u32[]{:S(2)}, u32[]{:S(2)}) async-start(bf16[4,144,512]{2,1,0:T(8,128)(2,1)} %shard_map.137), calls=%async_computation.4 | async-start | bytes 1179648 | tf_op jit(solution)/shard_map/all_to_all | solution.py:336
  125.0 0.3 fusion
  125.3 0.1 copy.29
  125.4 0.1 copy.30.cosine_ref
  126.2 0.1 pad_maximum_fusion.1.sine_ref
  126.3 8.5 %all-to-all-done.3.pieces_ref = bf16[4,144,512]{2,1,0:T(8,128)(2,1)S(1)} async-done(((bf16[4,144,512]{2,1,0:T(8,128)(2,1)}), bf16[4,144,512]{2,1,0:T(8,128)(2,1)S(1)}, u32[]{:S(2)}, u32[]{:S(2)}) %all-to-all-start.3) | async-done | bytes 589856 | tf_op jit(solution)/shard_map/all_to_all | solution.py:336
  134.8 0.1 broadcast_in_dim.52.valid_ref
  134.8 1.1 shard_map.138
  (39 shorter events, 0.2 us)
Async XLA Ops:
  7.4 27.7 %copy-start = (bf16[384,2048]{1,0:T(8,128)(2,1)S(1)}, bf16[384,2048]{1,0:T(8,128)(2,1)}, u32[]{:S(2)}) copy-start(bf16[384,2048]{1,0:T(8,128)(2,1)} %param.19) | copy-start | bytes 4718596
  7.4 12.9 %copy-start.7 = (f32[384]{0:T(512)S(1)}, f32[384]{0:T(512)}, u32[]{:S(2)}) copy-start(f32[384]{0:T(512)} %param.16) | copy-start | bytes 4612
  7.4 12.9 %copy-start.6 = (f32[384]{0:T(512)S(1)}, f32[384]{0:T(512)}, u32[]{:S(2)}) copy-start(f32[384]{0:T(512)} %param.17) | copy-start | bytes 4612
  7.4 12.9 %copy-start.1 = (bf16[4,8,8,384]{3,2,1,0:T(8,128)(2,1)S(1)}, bf16[4,8,8,384]{3,2,1,0:T(8,128)(2,1)}, u32[]{:S(2)}) copy-start(bf16[4,8,8,384]{3,2,1,0:T(8,128)(2,1)} %tile_ref.1) | copy-start | bytes 589828
  7.4 12.9 %copy-start.2 = (f32[7,7,384]{2,1,0:T(8,128)S(1)}, f32[7,7,384]{2,1,0:T(8,128)}, u32[]{:S(2)}) copy-start(f32[7,7,384]{2,1,0:T(8,128)} %weight_ref.1) | copy-start | bytes 225796
  9.4 25.7 %all-to-all-start = ((bf16[4,2,128,256]{3,2,1,0:T(8,128)(2,1)}), bf16[4,2,128,256]{3,2,1,0:T(8,128)(2,1)S(1)}, u32[]{:S(2)}, u32[]{:S(2)}) async-start(bf16[4,2,128,256]{3,2,1,0:T(8,128)(2,1)} %copy.27), calls=%async_computation | async-start | bytes 1048576 | tf_op jit(solution)/shard_map/all_to_all | solution.py:268
  20.2 83.2 %reduce-scatter.2.cloned.1.call-start = ((), (), s32[]{:S(2)}) async-start(), calls=%async_computation.5 | async-start | bytes 4718592 | tf_op jit(solution)/shard_map/reduce_scatter | solution.py:290
  39.4 10.9 %copy-start.4 = (f32[16,8192]{1,0:T(8,128)S(1)}, f32[16,8192]{1,0:T(8,128)}, u32[]{:S(2)}) copy-start(f32[16,8192]{1,0:T(8,128)} %param.21) | copy-start | bytes 1572868
  39.4 13.0 %copy-start.8 = (f32[384]{0:T(512)S(1)}, f32[384]{0:T(512)}, u32[]{:S(2)}) copy-start(f32[384]{0:T(512)} %param.18) | copy-start | bytes 4612
  39.4 73.7 %all-gather.3.cloned.1.call-start = ((), (), s32[]{:S(2)}) async-start(), calls=%async_computation.6 | async-start | bytes 8912896 | tf_op jit(solution)/shard_map/all_gather | solution.py:281
  50.5 18.6 %copy-start.9 = (s32[1,128]{1,0:T(1,128)S(1)}, s32[1,128]{1,0:T(1,128)}, u32[]{:S(2)}) copy-start(s32[1,128]{1,0:T(1,128)} %param.24) | copy-start | bytes 1540
  52.5 26.9 %copy-start.5 = (f32[2048]{0:T(1024)S(1)}, f32[2048]{0:T(1024)}, u32[]{:S(2)}) copy-start(f32[2048]{0:T(1024)} %param.20) | copy-start | bytes 24580
  62.2 16.5 %all-to-all-start.1 = ((f32[8,1,4352]{2,1,0:T(1,128)}), f32[8,1,4352]{2,1,0:T(1,128)S(1)}, u32[]{:S(2)}, u32[]{:S(2)}) async-start(f32[8,1,4352]{2,1,0:T(1,128)} %all_to_all.18), calls=%async_computation.2 | async-start | bytes 278528 | tf_op jit(solution)/shard_map/all_to_all | solution.py:300
  120.9 13.9 %copy-start.3 = (f32[2,256]{1,0:T(2,128)S(1)}, f32[2,256]{1,0:T(2,128)}, u32[]{:S(2)}) copy-start(f32[2,256]{1,0:T(2,128)} %bias_ref.1) | copy-start | bytes 6148
  120.9 13.8 %all-to-all-start.3 = ((bf16[4,144,512]{2,1,0:T(8,128)(2,1)}), bf16[4,144,512]{2,1,0:T(8,128)(2,1)S(1)}, u32[]{:S(2)}, u32[]{:S(2)}) async-start(bf16[4,144,512]{2,1,0:T(8,128)(2,1)} %shard_map.137), calls=%async_computation.4 | async-start | bytes 1179648 | tf_op jit(solution)/shard_map/all_to_all | solution.py:336
Sparse Core Ops, SparseCore 0:
  39.5 63.8 reduce-scatter.1
Sparse Core Ops, SparseCore 1:
  49.8 63.3 all-gather.2

commit v3 on v2

--- a/solution.py
+++ b/solution.py
@@ -9,6 +9,7 @@
 D = 8192
 HEAD = 128
 SIDE = 8
+INNER = 4
 
 
 epsilon = 1e-06
@@ -76,7 +77,7 @@
             jax.ShapeDtypeStruct((2, count, cells, width, 128), jnp.float32),
         ],
         scratch_shapes=[pltpu.VMEM((cells, width, channels), jnp.float32)],
-        compiler_params=pltpu.CompilerParams(vmem_limit_bytes=32 * 2**20),
+        compiler_params=pltpu.CompilerParams(vmem_limit_bytes=60 * 2**20),
     )(tiles, kernel, shift[None], gain[None])
 
 
@@ -104,14 +105,47 @@
 STEP = 16
 
 
+def project_kernel(rows_ref, weight_ref, out_ref):
+    halves, _, columns = out_ref.shape
+    width = columns // INNER
+    for half in range(halves):
+        for block in range(INNER):
+            begin = (block * halves + half) * width
+            out_ref[half, :, block * width : (block + 1) * width] = jnp.dot(
+                rows_ref[...],
+                weight_ref[:, begin : begin + width],
+                preferred_element_type=jnp.float32,
+            ).astype(out_ref.dtype)
+
+
+def project(rows, weight, groups, halves):
+    count, depth = rows.shape
+    columns = weight.shape[1]
+    return pl.pallas_call(
+        project_kernel,
+        grid=(groups,),
+        in_specs=[
+            pl.BlockSpec((count // groups, depth), lambda g: (g, 0)),
+            pl.BlockSpec(weight.shape, lambda g: (0, 0)),
+        ],
+        out_specs=pl.BlockSpec((halves, count // groups, columns // halves), lambda g: (g, 0, 0)),
+        out_shape=jax.ShapeDtypeStruct(
+            (groups * halves, count // groups, columns // halves), jnp.bfloat16
+        ),
+        compiler_params=pltpu.CompilerParams(vmem_limit_bytes=60 * 2**20),
+    )(rows, weight)
+
+
 def kv_kernel(
     summed_ref, means_ref, squares_ref, gains_ref, bias_ref, unit_ref, scale_ref, weight_ref,
     out_ref, rows, stats,
 ):
     count, features = summed_ref.shape
-    towers, _, _, depth, width = weight_ref.shape
+    _, _, depth, lanes = weight_ref.shape
     n_seq = means_ref.shape[0]
-    inner = features // depth // 4
+    halves = out_ref.shape[0]
+    own = count // halves
+    width = out_ref.shape[3] // 2
 
     @pl.when(pl.program_id(0) == 0)
     def _():
@@ -140,47 +174,47 @@
             along = jnp.sum(hidden * unit, -1, keepdims=True)
             across = hidden - (along / unit_square) * unit
             square = jnp.sum(across * across, -1, keepdims=True)
-            lane = lax.broadcasted_iota(jnp.int32, (STEP, count), 1)
+            lane = lax.broadcasted_iota(jnp.int32, (STEP, 128), 1)
             stats[here, :] = jnp.where(lane == 0, along, jnp.where(lane == 1, square, unit_square))
-            scaled = (across * gain).astype(jnp.bfloat16)
-            for place in range(features // depth):
-                first, second = place // inner, place % inner
-                source = second * 4 + first
-                rows[here, place * depth : (place + 1) * depth] = scaled[
-                    :, source * depth : (source + 1) * depth
-                ]
-        parts = jnp.concatenate(
+            rows[here, :] = (across * gain).astype(jnp.bfloat16)
+        rows[count:, :] = jnp.concatenate(
             [*three_parts(unit * gain), jnp.zeros((EXTRA - 3, features), jnp.float32)], 0
         ).astype(jnp.bfloat16)
-        for place in range(features // depth):
-            first, second = place // inner, place % inner
-            source = second * 4 + first
-            rows[count:, place * depth : (place + 1) * depth] = parts[
-                :, source * depth : (source + 1) * depth
-            ]
 
     turned = jnp.transpose(stats[...])[:8]
     for pair in range(2):
         there = slice(pair * width, (pair + 1) * width)
-        weight = weight_ref[:, 0, pair].reshape(towers * depth, width)
+        weight = jnp.concatenate(
+            [
+                weight_ref[(pair * 2 + side) * INNER : (pair * 2 + side + 1) * INNER, 0].reshape(
+                    features, lanes
+                )
+                for side in range(width // lanes)
+            ],
+            1,
+        )
         total = jnp.dot(rows[...], weight, preferred_element_type=jnp.float32)
-        out_ref[0, :count, there] = total[:count].astype(out_ref.dtype)
         vector = total[count : count + 1] + total[count + 1 : count + 2] + total[count + 2 : count + 3]
-        line = jnp.concatenate([turned[pair : pair + 1], turned[2:3]], 1)
-        extra = jnp.concatenate(
-            [
-                *three_parts(vector),
-                *three_parts(line),
-                jnp.zeros((EXTRA - 6, width), jnp.float32),
-            ],
-            0,
-        )
-        out_ref[0, count:, there] = extra.astype(out_ref.dtype)
-
-
-def kv_partial(summed, means, squares, gains, bias, unit, scale, weight):
+        for half in range(halves):
+            mine = slice(half * own, (half + 1) * own)
+            out_ref[half, 0, :own, there] = total[mine].astype(out_ref.dtype)
+            line = jnp.concatenate([turned[pair : pair + 1, mine], turned[2:3, mine]], 1)
+            extra = jnp.concatenate(
+                [
+                    *three_parts(vector),
+                    *three_parts(line),
+                    jnp.zeros((EXTRA - 6, width), jnp.float32),
+                ],
+                0,
+            )
+            out_ref[half, 0, own:, there] = extra.astype(out_ref.dtype)
+
+
+def kv_partial(summed, means, squares, gains, bias, unit, scale, weight, halves):
     count, features = summed.shape
-    towers, groups, pairs, depth, width = weight.shape
+    towers, groups, depth, lanes = weight.shape
+    both = 4 * lanes
+    rows_out = count // halves + EXTRA
 
     def whole(array):
         return pl.BlockSpec(array.shape, lambda g: (0,) * array.ndim)
@@ -190,15 +224,15 @@
         grid=(groups,),
         in_specs=[
             *(whole(a) for a in (summed, means, squares, gains, bias, unit, scale)),
-            pl.BlockSpec((towers, 1, pairs, depth, width), lambda g: (0, g, 0, 0, 0)),
-        ],
-        out_specs=pl.BlockSpec((1, count + EXTRA, pairs * width), lambda g: (g, 0, 0)),
-        out_shape=jax.ShapeDtypeStruct((groups, count + EXTRA, pairs * width), jnp.bfloat16),
+            pl.BlockSpec((towers, 1, depth, lanes), lambda g: (0, g, 0, 0)),
+        ],
+        out_specs=pl.BlockSpec((halves, 1, rows_out, both), lambda g: (0, g, 0, 0)),
+        out_shape=jax.ShapeDtypeStruct((halves, groups, rows_out, both), jnp.bfloat16),
         scratch_shapes=[
             pltpu.VMEM((count + EXTRA, features), jnp.bfloat16),
-            pltpu.VMEM((count, count), jnp.float32),
-        ],
-        compiler_params=pltpu.CompilerParams(vmem_limit_bytes=56 * 2**20),
+            pltpu.VMEM((count, 128), jnp.float32),
+        ],
+        compiler_params=pltpu.CompilerParams(vmem_limit_bytes=60 * 2**20),
     )(summed, means, squares, gains, bias, unit, scale, weight)
 
 
@@ -217,7 +251,7 @@
     mean_square = jnp.sum(across + left * left * unit_square, 0, keepdims=True) / D
     inverse = lax.rsqrt(mean_square + epsilon)
     columns = jnp.transpose(
-        jnp.concatenate([left, jnp.broadcast_to(inverse, (8 - groups, count))], 0)
+        jnp.concatenate([left, jnp.broadcast_to(inverse, (8, count))], 0)
     )
     total = jnp.zeros((count, both), jnp.float32)
     for group in range(groups):
@@ -239,7 +273,7 @@
     return pl.pallas_call(
         end_kernel,
         out_shape=jax.ShapeDtypeStruct((1, 2, rows - EXTRA, both // 2), jnp.bfloat16),
-        compiler_params=pltpu.CompilerParams(vmem_limit_bytes=32 * 2**20),
+        compiler_params=pltpu.CompilerParams(vmem_limit_bytes=60 * 2**20),
     )(pieces, bias, cosine, sine, valid)
 
 
@@ -259,56 +293,71 @@
     kv_weight,
     kv_bias,
 ):
-    n_seq = lax.axis_size("seq")
+    n_row = lax.axis_size("row")
+    n_half = lax.axis_size("half")
     n_mp = lax.axis_size("mp")
-    n_tower = lax.axis_size("tower")
+    n_seq = n_row * n_half
+    half = lax.axis_index("half")
+
+    block_rows, stats = conv_rows(tiles, dw_weight, dw_bias, block_gain)
+    channels = tiles.shape[3]
+    gathered = lax.all_gather(block_rows.reshape(-1, channels), "mp", axis=0, tiled=True)
+    partial = project(gathered, proj_weight, n_row, n_half)
+    partial, kv_weight = lax.optimization_barrier((partial, kv_weight))
+    summed = lax.psum_scatter(partial, ("row", "half"), scatter_dimension=0, tiled=True)[0]
+
     pairs, depth, width = kv_weight.shape
-    inner = n_tower // n_mp
-    cut = kv_weight.reshape(pairs, n_mp, depth // n_mp, width).swapaxes(0, 1)
+    cut = lax.dynamic_slice_in_dim(kv_weight, half * (depth // n_half), depth // n_half, 1)
+    sides = n_mp // pairs
+    cut = cut.reshape(pairs, depth // n_half, sides, width // sides).swapaxes(1, 2)
+    cut = cut.reshape(n_mp, depth // n_half, width // sides)
     cut = lax.all_to_all(
         cut,
         "tower",
         0,
         0,
         tiled=True,
-        axis_index_groups=[[a * inner + b for a in range(n_mp)] for b in range(inner)],
-    )
-
-    block_rows, stats = conv_rows(tiles, dw_weight, dw_bias, block_gain)
-    channels = tiles.shape[3]
-    gathered = lax.all_gather(block_rows.reshape(-1, channels), "mp", axis=0, tiled=True)
-    gathered, cut = lax.optimization_barrier((gathered, cut))
-    kv_rows = lax.all_gather(
-        lax.all_to_all(cut, "mp", 0, 0, tiled=True), "tower", axis=0, tiled=False
-    )
-    partial = jnp.dot(gathered, proj_weight, preferred_element_type=jnp.float32).astype(
-        jnp.bfloat16
-    )
-    partial, stats, block_gain, block_bias = lax.optimization_barrier(
-        (partial, stats, block_gain, block_bias)
-    )
-    summed = lax.psum_scatter(partial, "seq", scatter_dimension=0, tiled=True)
+        axis_index_groups=[[a * INNER + b for a in range(n_mp)] for b in range(INNER)],
+    )
+    cut = lax.all_to_all(cut, "mp", 0, 0, tiled=True)
+    cut, stats, block_gain, block_bias = lax.optimization_barrier(
+        (cut, stats, block_gain, block_bias)
+    )
+    kv_rows = lax.all_gather(cut, "tower", axis=0, tiled=False)
 
     vectors = split_dot(jnp.stack([block_gain, block_bias]), proj_weight)
+    column_count = vectors.shape[1]
+    own_count = column_count // n_half
+
+    def own_half(row):
+        row = row.reshape(INNER, n_half, -1)
+        return lax.dynamic_index_in_dim(row, half, 1, False).reshape(-1)
+
     stats = stats[..., 0].reshape(2, -1)
     stats = lax.all_gather(stats, "mp", axis=1, tiled=True)
-    rows_here = stats.shape[1] // n_seq
-    stats = stats.reshape(2, n_seq, rows_here).swapaxes(0, 1).reshape(n_seq, -1)
+    rows_here = stats.shape[1] // n_row
+    stats = stats.reshape(2, n_row, rows_here).swapaxes(0, 1).reshape(n_row, 1, -1)
+    vectors = vectors.reshape(2, INNER, n_half, -1).transpose(2, 0, 1, 3).reshape(1, n_half, -1)
     payload = jnp.concatenate(
-        [stats, jnp.broadcast_to(vectors.reshape(1, -1), (n_seq, vectors.size))], 1
-    )
-    payload = lax.all_to_all(payload, "seq", 0, 0, tiled=True)
+        [
+            jnp.broadcast_to(stats, (n_row, n_half, stats.shape[2])),
+            jnp.broadcast_to(vectors, (n_row, n_half, vectors.shape[2])),
+        ],
+        2,
+    ).reshape(n_seq, -1)
+    payload = lax.all_to_all(payload, ("row", "half"), 0, 0, tiled=True)
     means = payload[:, :rows_here]
     squares = payload[:, rows_here : 2 * rows_here]
-    column_count = vectors.shape[1]
-    gain_rows = payload[:, 2 * rows_here : 2 * rows_here + column_count]
-    bias_row = jnp.sum(payload[:, 2 * rows_here + column_count :], 0) + proj_bias
+    gain_rows = payload[:, 2 * rows_here : 2 * rows_here + own_count]
+    bias_row = jnp.sum(payload[:, 2 * rows_here + own_count :], 0) + own_half(proj_bias)
 
     picked = jnp.arange(directions.shape[0], dtype=jnp.int32)[:, None] == dir_index[0]
     chosen = jnp.sum(jnp.where(picked, directions, 0.0), 0)
     unit_dir = chosen / jnp.sqrt(jnp.sum(chosen * chosen))
-    local_unit = lax.dynamic_slice_in_dim(
-        unit_dir, lax.axis_index("mp") * column_count, column_count, 0
+    local_unit = own_half(
+        lax.dynamic_slice_in_dim(
+            unit_dir, lax.axis_index("mp") * column_count, column_count, 0
+        )
     )
 
     half_head = HEAD // 2
@@ -319,7 +368,10 @@
     cosine = jnp.tile(jnp.cos(angles), (1, 2))
     sine_part = jnp.sin(angles)
     sine = jnp.concatenate([-sine_part, sine_part], 1)
-    row_ids = lax.axis_index("seq") * rows_here + jnp.arange(rows_here, dtype=jnp.int32)
+    out_rows = rows_here // n_half
+    row_ids = (lax.axis_index("row") * n_half + half) * out_rows + jnp.arange(
+        out_rows, dtype=jnp.int32
+    )
     row_valid = (row_ids // (SIDE * SIDE) < tile_counts[0]).astype(jnp.float32)[:, None]
     row_valid = jnp.broadcast_to(row_valid, cosine.shape)
 
@@ -330,33 +382,40 @@
         gain_rows,
         bias_row[None],
         local_unit[None],
-        rms_gain[None],
+        own_half(rms_gain)[None],
         kv_rows,
-    )
-    pieces = lax.all_to_all(pieces, "mp", 0, 0, tiled=True)
+        n_half,
+    )
+    pieces = pieces.reshape(n_half * n_mp, *pieces.shape[2:])
+    pieces = lax.all_to_all(pieces, ("half", "mp"), 0, 0, tiled=True)
     return end_rows(pieces, kv_bias, cosine, sine, row_valid)
 
 
 def solution(mesh):
+    towers, seq, mp = mesh.devices.shape
+    mesh = jax.sharding.Mesh(
+        mesh.devices.reshape(towers, seq // 2, 2, mp), ("tower", "row", "half", "mp")
+    )
+    seq = ("row", "half")
     return jax.shard_map(
         local,
         mesh=mesh,
         in_specs=(
-            P(("tower", "mp"), None, None, "seq"),
-            P(None, None, "seq"),
-            P("seq"),
-            P("seq"),
-            P("seq"),
-            P("seq", "mp"),
+            P(("tower", "mp"), None, None, seq),
+            P(None, None, seq),
+            P(seq),
+            P(seq),
+            P(seq),
+            P(seq, "mp"),
             P("mp"),
             P(),
             P("tower"),
             P("tower"),
-            P("tower", "seq"),
+            P("tower", seq),
             P("mp"),
             P(None, "tower", "mp"),
             P(None, "mp"),
         ),
-        out_specs=P("tower", None, "seq", "mp"),
+        out_specs=P("tower", None, seq, "mp"),
         check_vma=False,
     )

time: 144 us -> 150 us (1.042)
  blocking collectives: 31.2 us -> 50.8 us
  waiting for transfers between devices: 50.7 us -> 38.1 us
  starting transfers between devices: 21.8 us -> 11.9 us
  Pallas kernels: 11 us -> 20.7 us
  matrix products: 4.63 us -> 0.32 us
  local copies, waits for them, and re-layouts: 3.91 us -> 7.66 us
    all_to_all x1 -> x2, blocking collectives: 10.2 us -> 27.6 us  [the longest x1 18.9 us: local(): lax.all_to_all(cut, 'tower', 0, 0, tiled=True, axis_index_groups=[[a * IN...]
    reduce_scatter x1, waiting for transfers between devices: 22.8 us -> 6.61 us  [local(): lax.psum_scatter(partial, ('row', 'half'), scatter_dimension=0, tiled=True)]
    all_to_all x3 -> x2, starting transfers between devices: 21.8 us -> 11.9 us  [the longest x1 6.83 us: local(): payload = lax.all_to_all(payload, ('row', 'half'), 0, 0, tiled=True)]
    pallas_call x0 -> x1, Pallas kernels: none -> 6.01 us  [project(): pl.pallas_call(project_kernel, grid=(groups,), in_specs=[pl.BlockSpec((co...]
    dot_general x1 -> x0, matrix products: 4.31 us -> none  [local(): jnp.dot(gathered, proj_weight, preferred_element_type=jnp.float32)]
    all_to_all x3 -> x2, waiting for transfers between devices: 18.1 us -> 21.6 us  [the longest x1 13.8 us: local(): pieces = lax.all_to_all(pieces, ('half', 'mp'), 0, 0, tiled=True)]
    transpose x1 -> x0, local copies, waits for them, and re-layouts: 2.01 us -> none  [local(): cut = kv_weight.reshape(pairs, n_mp, depth // n_mp, width).swapaxes(0, 1)]
    pallas_call x1, Pallas kernels: 2.13 us -> 4.01 us  [conv_rows(): pl.pallas_call(conv_kernel, grid=(count,), in_specs=[pl.BlockSpec((1, cel...]
  transfers between devices with their start and end apart: 5 -> 4, of which waited for: 4 -> 4; matrix products, arithmetic and copies ran while one was open for 3% -> 4% of each run, Pallas kernels for 1% -> 0%
where the time goes in v3:
time: 150 us
  blocking collectives  50.8 us (34%)
  waiting for transfers between devices  38.1 us (25%)
  Pallas kernels  20.7 us (14%)
  between operations  17.1 us (11%)
  starting transfers between devices  11.9 us (8%)
  local copies, waits for them, and re-layouts  7.66 us (5%)
  other arithmetic  3.14 us (2%)
    all_to_all x1, blocking collectives, local(): lax.all_to_all(cut, 'tower', 0, 0, tiled=True, axis_index_groups=[[a * IN...  18.9 us
    all_gather x1, blocking collectives, local(): lax.all_gather(block_rows.reshape(-1, channels), 'mp', axis=0, tiled=True)  14 us
    all_to_all x1, waiting for transfers between devices, local(): pieces = lax.all_to_all(pieces, ('half', 'mp'), 0, 0, tiled=True)  13.8 us
    all_gather x1, waiting for transfers between devices, local(): kv_rows = lax.all_gather(cut, 'tower', axis=0, tiled=False)  9.8 us
    all_gather x1, blocking collectives, local(): stats = lax.all_gather(stats, 'mp', axis=1, tiled=True)  9.11 us
    all_to_all x1, blocking collectives, local(): cut = lax.all_to_all(cut, 'mp', 0, 0, tiled=True)  8.71 us
    pallas_call x1, Pallas kernels, kv_partial(): pl.pallas_call(kv_kernel, grid=(groups,), in_specs=[*(whole(a) for a in (...  8.18 us
    all_to_all x1, waiting for transfers between devices, local(): payload = lax.all_to_all(payload, ('row', 'half'), 0, 0, tiled=True)  7.79 us
  transfers between devices with their start and end apart: 4, of which 4 were waited for; matrix products, arithmetic and copies ran while one was open for 4% of the time, Pallas kernels for 0%

profile of v3, /device:TPU:1, one launch (start us, length us, event | category | flops | bytes accessed | tf_op | source)
XLA Modules:
  0.0 149.7 jit_solution(16973701798160517974)
XLA Ops:
  7.4 1.2 broadcast_in_dim.42.shift_ref
  8.6 1.2 broadcast_in_dim.43.gain_ref
  9.9 4.0 %shard_map.136 = (bf16[4,8,8,384]{3,2,1,0:T(8,128)(2,1)}, f32[2,4,8,8,128]{4,3,2,1,0:T(8,128)}) custom-call(bf16[4,8,8,384]{3,2,1,0:T(8,128)(2,1)} %tile_ref.1, f32[7,7,384]{2,1,0:T(8,128)} %weight_ref.2, f32[1,384]{1,0:T(1,128)} %broadcast_in_dim.42.shift_ref, f32[1,384]{1,0:T(1,128)} %broadcast_in_dim.43.gain_ref), custom_call_target="tpu_custom_call" | custom-call | tf_op jit(solution)/shard_map/pallas_call | solution.py:62
  13.9 14.0 %all_gather.12.rows_ref = bf16[1024,384]{1,0:T(8,128)(2,1)} all-gather(bf16[256,384]{1,0:T(8,128)(2,1)} %bitcast.35), channel_id=1, replica_groups=mesh['tower'=16,'row'=4,'half'=2,'mp'=4] {'mp'}, dimensions={0}, use_global_device_ids=true | all-gather | bytes 983040 | tf_op jit(solution)/shard_map/all_gather | solution.py:304
  27.9 6.0 %shard_map.137 = bf16[8,256,1024]{2,1,0:T(8,128)(2,1)} custom-call(bf16[1024,384]{1,0:T(8,128)(2,1)} %all_gather.12.rows_ref, bf16[384,2048]{1,0:T(8,128)(2,1)} %weight_ref.3), custom_call_target="tpu_custom_call" | custom-call | tf_op jit(solution)/shard_map/pallas_call | solution.py:124
  34.0 0.9 copy-done.4
  35.0 18.9 %all_to_all.27 = bf16[4,256,128]{2,1,0:T(8,128)(2,1)S(1)} all-to-all(bf16[4,256,128]{2,1,0:T(8,128)(2,1)S(1)} %bitcast.30), channel_id=1, replica_groups={{0,128,256,384},{32,160,288,416},{64,192,320,448},{96,224,352,480},{1,1..., dimensions={0} | all-to-all | bytes 524288 | tf_op jit(solution)/shard_map/all_to_all | solution.py:314
  53.9 8.7 %all_to_all.28 = bf16[4,256,128]{2,1,0:T(8,128)(2,1)} all-to-all(bf16[4,256,128]{2,1,0:T(8,128)(2,1)S(1)} %all_to_all.27), channel_id=1, replica_groups=mesh['tower'=16,'row'=4,'half'=2,'mp'=4] {'mp'}, dimensions={0} | all-to-all | bytes 524288 | tf_op jit(solution)/shard_map/all_to_all | solution.py:322
  63.4 0.2 select_reduce_fusion
  63.5 0.6 multiply_reduce_fusion
  64.9 0.3 fusion.1
  65.3 0.1 slice_reduce_fusion
  65.5 0.1 reshape_squeeze.3
  65.6 9.1 %all_gather.13 = f32[2,1024]{1,0:T(2,128)S(1)} all-gather(f32[2,256]{1,0:T(2,128)S(1)} %reshape_squeeze.3), channel_id=1, replica_groups=mesh['tower'=16,'row'=4,'half'=2,'mp'=4] {'mp'}, dimensions={1}, use_global_device_ids=true | all-gather | bytes 10240 | tf_op jit(solution)/shard_map/all_gather | solution.py:337
  74.8 0.8 all_to_all.19
  75.5 6.8 %all-to-all-start.2 = ((f32[8,1,2560]{2,1,0:T(1,128)}), f32[8,1,2560]{2,1,0:T(1,128)S(1)}, u32[]{:S(2)}, u32[]{:S(2)}) async-start(f32[8,1,2560]{2,1,0:T(1,128)} %all_to_all.19), calls=%async_computation.3 | async-start | bytes 163840 | tf_op jit(solution)/shard_map/all_to_all | solution.py:348
  82.4 0.6 constant_dynamic-slice_fusion.1
  83.0 7.8 %all-to-all-done.2 = f32[8,1,2560]{2,1,0:T(1,128)S(1)} async-done(((f32[8,1,2560]{2,1,0:T(1,128)}), f32[8,1,2560]{2,1,0:T(1,128)S(1)}, u32[]{:S(2)}, u32[]{:S(2)}) %all-to-all-start.2) | async-done | bytes 81952 | tf_op jit(solution)/shard_map/all_to_all | solution.py:348
  90.8 0.6 slice_reduce_fusion.1
  91.4 0.6 add.52.bias_ref
  92.0 0.6 fusion.10
  92.7 6.6 %reduce-scatter.2.cloned.1.call-done = bf16[1,256,1024]{2,1,0:T(8,128)(2,1)} async-done(((bf16[8,256,1024]{2,1,0:T(8,128)(2,1)}), bf16[1,256,1024]{2,1,0:T(8,128)(2,1)}) %reduce-scatter.2.cloned.1.call-update) | async-done | bytes 524304 | tf_op jit(solution)/shard_map/reduce_scatter | solution.py:307
  99.3 9.8 %all-gather.3.cloned.1.call-done = bf16[64,256,128]{2,1,0:T(8,128)(2,1)} async-done(((bf16[4,256,128]{2,1,0:T(8,128)(2,1)}), bf16[64,256,128]{2,1,0:T(8,128)(2,1)}) %all-gather.3.cloned.1.call-update) | async-done | bytes 4194320 | tf_op jit(solution)/shard_map/all_gather | solution.py:326
  109.1 8.2 %shard_map.138 = bf16[2,4,144,512]{3,2,1,0:T(8,128)(2,1)} custom-call(bf16[256,1024]{1,0:T(8,128)(2,1)} %bitcast.31, f32[8,256]{1,0:T(8,128)} %get-tuple-element.26.means_ref, f32[8,256]{1,0:T(8,128)} %get-tuple-element.25.squares_ref, f32[8,1024]{1,0:T(8,128)} %get-tuple-element.24.gains_ref, f32[1,1024]{1,0:T(1,128)} %add.52.bias_ref, f32[1,1024]{1,0:T(1,128)} %bitcast.39, ...), custom_call_target="tpu_custom_call" | custom-call | tf_op jit(solution)/shard_map/pallas_call | solution.py:222
  117.3 5.0 %all-to-all-start.3 = ((bf16[8,144,512]{2,1,0:T(8,128)(2,1)}), bf16[8,144,512]{2,1,0:T(8,128)(2,1)S(1)}, u32[]{:S(2)}, u32[]{:S(2)}) async-start(bf16[8,144,512]{2,1,0:T(8,128)(2,1)} %bitcast.28), calls=%async_computation.4 | async-start | bytes 2359296 | tf_op jit(solution)/shard_map/all_to_all | solution.py:390
  122.3 0.3 fusion
  122.7 0.7 copy.21.cosine_ref
  124.1 0.7 pad_maximum_fusion.2.sine_ref
  124.8 13.8 %all-to-all-done.3.pieces_ref = bf16[8,144,512]{2,1,0:T(8,128)(2,1)S(1)} async-done(((bf16[8,144,512]{2,1,0:T(8,128)(2,1)}), bf16[8,144,512]{2,1,0:T(8,128)(2,1)S(1)}, u32[]{:S(2)}, u32[]{:S(2)}) %all-to-all-start.3) | async-done | bytes 1179680 | tf_op jit(solution)/shard_map/all_to_all | solution.py:390
  138.7 0.8 broadcast_in_dim.50.valid_ref
  139.5 0.2 copy-done.1
  139.7 2.5 %shard_map.139 = bf16[1,2,128,256]{3,2,1,0:T(8,128)(2,1)} custom-call(bf16[8,144,512]{2,1,0:T(8,128)(2,1)} %copy-done.1, f32[2,256]{1,0:T(2,128)} %bias_ref.1, f32[128,128]{1,0:T(8,128)} %copy.21.cosine_ref, f32[128,128]{1,0:T(8,128)} %pad_maximum_fusion.2.sine_ref, f32[128,128]{1,0:T(8,128)} %broadcast_in_dim.50.valid_ref), custom_call_target="tpu_custom_call" | custom-call | tf_op jit(solution)/shard_map/pallas_call | solution.py:273
  (45 shorter events, 0.5 us)
Async XLA Ops:
  7.4 91.9 %reduce-scatter.2.cloned.1.call-start = ((), (), s32[]{:S(2)}) async-start(), calls=%async_computation.5 | async-start | bytes 4718592 | tf_op jit(solution)/shard_map/reduce_scatter | solution.py:307
  33.9 1.0 copy-start.4
  33.9 28.7 %copy-start.6 = (f32[2048]{0:T(1024)S(1)}, f32[2048]{0:T(1024)}, u32[]{:S(2)}) copy-start(f32[2048]{0:T(1024)} %param.20) | copy-start | bytes 24580
  33.9 29.4 %copy-start.2 = (f32[16,8192]{1,0:T(8,128)S(1)}, f32[16,8192]{1,0:T(8,128)}, u32[]{:S(2)}) copy-start(f32[16,8192]{1,0:T(8,128)} %param.21) | copy-start | bytes 1572868
  33.9 30.9 %copy-start.8 = (f32[384]{0:T(512)S(1)}, f32[384]{0:T(512)}, u32[]{:S(2)}) copy-start(f32[384]{0:T(512)} %param.18) | copy-start | bytes 4612
  34.0 30.9 %copy-start.5 = (f32[384]{0:T(512)S(1)}, f32[384]{0:T(512)}, u32[]{:S(2)}) copy-start(f32[384]{0:T(512)} %param.17) | copy-start | bytes 4612
  34.0 31.0 %copy-start = (bf16[384,2048]{1,0:T(8,128)(2,1)S(1)}, bf16[384,2048]{1,0:T(8,128)(2,1)}, u32[]{:S(2)}) copy-start(bf16[384,2048]{1,0:T(8,128)(2,1)} %weight_ref.3) | copy-start | bytes 4718596
  34.0 75.1 %all-gather.3.cloned.1.call-start = ((), (), s32[]{:S(2)}) async-start(), calls=%async_computation.6 | async-start | bytes 4456448 | tf_op jit(solution)/shard_map/all_gather | solution.py:326
  53.9 11.4 %copy-start.3 = (f32[2,4,8,8,128]{4,3,2,1,0:T(8,128)S(1)}, f32[2,4,8,8,128]{4,3,2,1,0:T(8,128)}, u32[]{:S(2)}) copy-start(f32[2,4,8,8,128]{4,3,2,1,0:T(8,128)} %get-tuple-element.17) | copy-start | bytes 786436
  63.4 19.0 %copy-start.7 = (f32[2048]{0:T(1024)S(1)}, f32[2048]{0:T(1024)}, u32[]{:S(2)}) copy-start(f32[2048]{0:T(1024)} %param.25) | copy-start | bytes 24580
  75.5 15.3 %all-to-all-start.2 = ((f32[8,1,2560]{2,1,0:T(1,128)}), f32[8,1,2560]{2,1,0:T(1,128)S(1)}, u32[]{:S(2)}, u32[]{:S(2)}) async-start(f32[8,1,2560]{2,1,0:T(1,128)} %all_to_all.19), calls=%async_computation.3 | async-start | bytes 163840 | tf_op jit(solution)/shard_map/all_to_all | solution.py:348
  117.3 5.0 %copy-start.9 = (s32[1,128]{1,0:T(1,128)S(1)}, s32[1,128]{1,0:T(1,128)}, u32[]{:S(2)}) copy-start(s32[1,128]{1,0:T(1,128)} %param.24) | copy-start | bytes 1540
  117.3 21.4 %all-to-all-start.3 = ((bf16[8,144,512]{2,1,0:T(8,128)(2,1)}), bf16[8,144,512]{2,1,0:T(8,128)(2,1)S(1)}, u32[]{:S(2)}, u32[]{:S(2)}) async-start(bf16[8,144,512]{2,1,0:T(8,128)(2,1)} %bitcast.28), calls=%async_computation.4 | async-start | bytes 2359296 | tf_op jit(solution)/shard_map/all_to_all | solution.py:390
  138.7 1.0 copy-start.1
Sparse Core Ops, SparseCore 0:
  34.0 65.1 reduce-scatter.1
Sparse Core Ops, SparseCore 1:
  62.7 46.3 all-gather.2

commit v4 on v2

--- a/solution.py
+++ b/solution.py
@@ -102,71 +102,86 @@
 
 EXTRA = 16
 STEP = 16
-
-
-def kv_kernel(
-    summed_ref, means_ref, squares_ref, gains_ref, bias_ref, unit_ref, scale_ref, weight_ref,
-    out_ref, rows, stats,
+PLACES = 8
+
+
+def hidden_kernel(
+    summed_ref, means_ref, squares_ref, gains_ref, bias_ref, unit_ref, scale_ref, rows_ref, sums_ref,
+    stats,
 ):
     count, features = summed_ref.shape
-    towers, _, _, depth, width = weight_ref.shape
     n_seq = means_ref.shape[0]
-    inner = features // depth // 4
-
-    @pl.when(pl.program_id(0) == 0)
-    def _():
-        means = means_ref[...]
-        average = jnp.sum(means, 0, keepdims=True) / n_seq
-        offsets = means - average
-        block = C // n_seq
-        variance = (
-            jnp.sum(squares_ref[...], 0, keepdims=True)
-            + block * jnp.sum(offsets * offsets, 0, keepdims=True)
-        ) / C
-        inverse = lax.rsqrt(variance + epsilon)
-        columns = jnp.transpose(
-            jnp.concatenate([offsets, jnp.broadcast_to(inverse, (n_seq, count))], 0)
-        )
-        unit = unit_ref[...]
-        gain = scale_ref[...]
-        unit_square = jnp.sum(unit * unit)
-        for begin in range(0, count, STEP):
-            here = slice(begin, begin + STEP)
-            value = summed_ref[here, :].astype(jnp.float32)
-            for source in range(n_seq):
-                value = value + columns[here, source : source + 1] * gains_ref[source : source + 1, :]
-            value = value * columns[here, n_seq : n_seq + 1] + bias_ref[...]
-            hidden = 0.5 * value * (1.0 + lax.erf(value * 0.7071067811865476))
-            along = jnp.sum(hidden * unit, -1, keepdims=True)
-            across = hidden - (along / unit_square) * unit
-            square = jnp.sum(across * across, -1, keepdims=True)
-            lane = lax.broadcasted_iota(jnp.int32, (STEP, count), 1)
-            stats[here, :] = jnp.where(lane == 0, along, jnp.where(lane == 1, square, unit_square))
-            scaled = (across * gain).astype(jnp.bfloat16)
-            for place in range(features // depth):
-                first, second = place // inner, place % inner
-                source = second * 4 + first
-                rows[here, place * depth : (place + 1) * depth] = scaled[
-                    :, source * depth : (source + 1) * depth
-                ]
-        parts = jnp.concatenate(
-            [*three_parts(unit * gain), jnp.zeros((EXTRA - 3, features), jnp.float32)], 0
-        ).astype(jnp.bfloat16)
-        for place in range(features // depth):
-            first, second = place // inner, place % inner
-            source = second * 4 + first
-            rows[count:, place * depth : (place + 1) * depth] = parts[
+    depth = features // PLACES
+    inner = PLACES // 2
+
+    def store(here, value):
+        for place in range(PLACES):
+            source = (place % inner) * 2 + place // inner
+            rows_ref[here, place * depth : (place + 1) * depth] = value[
                 :, source * depth : (source + 1) * depth
             ]
 
-    turned = jnp.transpose(stats[...])[:8]
+    means = means_ref[...]
+    average = jnp.sum(means, 0, keepdims=True) / n_seq
+    offsets = means - average
+    block = C // n_seq
+    variance = (
+        jnp.sum(squares_ref[...], 0, keepdims=True)
+        + block * jnp.sum(offsets * offsets, 0, keepdims=True)
+    ) / C
+    inverse = lax.rsqrt(variance + epsilon)
+    columns = jnp.transpose(
+        jnp.concatenate([offsets, jnp.broadcast_to(inverse, (n_seq, count))], 0)
+    )
+    unit = unit_ref[...]
+    gain = scale_ref[...]
+    unit_square = jnp.sum(unit * unit)
+    for begin in range(0, count, STEP):
+        here = slice(begin, begin + STEP)
+        value = summed_ref[here, :].astype(jnp.float32)
+        for source in range(n_seq):
+            value = value + columns[here, source : source + 1] * gains_ref[source : source + 1, :]
+        value = value * columns[here, n_seq : n_seq + 1] + bias_ref[...]
+        hidden = 0.5 * value * (1.0 + lax.erf(value * 0.7071067811865476))
+        along = jnp.sum(hidden * unit, -1, keepdims=True)
+        across = hidden - (along / unit_square) * unit
+        square = jnp.sum(across * across, -1, keepdims=True)
+        lane = lax.broadcasted_iota(jnp.int32, (STEP, count), 1)
+        stats[here, :] = jnp.where(lane == 0, along, jnp.where(lane == 1, square, unit_square))
+        store(here, (across * gain).astype(jnp.bfloat16))
+    store(
+        slice(count, count + EXTRA),
+        jnp.concatenate(
+            [*three_parts(unit * gain), jnp.zeros((EXTRA - 3, features), jnp.float32)], 0
+        ).astype(jnp.bfloat16),
+    )
+    sums_ref[...] = jnp.transpose(stats[...])[:8]
+
+
+def hidden_rows(summed, means, squares, gains, bias, unit, scale):
+    count, features = summed.shape
+    return pl.pallas_call(
+        hidden_kernel,
+        out_shape=[
+            jax.ShapeDtypeStruct((count + EXTRA, features), jnp.bfloat16),
+            jax.ShapeDtypeStruct((8, count), jnp.float32),
+        ],
+        scratch_shapes=[pltpu.VMEM((count, count), jnp.float32)],
+        compiler_params=pltpu.CompilerParams(vmem_limit_bytes=32 * 2**20),
+    )(summed, means, squares, gains, bias, unit, scale)
+
+
+def kv_kernel(rows_ref, sums_ref, weight_ref, out_ref):
+    count = rows_ref.shape[0] - EXTRA
+    features = rows_ref.shape[1]
+    width = weight_ref.shape[3]
     for pair in range(2):
         there = slice(pair * width, (pair + 1) * width)
-        weight = weight_ref[:, 0, pair].reshape(towers * depth, width)
-        total = jnp.dot(rows[...], weight, preferred_element_type=jnp.float32)
+        weight = weight_ref[pair * PLACES : (pair + 1) * PLACES, 0].reshape(features, width)
+        total = jnp.dot(rows_ref[...], weight, preferred_element_type=jnp.float32)
         out_ref[0, :count, there] = total[:count].astype(out_ref.dtype)
         vector = total[count : count + 1] + total[count + 1 : count + 2] + total[count + 2 : count + 3]
-        line = jnp.concatenate([turned[pair : pair + 1], turned[2:3]], 1)
+        line = jnp.concatenate([sums_ref[pair : pair + 1], sums_ref[2:3]], 1)
         extra = jnp.concatenate(
             [
                 *three_parts(vector),
@@ -178,28 +193,20 @@
         out_ref[0, count:, there] = extra.astype(out_ref.dtype)
 
 
-def kv_partial(summed, means, squares, gains, bias, unit, scale, weight):
-    count, features = summed.shape
-    towers, groups, pairs, depth, width = weight.shape
-
-    def whole(array):
-        return pl.BlockSpec(array.shape, lambda g: (0,) * array.ndim)
-
+def kv_partial(rows, sums, weight):
+    towers, groups, depth, width = weight.shape
     return pl.pallas_call(
         kv_kernel,
         grid=(groups,),
         in_specs=[
-            *(whole(a) for a in (summed, means, squares, gains, bias, unit, scale)),
-            pl.BlockSpec((towers, 1, pairs, depth, width), lambda g: (0, g, 0, 0, 0)),
-        ],
-        out_specs=pl.BlockSpec((1, count + EXTRA, pairs * width), lambda g: (g, 0, 0)),
-        out_shape=jax.ShapeDtypeStruct((groups, count + EXTRA, pairs * width), jnp.bfloat16),
-        scratch_shapes=[
-            pltpu.VMEM((count + EXTRA, features), jnp.bfloat16),
-            pltpu.VMEM((count, count), jnp.float32),
-        ],
-        compiler_params=pltpu.CompilerParams(vmem_limit_bytes=56 * 2**20),
-    )(summed, means, squares, gains, bias, unit, scale, weight)
+            pl.BlockSpec(rows.shape, lambda g: (0, 0)),
+            pl.BlockSpec(sums.shape, lambda g: (0, 0)),
+            pl.BlockSpec((towers, 1, depth, width), lambda g: (0, g, 0, 0)),
+        ],
+        out_specs=pl.BlockSpec((1, rows.shape[0], 2 * width), lambda g: (g, 0, 0)),
+        out_shape=jax.ShapeDtypeStruct((groups, rows.shape[0], 2 * width), jnp.bfloat16),
+        compiler_params=pltpu.CompilerParams(vmem_limit_bytes=58 * 2**20),
+    )(rows, sums, weight)
 
 
 def end_kernel(pieces_ref, bias_ref, cosine_ref, sine_ref, valid_ref, out_ref):
@@ -264,7 +271,7 @@
     n_tower = lax.axis_size("tower")
     pairs, depth, width = kv_weight.shape
     inner = n_tower // n_mp
-    cut = kv_weight.reshape(pairs, n_mp, depth // n_mp, width).swapaxes(0, 1)
+    cut = kv_weight.reshape(n_mp, pairs * depth // n_mp, width)
     cut = lax.all_to_all(
         cut,
         "tower",
@@ -323,7 +330,7 @@
     row_valid = (row_ids // (SIDE * SIDE) < tile_counts[0]).astype(jnp.float32)[:, None]
     row_valid = jnp.broadcast_to(row_valid, cosine.shape)
 
-    pieces = kv_partial(
+    rows, sums = hidden_rows(
         summed,
         means,
         squares,
@@ -331,8 +338,8 @@
         bias_row[None],
         local_unit[None],
         rms_gain[None],
-        kv_rows,
-    )
+    )
+    pieces = kv_partial(rows, sums, kv_rows)
     pieces = lax.all_to_all(pieces, "mp", 0, 0, tiled=True)
     return end_rows(pieces, kv_bias, cosine, sine, row_valid)
 

time: 144 us -> 143 us (level)
  local copies, waits for them, and re-layouts: 3.91 us -> 7 us
  waiting for transfers between devices: 50.7 us -> 48.6 us
  other arithmetic: 3.08 us -> 1.27 us
    all_gather x1, waiting for transfers between devices: 9.73 us -> 5.19 us  [local(): lax.all_gather(lax.all_to_all(cut, 'mp', 0, 0, tiled=True), 'tower', axis...]
    unnamed x23 -> x29, local copies, waits for them, and re-layouts: 0.06 us -> 4.4 us
    reduce_scatter x1, waiting for transfers between devices: 22.8 us -> 25.2 us  [local(): summed = lax.psum_scatter(partial, 'seq', scatter_dimension=0, tiled=True)]
    transpose x1 -> x0, local copies, waits for them, and re-layouts: 2.01 us -> none  [local(): cut = kv_weight.reshape(pairs, n_mp, depth // n_mp, width).swapaxes(0, 1)]
    pallas_call x1 -> x2, Pallas kernels: 7.77 us -> 7.85 us  [the longest x1 5.88 us: kv_partial(): pl.pallas_call(kv_kernel, grid=(groups,), in_specs=[pl.BlockSpec(rows.sha...]
  transfers between devices with their start and end apart: 5 -> 5, of which waited for: 4 -> 4; matrix products, arithmetic and copies ran while one was open for 3% -> 2% of each run, Pallas kernels for 1% -> 3%
where the time goes in v4:
time: 143 us
  waiting for transfers between devices  48.6 us (34%)
  blocking collectives  31.2 us (22%)
  starting transfers between devices  21.9 us (15%)
  between operations  17.1 us (12%)
  Pallas kernels  11.2 us (8%)
  local copies, waits for them, and re-layouts  7 us (5%)
  matrix products  4.63 us (3%)
    reduce_scatter x1, waiting for transfers between devices, local(): summed = lax.psum_scatter(partial, 'seq', scatter_dimension=0, tiled=True)  25.2 us
    all_gather x1, blocking collectives, local(): lax.all_gather(block_rows.reshape(-1, channels), 'mp', axis=0, tiled=True)  12.6 us
    all_to_all x1, starting transfers between devices, local(): lax.all_to_all(cut, 'tower', 0, 0, tiled=True, axis_index_groups=[[a * in...  11 us
    all_to_all x1, blocking collectives, local(): lax.all_to_all(cut, 'mp', 0, 0, tiled=True)  10.2 us
    all_to_all x1, waiting for transfers between devices, local(): payload = lax.all_to_all(payload, 'seq', 0, 0, tiled=True)  9.65 us
    all_to_all x1, waiting for transfers between devices, local(): pieces = lax.all_to_all(pieces, 'mp', 0, 0, tiled=True)  8.46 us
    all_gather x1, blocking collectives, local(): stats = lax.all_gather(stats, 'mp', axis=1, tiled=True)  8.4 us
    all_to_all x1, starting transfers between devices, local(): payload = lax.all_to_all(payload, 'seq', 0, 0, tiled=True)  6.82 us
  transfers between devices with their start and end apart: 5, of which 4 were waited for; matrix products, arithmetic and copies ran while one was open for 2% of the time, Pallas kernels for 3%

profile of v4, /device:TPU:1, one launch (start us, length us, event | category | flops | bytes accessed | tf_op | source)
XLA Modules:
  0.0 142.9 jit_solution(5130353525356036643)
XLA Ops:
  7.4 11.0 %all-to-all-start = ((bf16[4,256,256]{2,1,0:T(8,128)(2,1)}), bf16[4,256,256]{2,1,0:T(8,128)(2,1)S(1)}, u32[]{:S(2)}, u32[]{:S(2)}) async-start(bf16[4,256,256]{2,1,0:T(8,128)(2,1)} %bitcast.40), calls=%async_computation | async-start | bytes 1048576 | tf_op jit(solution)/shard_map/all_to_all | solution.py:275
  18.4 0.7 broadcast_in_dim.43.shift_ref
  19.0 0.7 broadcast_in_dim.44.gain_ref
  19.7 0.9 copy-done.3
  20.6 0.9 copy-done.4
  21.5 2.3 %shard_map.136 = (bf16[4,8,8,384]{3,2,1,0:T(8,128)(2,1)S(1)}, f32[2,4,8,8,128]{4,3,2,1,0:T(8,128)S(1)}) custom-call(bf16[4,8,8,384]{3,2,1,0:T(8,128)(2,1)S(1)} %copy-done.3, f32[7,7,384]{2,1,0:T(8,128)S(1)} %copy-done.4, f32[1,384]{1,0:T(1,128)S(1)} %broadcast_in_dim.43.shift_ref, f32[1,384]{1,0:T(1,128)S(1)} %broadcast_in_dim.44.gain_ref), custom_call_target="tpu_custom_call" | custom-call | tf_op jit(solution)/shard_map/pallas_call | solution.py:61
  23.8 12.6 %all_gather.12 = bf16[1024,384]{1,0:T(8,128)(2,1)S(1)} all-gather(bf16[256,384]{1,0:T(8,128)(2,1)S(1)} %bitcast.33), channel_id=1, replica_groups=mesh['tower'=16,'seq'=8,'mp'=4] {'mp'}, dimensions={0}, use_global_device_ids=true | all-gather | bytes 983040 | tf_op jit(solution)/shard_map/all_gather | solution.py:286
  36.4 4.3 %convolution_convert_fusion = bf16[1024,2048]{1,0:T(8,128)(2,1)} fusion(bf16[1024,384]{1,0:T(8,128)(2,1)S(1)} %all_gather.12, bf16[384,2048]{1,0:T(8,128)(2,1)S(1)} %copy-done), kind=kOutput, calls=%fused_computation | convolution fusion | flops 1612709888 | bytes 6553600 | tf_op jit(solution)/shard_map/dot_general | solution.py:291
  40.8 10.2 %all_to_all.27 = bf16[4,256,256]{2,1,0:T(8,128)(2,1)} all-to-all(bf16[4,256,256]{2,1,0:T(8,128)(2,1)S(1)} %all-to-all-done), channel_id=1, replica_groups=mesh['tower'=16,'seq'=8,'mp'=4] {'mp'}, dimensions={0} | all-to-all | bytes 1048576 | tf_op jit(solution)/shard_map/all_to_all | solution.py:289
  51.7 0.2 select_reduce_fusion
  51.9 0.6 multiply_reduce_fusion
  53.3 0.3 fusion.2
  53.6 0.1 slice_reduce_fusion
  53.8 0.1 reshape_squeeze.3
  53.9 8.4 %all_gather.13 = f32[2,1024]{1,0:T(2,128)S(1)} all-gather(f32[2,256]{1,0:T(2,128)S(1)} %reshape_squeeze.3), channel_id=1, replica_groups=mesh['tower'=16,'seq'=8,'mp'=4] {'mp'}, dimensions={1}, use_global_device_ids=true | all-gather | bytes 10240 | tf_op jit(solution)/shard_map/all_gather | solution.py:301
  62.3 0.7 all_to_all.18
  63.1 6.8 %all-to-all-start.1 = ((f32[8,1,4352]{2,1,0:T(1,128)}), f32[8,1,4352]{2,1,0:T(1,128)S(1)}, u32[]{:S(2)}, u32[]{:S(2)}) async-start(f32[8,1,4352]{2,1,0:T(1,128)} %all_to_all.18), calls=%async_computation.2 | async-start | bytes 278528 | tf_op jit(solution)/shard_map/all_to_all | solution.py:307
  69.9 9.6 %all-to-all-done.1 = f32[8,1,4352]{2,1,0:T(1,128)S(1)} async-done(((f32[8,1,4352]{2,1,0:T(1,128)}), f32[8,1,4352]{2,1,0:T(1,128)S(1)}, u32[]{:S(2)}, u32[]{:S(2)}) %all-to-all-start.1) | async-done | bytes 139296 | tf_op jit(solution)/shard_map/all_to_all | solution.py:307
  79.6 25.2 %reduce-scatter.2.cloned.1.call-done.summed_ref = bf16[128,2048]{1,0:T(8,128)(2,1)} async-done(((bf16[1024,2048]{1,0:T(8,128)(2,1)}), bf16[128,2048]{1,0:T(8,128)(2,1)}) %reduce-scatter.2.cloned.1.call-update) | async-done | bytes 524304 | tf_op jit(solution)/shard_map/reduce_scatter | solution.py:297
  104.8 1.1 copy-done.2
  105.9 2.0 %shard_map.137 = (bf16[144,2048]{1,0:T(8,128)(2,1)S(1)}, f32[8,128]{1,0:T(8,128)S(1)}) custom-call(bf16[128,2048]{1,0:T(8,128)(2,1)S(1)} %copy-done.2, f32[8,128]{1,0:T(8,128)S(1)} %get-tuple-element.28.means_ref, f32[8,128]{1,0:T(8,128)S(1)} %get-tuple-element.27.squares_ref, f32[8,2048]{1,0:T(8,128)S(1)} %get-tuple-element.26.gains_ref, ...), custom_call_target="tpu_custom_call" | custom-call | tf_op jit(solution)/shard_map/pallas_call | solution.py:163
  107.9 0.9 copy-done.1
  108.8 0.6 copy-done.6
  109.3 5.2 %all-gather.3.cloned.1.call-done = bf16[64,256,256]{2,1,0:T(8,128)(2,1)} async-done(((bf16[4,256,256]{2,1,0:T(8,128)(2,1)}), bf16[64,256,256]{2,1,0:T(8,128)(2,1)}) %all-gather.3.cloned.1.call-update) | async-done | bytes 8388624 | tf_op jit(solution)/shard_map/all_gather | solution.py:288
  114.5 5.9 %shard_map.138 = bf16[4,144,512]{2,1,0:T(8,128)(2,1)} custom-call(bf16[144,2048]{1,0:T(8,128)(2,1)} %copy-done.1, f32[8,128]{1,0:T(8,128)} %copy-done.6, bf16[16,4,256,256]{3,2,1,0:T(8,128)(2,1)} %bitcast.37), custom_call_target="tpu_custom_call" | custom-call | tf_op jit(solution)/shard_map/pallas_call | solution.py:198
  120.4 4.1 %all-to-all-start.3 = ((bf16[4,144,512]{2,1,0:T(8,128)(2,1)}), bf16[4,144,512]{2,1,0:T(8,128)(2,1)S(1)}, u32[]{:S(2)}, u32[]{:S(2)}) async-start(bf16[4,144,512]{2,1,0:T(8,128)(2,1)} %shard_map.138), calls=%async_computation.4 | async-start | bytes 1179648 | tf_op jit(solution)/shard_map/all_to_all | solution.py:343
  124.5 0.3 fusion
  124.9 0.1 copy.21.cosine_ref
  125.7 0.1 pad_maximum_fusion.1.sine_ref
  125.8 8.5 %all-to-all-done.3.pieces_ref = bf16[4,144,512]{2,1,0:T(8,128)(2,1)S(1)} async-done(((bf16[4,144,512]{2,1,0:T(8,128)(2,1)}), bf16[4,144,512]{2,1,0:T(8,128)(2,1)S(1)}, u32[]{:S(2)}, u32[]{:S(2)}) %all-to-all-start.3) | async-done | bytes 589856 | tf_op jit(solution)/shard_map/all_to_all | solution.py:343
  134.3 0.1 broadcast_in_dim.52.valid_ref
  134.3 1.1 shard_map.139
  (45 shorter events, 0.4 us)
Async XLA Ops:
  7.4 29.1 %copy-start = (bf16[384,2048]{1,0:T(8,128)(2,1)S(1)}, bf16[384,2048]{1,0:T(8,128)(2,1)}, u32[]{:S(2)}) copy-start(bf16[384,2048]{1,0:T(8,128)(2,1)} %param.19) | copy-start | bytes 4718596
  7.4 29.0 %all-to-all-start = ((bf16[4,256,256]{2,1,0:T(8,128)(2,1)}), bf16[4,256,256]{2,1,0:T(8,128)(2,1)S(1)}, u32[]{:S(2)}, u32[]{:S(2)}) async-start(bf16[4,256,256]{2,1,0:T(8,128)(2,1)} %bitcast.40), calls=%async_computation | async-start | bytes 1048576 | tf_op jit(solution)/shard_map/all_to_all | solution.py:275
  18.3 86.5 %reduce-scatter.2.cloned.1.call-start = ((), (), s32[]{:S(2)}) async-start(), calls=%async_computation.5 | async-start | bytes 4718592 | tf_op jit(solution)/shard_map/reduce_scatter | solution.py:297
  19.7 0.9 copy-start.3
  20.6 0.9 copy-start.4
  40.8 10.9 %copy-start.8 = (f32[16,8192]{1,0:T(8,128)S(1)}, f32[16,8192]{1,0:T(8,128)}, u32[]{:S(2)}) copy-start(f32[16,8192]{1,0:T(8,128)} %param.21) | copy-start | bytes 1572868
  40.8 12.4 %copy-start.11 = (f32[384]{0:T(512)S(1)}, f32[384]{0:T(512)}, u32[]{:S(2)}) copy-start(f32[384]{0:T(512)} %param.18) | copy-start | bytes 4612
  40.8 12.4 %copy-start.10 = (f32[384]{0:T(512)S(1)}, f32[384]{0:T(512)}, u32[]{:S(2)}) copy-start(f32[384]{0:T(512)} %param.17) | copy-start | bytes 4612
  40.8 73.7 %all-gather.3.cloned.1.call-start = ((), (), s32[]{:S(2)}) async-start(), calls=%async_computation.6 | async-start | bytes 8912896 | tf_op jit(solution)/shard_map/all_gather | solution.py:288
  51.9 18.0 %copy-start.12 = (s32[1,128]{1,0:T(1,128)S(1)}, s32[1,128]{1,0:T(1,128)}, u32[]{:S(2)}) copy-start(s32[1,128]{1,0:T(1,128)} %param.24) | copy-start | bytes 1540
  53.3 26.3 %copy-start.9 = (f32[2048]{0:T(1024)S(1)}, f32[2048]{0:T(1024)}, u32[]{:S(2)}) copy-start(f32[2048]{0:T(1024)} %param.20) | copy-start | bytes 24580
  53.3 51.6 %copy-start.5 = (f32[2048]{0:T(1024)S(1)}, f32[2048]{0:T(1024)}, u32[]{:S(2)}) copy-start(f32[2048]{0:T(1024)} %param.25) | copy-start | bytes 24580
  63.1 16.5 %all-to-all-start.1 = ((f32[8,1,4352]{2,1,0:T(1,128)}), f32[8,1,4352]{2,1,0:T(1,128)S(1)}, u32[]{:S(2)}, u32[]{:S(2)}) async-start(f32[8,1,4352]{2,1,0:T(1,128)} %all_to_all.18), calls=%async_computation.2 | async-start | bytes 278528 | tf_op jit(solution)/shard_map/all_to_all | solution.py:307
  104.8 1.1 copy-start.2
  107.9 0.9 copy-start.1
  108.7 0.6 copy-start.6
  120.4 13.9 %copy-start.7 = (f32[2,256]{1,0:T(2,128)S(1)}, f32[2,256]{1,0:T(2,128)}, u32[]{:S(2)}) copy-start(f32[2,256]{1,0:T(2,128)} %bias_ref.1) | copy-start | bytes 6148
  120.4 13.8 %all-to-all-start.3 = ((bf16[4,144,512]{2,1,0:T(8,128)(2,1)}), bf16[4,144,512]{2,1,0:T(8,128)(2,1)S(1)}, u32[]{:S(2)}, u32[]{:S(2)}) async-start(bf16[4,144,512]{2,1,0:T(8,128)(2,1)} %shard_map.138), calls=%async_computation.4 | async-start | bytes 1179648 | tf_op jit(solution)/shard_map/all_to_all | solution.py:343
Sparse Core Ops, SparseCore 0:
  40.9 63.9 reduce-scatter.1
Sparse Core Ops, SparseCore 1:
  51.1 63.4 all-gather.2

commit v5 on v3

--- a/solution.py
+++ b/solution.py
@@ -26,7 +26,7 @@
         part = slice(group * lanes, (group + 1) * lanes)
         cell = tile_ref[0, :, :, part].astype(jnp.float32)
         sums = [
-            jnp.broadcast_to(shift_ref[:, part], (width, lanes)) for _ in range(cells)
+            jnp.broadcast_to(shift_ref[part][None], (width, lanes)) for _ in range(cells)
         ]
         for col_off in range(side):
             move = col_off - reach
@@ -51,14 +51,14 @@
         part = slice(group * lanes, (group + 1) * lanes)
         centered = held[:, :, part] - average
         square = square + jnp.sum(centered * centered, -1, keepdims=True)
-        rows_ref[0, :, :, part] = (centered * gain_ref[0, part]).astype(rows_ref.dtype)
+        rows_ref[0, :, :, part] = (centered * gain_ref[part]).astype(rows_ref.dtype)
     stats_ref[0, 0] = jnp.broadcast_to(average, (cells, width, lanes))
     stats_ref[1, 0] = jnp.broadcast_to(square, (cells, width, lanes))
 
 
 def conv_rows(tiles, kernel, shift, gain):
     count, cells, width, channels = tiles.shape
-    whole = pl.BlockSpec((1, channels), lambda t: (0, 0))
+    whole = pl.BlockSpec((channels,), lambda t: (0,))
     return pl.pallas_call(
         conv_kernel,
         grid=(count,),
@@ -78,7 +78,7 @@
         ],
         scratch_shapes=[pltpu.VMEM((cells, width, channels), jnp.float32)],
         compiler_params=pltpu.CompilerParams(vmem_limit_bytes=60 * 2**20),
-    )(tiles, kernel, shift[None], gain[None])
+    )(tiles, kernel, shift, gain)
 
 
 def split_dot(rows, weight):
@@ -106,99 +106,105 @@
 
 
 def project_kernel(rows_ref, weight_ref, out_ref):
-    halves, _, columns = out_ref.shape
-    width = columns // INNER
-    for half in range(halves):
-        for block in range(INNER):
-            begin = (block * halves + half) * width
-            out_ref[half, :, block * width : (block + 1) * width] = jnp.dot(
-                rows_ref[...],
-                weight_ref[:, begin : begin + width],
-                preferred_element_type=jnp.float32,
-            ).astype(out_ref.dtype)
+    groups, _, count, _ = out_ref.shape
+    for group in range(groups):
+        out_ref[group, 0] = jnp.dot(
+            rows_ref[group * count : (group + 1) * count, :],
+            weight_ref[...],
+            preferred_element_type=jnp.float32,
+        ).astype(out_ref.dtype)
 
 
 def project(rows, weight, groups, halves):
     count, depth = rows.shape
     columns = weight.shape[1]
-    return pl.pallas_call(
+    width = columns // (INNER * halves)
+    out = pl.pallas_call(
         project_kernel,
-        grid=(groups,),
+        grid=(INNER * halves,),
         in_specs=[
-            pl.BlockSpec((count // groups, depth), lambda g: (g, 0)),
-            pl.BlockSpec(weight.shape, lambda g: (0, 0)),
-        ],
-        out_specs=pl.BlockSpec((halves, count // groups, columns // halves), lambda g: (g, 0, 0)),
+            pl.BlockSpec((count, depth), lambda g: (0, 0)),
+            pl.BlockSpec((depth, width), lambda g: (0, g)),
+        ],
+        out_specs=pl.BlockSpec(
+            (groups, 1, count // groups, width), lambda g: (0, g % halves, 0, g // halves)
+        ),
         out_shape=jax.ShapeDtypeStruct(
-            (groups * halves, count // groups, columns // halves), jnp.bfloat16
+            (groups, halves, count // groups, columns // halves), jnp.bfloat16
         ),
         compiler_params=pltpu.CompilerParams(vmem_limit_bytes=60 * 2**20),
     )(rows, weight)
-
-
-def kv_kernel(
-    summed_ref, means_ref, squares_ref, gains_ref, bias_ref, unit_ref, scale_ref, weight_ref,
-    out_ref, rows, stats,
+    return out.reshape(groups * halves, count // groups, columns // halves)
+
+
+def hidden_kernel(
+    summed_ref, means_ref, squares_ref, gains_ref, bias_ref, unit_ref, scale_ref, rows_ref, sums_ref,
+    stats,
 ):
     count, features = summed_ref.shape
-    _, _, depth, lanes = weight_ref.shape
     n_seq = means_ref.shape[0]
+    means = means_ref[...]
+    average = jnp.sum(means, 0, keepdims=True) / n_seq
+    offsets = means - average
+    block = C // n_seq
+    variance = (
+        jnp.sum(squares_ref[...], 0, keepdims=True)
+        + block * jnp.sum(offsets * offsets, 0, keepdims=True)
+    ) / C
+    inverse = lax.rsqrt(variance + epsilon)
+    columns = jnp.transpose(
+        jnp.concatenate([offsets, jnp.broadcast_to(inverse, (n_seq, count))], 0)
+    )
+    unit = unit_ref[...]
+    gain = scale_ref[...]
+    unit_square = jnp.sum(unit * unit)
+    for begin in range(0, count, STEP):
+        here = slice(begin, begin + STEP)
+        value = summed_ref[here, :].astype(jnp.float32)
+        for source in range(n_seq):
+            value = value + columns[here, source : source + 1] * gains_ref[source : source + 1, :]
+        value = value * columns[here, n_seq : n_seq + 1] + bias_ref[...]
+        hidden = 0.5 * value * (1.0 + lax.erf(value * 0.7071067811865476))
+        along = jnp.sum(hidden * unit, -1, keepdims=True)
+        across = hidden - (along / unit_square) * unit
+        square = jnp.sum(across * across, -1, keepdims=True)
+        lane = lax.broadcasted_iota(jnp.int32, (STEP, 128), 1)
+        stats[here, :] = jnp.where(lane == 0, along, jnp.where(lane == 1, square, unit_square))
+        rows_ref[here, :] = (across * gain).astype(jnp.bfloat16)
+    rows_ref[count:, :] = jnp.concatenate(
+        [*three_parts(unit * gain), jnp.zeros((EXTRA - 3, features), jnp.float32)], 0
+    ).astype(jnp.bfloat16)
+    sums_ref[...] = jnp.transpose(stats[...])[:8]
+
+
+def hidden_rows(summed, means, squares, gains, bias, unit, scale):
+    count, features = summed.shape
+    return pl.pallas_call(
+        hidden_kernel,
+        out_shape=[
+            jax.ShapeDtypeStruct((count + EXTRA, features), jnp.bfloat16),
+            jax.ShapeDtypeStruct((8, count), jnp.float32),
+        ],
+        scratch_shapes=[pltpu.VMEM((count, 128), jnp.float32)],
+        compiler_params=pltpu.CompilerParams(vmem_limit_bytes=60 * 2**20),
+    )(summed, means, squares, gains, bias, unit, scale)
+
+
+def kv_kernel(rows_ref, sums_ref, weight_ref, out_ref):
     halves = out_ref.shape[0]
+    features = rows_ref.shape[1]
+    count = rows_ref.shape[0] - EXTRA
     own = count // halves
-    width = out_ref.shape[3] // 2
-
-    @pl.when(pl.program_id(0) == 0)
-    def _():
-        means = means_ref[...]
-        average = jnp.sum(means, 0, keepdims=True) / n_seq
-        offsets = means - average
-        block = C // n_seq
-        variance = (
-            jnp.sum(squares_ref[...], 0, keepdims=True)
-            + block * jnp.sum(offsets * offsets, 0, keepdims=True)
-        ) / C
-        inverse = lax.rsqrt(variance + epsilon)
-        columns = jnp.transpose(
-            jnp.concatenate([offsets, jnp.broadcast_to(inverse, (n_seq, count))], 0)
-        )
-        unit = unit_ref[...]
-        gain = scale_ref[...]
-        unit_square = jnp.sum(unit * unit)
-        for begin in range(0, count, STEP):
-            here = slice(begin, begin + STEP)
-            value = summed_ref[here, :].astype(jnp.float32)
-            for source in range(n_seq):
-                value = value + columns[here, source : source + 1] * gains_ref[source : source + 1, :]
-            value = value * columns[here, n_seq : n_seq + 1] + bias_ref[...]
-            hidden = 0.5 * value * (1.0 + lax.erf(value * 0.7071067811865476))
-            along = jnp.sum(hidden * unit, -1, keepdims=True)
-            across = hidden - (along / unit_square) * unit
-            square = jnp.sum(across * across, -1, keepdims=True)
-            lane = lax.broadcasted_iota(jnp.int32, (STEP, 128), 1)
-            stats[here, :] = jnp.where(lane == 0, along, jnp.where(lane == 1, square, unit_square))
-            rows[here, :] = (across * gain).astype(jnp.bfloat16)
-        rows[count:, :] = jnp.concatenate(
-            [*three_parts(unit * gain), jnp.zeros((EXTRA - 3, features), jnp.float32)], 0
-        ).astype(jnp.bfloat16)
-
-    turned = jnp.transpose(stats[...])[:8]
+    width = weight_ref.shape[3]
     for pair in range(2):
         there = slice(pair * width, (pair + 1) * width)
-        weight = jnp.concatenate(
-            [
-                weight_ref[(pair * 2 + side) * INNER : (pair * 2 + side + 1) * INNER, 0].reshape(
-                    features, lanes
-                )
-                for side in range(width // lanes)
-            ],
-            1,
-        )
-        total = jnp.dot(rows[...], weight, preferred_element_type=jnp.float32)
+        weight = weight_ref[:, pair].reshape(features, width)
+        total = jnp.dot(rows_ref[...], weight, preferred_element_type=jnp.float32)
         vector = total[count : count + 1] + total[count + 1 : count + 2] + total[count + 2 : count + 3]
         for half in range(halves):
             mine = slice(half * own, (half + 1) * own)
             out_ref[half, 0, :own, there] = total[mine].astype(out_ref.dtype)
-            line = jnp.concatenate([turned[pair : pair + 1, mine], turned[2:3, mine]], 1)
+            line = jnp.concatenate([sums_ref[pair : pair + 1, mine], sums_ref[2:3, mine]], 1)
             extra = jnp.concatenate(
                 [
                     *three_parts(vector),
@@ -210,30 +216,22 @@
             out_ref[half, 0, own:, there] = extra.astype(out_ref.dtype)
 
 
-def kv_partial(summed, means, squares, gains, bias, unit, scale, weight, halves):
-    count, features = summed.shape
-    towers, groups, depth, lanes = weight.shape
-    both = 4 * lanes
-    rows_out = count // halves + EXTRA
-
-    def whole(array):
-        return pl.BlockSpec(array.shape, lambda g: (0,) * array.ndim)
-
+def kv_partial(rows, sums, weight, halves):
+    towers, pairs, depth, width = weight.shape
+    groups = towers // INNER
+    rows_out = (rows.shape[0] - EXTRA) // halves + EXTRA
     return pl.pallas_call(
         kv_kernel,
         grid=(groups,),
         in_specs=[
-            *(whole(a) for a in (summed, means, squares, gains, bias, unit, scale)),
-            pl.BlockSpec((towers, 1, depth, lanes), lambda g: (0, g, 0, 0)),
-        ],
-        out_specs=pl.BlockSpec((halves, 1, rows_out, both), lambda g: (0, g, 0, 0)),
-        out_shape=jax.ShapeDtypeStruct((halves, groups, rows_out, both), jnp.bfloat16),
-        scratch_shapes=[
-            pltpu.VMEM((count + EXTRA, features), jnp.bfloat16),
-            pltpu.VMEM((count, 128), jnp.float32),
-        ],
+            pl.BlockSpec(rows.shape, lambda g: (0, 0)),
+            pl.BlockSpec(sums.shape, lambda g: (0, 0)),
+            pl.BlockSpec((INNER, pairs, depth, width), lambda g: (g, 0, 0, 0)),
+        ],
+        out_specs=pl.BlockSpec((halves, 1, rows_out, pairs * width), lambda g: (0, g, 0, 0)),
+        out_shape=jax.ShapeDtypeStruct((halves, groups, rows_out, pairs * width), jnp.bfloat16),
         compiler_params=pltpu.CompilerParams(vmem_limit_bytes=60 * 2**20),
-    )(summed, means, squares, gains, bias, unit, scale, weight)
+    )(rows, sums, weight)
 
 
 def end_kernel(pieces_ref, bias_ref, cosine_ref, sine_ref, valid_ref, out_ref):
@@ -273,7 +271,7 @@
     return pl.pallas_call(
         end_kernel,
         out_shape=jax.ShapeDtypeStruct((1, 2, rows - EXTRA, both // 2), jnp.bfloat16),
-        compiler_params=pltpu.CompilerParams(vmem_limit_bytes=60 * 2**20),
+        compiler_params=pltpu.CompilerParams(vmem_limit_bytes=32 * 2**20),
     )(pieces, bias, cosine, sine, valid)
 
 
@@ -306,20 +304,15 @@
     partial, kv_weight = lax.optimization_barrier((partial, kv_weight))
     summed = lax.psum_scatter(partial, ("row", "half"), scatter_dimension=0, tiled=True)[0]
 
-    pairs, depth, width = kv_weight.shape
-    cut = lax.dynamic_slice_in_dim(kv_weight, half * (depth // n_half), depth // n_half, 1)
-    sides = n_mp // pairs
-    cut = cut.reshape(pairs, depth // n_half, sides, width // sides).swapaxes(1, 2)
-    cut = cut.reshape(n_mp, depth // n_half, width // sides)
-    cut = lax.all_to_all(
-        cut,
-        "tower",
-        0,
-        0,
-        tiled=True,
-        axis_index_groups=[[a * INNER + b for a in range(n_mp)] for b in range(INNER)],
-    )
-    cut = lax.all_to_all(cut, "mp", 0, 0, tiled=True)
+    depth = kv_weight.shape[1] // n_half
+    swap = [
+        ((a * INNER + b) * n_mp + x, (x * INNER + b) * n_mp + a)
+        for a in range(n_mp)
+        for b in range(INNER)
+        for x in range(n_mp)
+    ]
+    cut = lax.dynamic_slice_in_dim(kv_weight, half * depth, depth, 1)
+    cut = lax.ppermute(cut, ("tower", "mp"), swap)
     cut, stats, block_gain, block_bias = lax.optimization_barrier(
         (cut, stats, block_gain, block_bias)
     )
@@ -375,7 +368,7 @@
     row_valid = (row_ids // (SIDE * SIDE) < tile_counts[0]).astype(jnp.float32)[:, None]
     row_valid = jnp.broadcast_to(row_valid, cosine.shape)
 
-    pieces = kv_partial(
+    rows, sums = hidden_rows(
         summed,
         means,
         squares,
@@ -383,9 +376,8 @@
         bias_row[None],
         local_unit[None],
         own_half(rms_gain)[None],
-        kv_rows,
-        n_half,
-    )
+    )
+    pieces = kv_partial(rows, sums, kv_rows, n_half)
     pieces = pieces.reshape(n_half * n_mp, *pieces.shape[2:])
     pieces = lax.all_to_all(pieces, ("half", "mp"), 0, 0, tiled=True)
     return end_rows(pieces, kv_bias, cosine, sine, row_valid)

time: 150 us -> 144 us (0.960)
  local copies, waits for them, and re-layouts: 7.66 us -> 3.37 us
  waiting for transfers between devices: 38.1 us -> 35.2 us
  Pallas kernels: 20.7 us -> 23.3 us
  blocking collectives: 50.8 us -> 49.2 us
    all_to_all x2 -> x0, blocking collectives: 27.6 us -> none  [the longest x1 18.9 us: local(): lax.all_to_all(cut, 'tower', 0, 0, tiled=True, axis_index_groups=[[a * IN...]
    all_gather x1, blocking collectives: 9.11 us -> 35.2 us  [local(): stats = lax.all_gather(stats, 'mp', axis=1, tiled=True)]
    all_gather x1, waiting for transfers between devices: 9.8 us -> 4.51 us  [local(): kv_rows = lax.all_gather(cut, 'tower', axis=0, tiled=False)]
    pallas_call x2 -> x3, Pallas kernels: 14.2 us -> 18 us  [the longest x1 7.99 us: project(): pl.pallas_call(project_kernel, grid=(INNER * halves,), in_specs=[pl.Block...]
    broadcast_in_dim x2 -> x0, local copies, waits for them, and re-layouts: 2.49 us -> none  [the longest x1 1.24 us: conv_rows(): shift[None]]
  transfers between devices with their start and end apart: 4 -> 5, of which waited for: 4 -> 4; matrix products, arithmetic and copies ran while one was open for 4% -> 3% of each run, Pallas kernels for 0% -> 3%
where the time goes in v5:
time: 144 us
  blocking collectives  49.2 us (34%)
  waiting for transfers between devices  35.2 us (24%)
  Pallas kernels  23.3 us (16%)
  between operations  17.1 us (12%)
  starting transfers between devices  12.7 us (9%)
  local copies, waits for them, and re-layouts  3.37 us (2%)
  other arithmetic  2.48 us (2%)
    all_gather x1, blocking collectives, local(): stats = lax.all_gather(stats, 'mp', axis=1, tiled=True)  35.2 us
    all_to_all x1, waiting for transfers between devices, local(): pieces = lax.all_to_all(pieces, ('half', 'mp'), 0, 0, tiled=True)  15.1 us
    all_gather x1, blocking collectives, local(): lax.all_gather(block_rows.reshape(-1, channels), 'mp', axis=0, tiled=True)  14 us
    pallas_call x1, Pallas kernels, project(): pl.pallas_call(project_kernel, grid=(INNER * halves,), in_specs=[pl.Block...  7.99 us
    all_to_all x1, waiting for transfers between devices, local(): payload = lax.all_to_all(payload, ('row', 'half'), 0, 0, tiled=True)  7.8 us
    reduce_scatter x1, waiting for transfers between devices, local(): lax.psum_scatter(partial, ('row', 'half'), scatter_dimension=0, tiled=True)  7.74 us
    all_to_all x1, starting transfers between devices, local(): payload = lax.all_to_all(payload, ('row', 'half'), 0, 0, tiled=True)  6.8 us
    all_to_all x1, starting transfers between devices, local(): pieces = lax.all_to_all(pieces, ('half', 'mp'), 0, 0, tiled=True)  5.04 us
  transfers between devices with their start and end apart: 5, of which 4 were waited for; matrix products, arithmetic and copies ran while one was open for 3% of the time, Pallas kernels for 3%

profile of v5, /device:TPU:1, one launch (start us, length us, event | category | flops | bytes accessed | tf_op | source)
XLA Modules:
  0.0 143.7 jit_solution(15217434517281740551)
XLA Ops:
  7.4 4.1 %shard_map.136 = (bf16[4,8,8,384]{3,2,1,0:T(8,128)(2,1)}, f32[2,4,8,8,128]{4,3,2,1,0:T(8,128)}) custom-call(bf16[4,8,8,384]{3,2,1,0:T(8,128)(2,1)} %tile_ref.1, f32[7,7,384]{2,1,0:T(8,128)} %weight_ref.2, f32[384]{0:T(512)} %shift_ref.1, f32[384]{0:T(512)} %gain_ref.1), custom_call_target="tpu_custom_call" | custom-call | tf_op jit(solution)/shard_map/pallas_call | solution.py:62
  11.5 14.0 %all_gather.12.rows_ref = bf16[1024,384]{1,0:T(8,128)(2,1)} all-gather(bf16[256,384]{1,0:T(8,128)(2,1)} %bitcast.35), channel_id=1, replica_groups=mesh['tower'=16,'row'=4,'half'=2,'mp'=4] {'mp'}, dimensions={0}, use_global_device_ids=true | all-gather | bytes 983040 | tf_op jit(solution)/shard_map/all_gather | solution.py:302
  25.5 8.0 %shard_map.137 = bf16[4,2,256,1024]{3,2,1,0:T(8,128)(2,1)} custom-call(bf16[1024,384]{1,0:T(8,128)(2,1)} %all_gather.12.rows_ref, bf16[384,2048]{1,0:T(8,128)(2,1)} %weight_ref.3), custom_call_target="tpu_custom_call" | custom-call | tf_op jit(solution)/shard_map/pallas_call | solution.py:122
  33.5 0.0 reduce-scatter.2.cloned.1.call-update
  33.5 0.0 all-gather.3.cloned.1.call-start
  33.6 0.8 collective-permute-start
  34.5 0.7 copy-done.5
  35.9 0.2 select_reduce_fusion
  36.1 0.6 multiply_reduce_fusion
  37.5 0.3 fusion.1
  37.9 0.1 slice_reduce_fusion
  38.0 0.1 reshape_squeeze.3
  38.1 35.2 %all_gather.13 = f32[2,1024]{1,0:T(2,128)S(1)} all-gather(f32[2,256]{1,0:T(2,128)S(1)} %reshape_squeeze.3), channel_id=1, replica_groups=mesh['tower'=16,'row'=4,'half'=2,'mp'=4] {'mp'}, dimensions={1}, use_global_device_ids=true | all-gather | bytes 10240 | tf_op jit(solution)/shard_map/all_gather | solution.py:330
  73.4 0.8 all_to_all.11
  74.2 6.8 %all-to-all-start = ((f32[8,1,2560]{2,1,0:T(1,128)}), f32[8,1,2560]{2,1,0:T(1,128)S(1)}, u32[]{:S(2)}, u32[]{:S(2)}) async-start(f32[8,1,2560]{2,1,0:T(1,128)} %all_to_all.11), calls=%async_computation.1 | async-start | bytes 163840 | tf_op jit(solution)/shard_map/all_to_all | solution.py:341
  81.0 0.6 constant_dynamic-slice_fusion
  81.6 7.8 %all-to-all-done = f32[8,1,2560]{2,1,0:T(1,128)S(1)} async-done(((f32[8,1,2560]{2,1,0:T(1,128)}), f32[8,1,2560]{2,1,0:T(1,128)S(1)}, u32[]{:S(2)}, u32[]{:S(2)}) %all-to-all-start) | async-done | bytes 81952 | tf_op jit(solution)/shard_map/all_to_all | solution.py:341
  89.5 0.6 slice_reduce_fusion.1
  90.1 0.6 add.52.bias_ref
  90.7 0.6 fusion.10
  91.3 7.7 %reduce-scatter.2.cloned.1.call-done = bf16[1,256,1024]{2,1,0:T(8,128)(2,1)} async-done(((bf16[8,256,1024]{2,1,0:T(8,128)(2,1)}), bf16[1,256,1024]{2,1,0:T(8,128)(2,1)}) %reduce-scatter.2.cloned.1.call-update) | async-done | bytes 524304 | tf_op jit(solution)/shard_map/reduce_scatter | solution.py:305
  99.0 5.0 %shard_map.138 = (bf16[272,1024]{1,0:T(8,128)(2,1)}, f32[8,256]{1,0:T(8,128)}) custom-call(bf16[256,1024]{1,0:T(8,128)(2,1)} %bitcast.31, f32[8,256]{1,0:T(8,128)} %get-tuple-element.28.means_ref, f32[8,256]{1,0:T(8,128)} %get-tuple-element.27.squares_ref, f32[8,1024]{1,0:T(8,128)} %get-tuple-element.26.gains_ref, f32[1,1024]{1,0:T(1,128)} %add.52.bias_ref, ...), custom_call_target="tpu_custom_call" | custom-call | tf_op jit(solution)/shard_map/pallas_call | solution.py:182
  104.0 4.5 %all-gather.3.cloned.1.call-done = bf16[32,256,256]{2,1,0:T(8,128)(2,1)} async-done(((bf16[2,256,256]{2,1,0:T(8,128)(2,1)}), bf16[32,256,256]{2,1,0:T(8,128)(2,1)}) %all-gather.3.cloned.1.call-update) | async-done | bytes 4194320 | tf_op jit(solution)/shard_map/all_gather | solution.py:319
  108.5 5.0 %shard_map.139 = bf16[2,4,144,512]{3,2,1,0:T(8,128)(2,1)} custom-call(bf16[272,1024]{1,0:T(8,128)(2,1)} %get-tuple-element.22.rows_ref, f32[8,256]{1,0:T(8,128)} %get-tuple-element.23.sums_ref, bf16[16,2,256,256]{3,2,1,0:T(8,128)(2,1)} %bitcast.30), custom_call_target="tpu_custom_call" | custom-call | tf_op jit(solution)/shard_map/pallas_call | solution.py:223
  113.6 5.0 %all-to-all-start.1 = ((bf16[8,144,512]{2,1,0:T(8,128)(2,1)}), bf16[8,144,512]{2,1,0:T(8,128)(2,1)S(1)}, u32[]{:S(2)}, u32[]{:S(2)}) async-start(bf16[8,144,512]{2,1,0:T(8,128)(2,1)} %bitcast.29), calls=%async_computation.2 | async-start | bytes 2359296 | tf_op jit(solution)/shard_map/all_to_all | solution.py:382
  119.3 0.3 fusion
  119.6 0.1 copy.20
  119.7 0.1 copy.21.cosine_ref
  119.8 0.1 pad_maximum_fusion.1.sine_ref
  119.9 15.1 %all-to-all-done.1.pieces_ref = bf16[8,144,512]{2,1,0:T(8,128)(2,1)S(1)} async-done(((bf16[8,144,512]{2,1,0:T(8,128)(2,1)}), bf16[8,144,512]{2,1,0:T(8,128)(2,1)S(1)}, u32[]{:S(2)}, u32[]{:S(2)}) %all-to-all-start.1) | async-done | bytes 1179680 | tf_op jit(solution)/shard_map/all_to_all | solution.py:382
  135.0 0.1 broadcast_in_dim.42.valid_ref
  135.1 1.2 shard_map.140
  (45 shorter events, 0.4 us)
Async XLA Ops:
  7.4 26.2 %copy-start = (bf16[2,512,256]{2,1,0:T(8,128)(2,1)S(1)}, bf16[2,512,256]{2,1,0:T(8,128)(2,1)}, u32[]{:S(2)}) copy-start(bf16[2,512,256]{2,1,0:T(8,128)(2,1)} %param.26) | copy-start | bytes 1572868
  7.4 91.6 %reduce-scatter.2.cloned.1.call-start = ((), (), s32[]{:S(2)}) async-start(), calls=%async_computation.3 | async-start | bytes 4718592 | tf_op jit(solution)/shard_map/reduce_scatter | solution.py:305
  33.5 1.8 %copy-start.7 = (f32[2048]{0:T(1024)S(1)}, f32[2048]{0:T(1024)}, u32[]{:S(2)}) copy-start(f32[2048]{0:T(1024)} %param.20) | copy-start | bytes 24580
  33.5 2.4 %copy-start.3 = (f32[16,8192]{1,0:T(8,128)S(1)}, f32[16,8192]{1,0:T(8,128)}, u32[]{:S(2)}) copy-start(f32[16,8192]{1,0:T(8,128)} %param.21) | copy-start | bytes 1572868
  33.5 4.0 %copy-start.9 = (f32[384]{0:T(512)S(1)}, f32[384]{0:T(512)}, u32[]{:S(2)}) copy-start(f32[384]{0:T(512)} %param.18) | copy-start | bytes 4612
  33.5 4.0 %copy-start.6 = (f32[384]{0:T(512)S(1)}, f32[384]{0:T(512)}, u32[]{:S(2)}) copy-start(f32[384]{0:T(512)} %gain_ref.1) | copy-start | bytes 4612
  33.5 4.0 %copy-start.2 = (bf16[384,2048]{1,0:T(8,128)(2,1)S(1)}, bf16[384,2048]{1,0:T(8,128)(2,1)}, u32[]{:S(2)}) copy-start(bf16[384,2048]{1,0:T(8,128)(2,1)} %weight_ref.3) | copy-start | bytes 4718596
  33.5 75.0 %all-gather.3.cloned.1.call-start = ((), (), s32[]{:S(2)}) async-start(), calls=%async_computation.4 | async-start | bytes 4456448 | tf_op jit(solution)/shard_map/all_gather | solution.py:319
  33.6 4.3 %copy-start.4 = (f32[2,4,8,8,128]{4,3,2,1,0:T(8,128)S(1)}, f32[2,4,8,8,128]{4,3,2,1,0:T(8,128)}, u32[]{:S(2)}) copy-start(f32[2,4,8,8,128]{4,3,2,1,0:T(8,128)} %get-tuple-element.19) | copy-start | bytes 786436
  33.6 0.8 collective-permute-start
  34.5 0.7 copy-start.5
  35.9 45.1 %copy-start.8 = (f32[2048]{0:T(1024)S(1)}, f32[2048]{0:T(1024)}, u32[]{:S(2)}) copy-start(f32[2048]{0:T(1024)} %param.25) | copy-start | bytes 24580
  74.2 15.3 %all-to-all-start = ((f32[8,1,2560]{2,1,0:T(1,128)}), f32[8,1,2560]{2,1,0:T(1,128)S(1)}, u32[]{:S(2)}, u32[]{:S(2)}) async-start(f32[8,1,2560]{2,1,0:T(1,128)} %all_to_all.11), calls=%async_computation.1 | async-start | bytes 163840 | tf_op jit(solution)/shard_map/all_to_all | solution.py:341
  113.6 5.7 %copy-start.10 = (s32[1,128]{1,0:T(1,128)S(1)}, s32[1,128]{1,0:T(1,128)}, u32[]{:S(2)}) copy-start(s32[1,128]{1,0:T(1,128)} %param.24) | copy-start | bytes 1540
  113.6 21.5 %copy-start.1 = (f32[2,256]{1,0:T(2,128)S(1)}, f32[2,256]{1,0:T(2,128)}, u32[]{:S(2)}) copy-start(f32[2,256]{1,0:T(2,128)} %bias_ref.1) | copy-start | bytes 6148
  113.6 21.4 %all-to-all-start.1 = ((bf16[8,144,512]{2,1,0:T(8,128)(2,1)}), bf16[8,144,512]{2,1,0:T(8,128)(2,1)S(1)}, u32[]{:S(2)}, u32[]{:S(2)}) async-start(bf16[8,144,512]{2,1,0:T(8,128)(2,1)} %bitcast.29), calls=%async_computation.2 | async-start | bytes 2359296 | tf_op jit(solution)/shard_map/all_to_all | solution.py:382
Sparse Core Ops, SparseCore 0:
  33.6 65.3 reduce-scatter.1
Sparse Core Ops, SparseCore 1:
  36.1 72.3 all-gather.2

commit v6 on v5

--- a/solution.py
+++ b/solution.py
@@ -106,35 +106,34 @@
 
 
 def project_kernel(rows_ref, weight_ref, out_ref):
-    groups, _, count, _ = out_ref.shape
-    for group in range(groups):
-        out_ref[group, 0] = jnp.dot(
-            rows_ref[group * count : (group + 1) * count, :],
-            weight_ref[...],
-            preferred_element_type=jnp.float32,
-        ).astype(out_ref.dtype)
+    halves, _, columns = out_ref.shape
+    width = columns // INNER
+    for half in range(halves):
+        for block in range(INNER):
+            begin = (block * halves + half) * width
+            out_ref[half, :, block * width : (block + 1) * width] = jnp.dot(
+                rows_ref[...],
+                weight_ref[:, begin : begin + width],
+                preferred_element_type=jnp.float32,
+            ).astype(out_ref.dtype)
 
 
 def project(rows, weight, groups, halves):
     count, depth = rows.shape
     columns = weight.shape[1]
-    width = columns // (INNER * halves)
-    out = pl.pallas_call(
+    return pl.pallas_call(
         project_kernel,
-        grid=(INNER * halves,),
+        grid=(groups,),
         in_specs=[
-            pl.BlockSpec((count, depth), lambda g: (0, 0)),
-            pl.BlockSpec((depth, width), lambda g: (0, g)),
-        ],
-        out_specs=pl.BlockSpec(
-            (groups, 1, count // groups, width), lambda g: (0, g % halves, 0, g // halves)
-        ),
+            pl.BlockSpec((count // groups, depth), lambda g: (g, 0)),
+            pl.BlockSpec(weight.shape, lambda g: (0, 0)),
+        ],
+        out_specs=pl.BlockSpec((halves, count // groups, columns // halves), lambda g: (g, 0, 0)),
         out_shape=jax.ShapeDtypeStruct(
-            (groups, halves, count // groups, columns // halves), jnp.bfloat16
+            (groups * halves, count // groups, columns // halves), jnp.bfloat16
         ),
         compiler_params=pltpu.CompilerParams(vmem_limit_bytes=60 * 2**20),
     )(rows, weight)
-    return out.reshape(groups * halves, count // groups, columns // halves)
 
 
 def hidden_kernel(

time: 144 us -> 142 us (0.986)
  Pallas kernels: 23.3 us -> 21.4 us
    pallas_call x1, Pallas kernels: 7.99 us -> 6.02 us  [project(): pl.pallas_call(project_kernel, grid=(groups,), in_specs=[pl.BlockSpec((co...]
  transfers between devices with their start and end apart: 5 -> 5, of which waited for: 4 -> 4; matrix products, arithmetic and copies ran while one was open for 3% -> 3% of each run, Pallas kernels for 3% -> 4%
where the time goes in v6:
time: 142 us
  blocking collectives  49.2 us (35%)
  waiting for transfers between devices  35.1 us (25%)
  Pallas kernels  21.4 us (15%)
  between operations  17.1 us (12%)
  starting transfers between devices  12.7 us (9%)
  local copies, waits for them, and re-layouts  3.37 us (2%)
  other arithmetic  2.48 us (2%)
    all_gather x1, blocking collectives, local(): stats = lax.all_gather(stats, 'mp', axis=1, tiled=True)  35.2 us
    all_to_all x1, waiting for transfers between devices, local(): pieces = lax.all_to_all(pieces, ('half', 'mp'), 0, 0, tiled=True)  15.1 us
    all_gather x1, blocking collectives, local(): lax.all_gather(block_rows.reshape(-1, channels), 'mp', axis=0, tiled=True)  14 us
    all_to_all x1, waiting for transfers between devices, local(): payload = lax.all_to_all(payload, ('row', 'half'), 0, 0, tiled=True)  7.79 us
    reduce_scatter x1, waiting for transfers between devices, local(): lax.psum_scatter(partial, ('row', 'half'), scatter_dimension=0, tiled=True)  7.77 us
    all_to_all x1, starting transfers between devices, local(): payload = lax.all_to_all(payload, ('row', 'half'), 0, 0, tiled=True)  6.81 us
    pallas_call x1, Pallas kernels, project(): pl.pallas_call(project_kernel, grid=(groups,), in_specs=[pl.BlockSpec((co...  6.02 us
    all_to_all x1, starting transfers between devices, local(): pieces = lax.all_to_all(pieces, ('half', 'mp'), 0, 0, tiled=True)  5.05 us
  transfers between devices with their start and end apart: 5, of which 4 were waited for; matrix products, arithmetic and copies ran while one was open for 3% of the time, Pallas kernels for 4%

profile of v6, /device:TPU:1, one launch (start us, length us, event | category | flops | bytes accessed | tf_op | source)
XLA Modules:
  0.0 141.8 jit_solution(11025662754529795478)
XLA Ops:
  7.4 4.1 %shard_map.136 = (bf16[4,8,8,384]{3,2,1,0:T(8,128)(2,1)}, f32[2,4,8,8,128]{4,3,2,1,0:T(8,128)}) custom-call(bf16[4,8,8,384]{3,2,1,0:T(8,128)(2,1)} %tile_ref.1, f32[7,7,384]{2,1,0:T(8,128)} %weight_ref.2, f32[384]{0:T(512)} %shift_ref.1, f32[384]{0:T(512)} %gain_ref.1), custom_call_target="tpu_custom_call" | custom-call | tf_op jit(solution)/shard_map/pallas_call | solution.py:62
  11.5 14.0 %all_gather.12.rows_ref = bf16[1024,384]{1,0:T(8,128)(2,1)} all-gather(bf16[256,384]{1,0:T(8,128)(2,1)} %bitcast.33), channel_id=1, replica_groups=mesh['tower'=16,'row'=4,'half'=2,'mp'=4] {'mp'}, dimensions={0}, use_global_device_ids=true | all-gather | bytes 983040 | tf_op jit(solution)/shard_map/all_gather | solution.py:301
  25.5 6.0 %shard_map.137 = bf16[8,256,1024]{2,1,0:T(8,128)(2,1)} custom-call(bf16[1024,384]{1,0:T(8,128)(2,1)} %all_gather.12.rows_ref, bf16[384,2048]{1,0:T(8,128)(2,1)} %weight_ref.3), custom_call_target="tpu_custom_call" | custom-call | tf_op jit(solution)/shard_map/pallas_call | solution.py:124
  31.5 0.0 reduce-scatter.2.cloned.1.call-update
  31.5 0.0 all-gather.3.cloned.1.call-start
  31.7 0.8 collective-permute-start
  32.5 0.7 copy-done.5
  34.0 0.2 select_reduce_fusion
  34.1 0.6 multiply_reduce_fusion
  35.5 0.3 fusion.1
  35.9 0.1 slice_reduce_fusion
  36.0 0.1 reshape_squeeze.3
  36.1 35.2 %all_gather.13 = f32[2,1024]{1,0:T(2,128)S(1)} all-gather(f32[2,256]{1,0:T(2,128)S(1)} %reshape_squeeze.3), channel_id=1, replica_groups=mesh['tower'=16,'row'=4,'half'=2,'mp'=4] {'mp'}, dimensions={1}, use_global_device_ids=true | all-gather | bytes 10240 | tf_op jit(solution)/shard_map/all_gather | solution.py:329
  71.4 0.8 all_to_all.11
  72.2 6.8 %all-to-all-start = ((f32[8,1,2560]{2,1,0:T(1,128)}), f32[8,1,2560]{2,1,0:T(1,128)S(1)}, u32[]{:S(2)}, u32[]{:S(2)}) async-start(f32[8,1,2560]{2,1,0:T(1,128)} %all_to_all.11), calls=%async_computation.1 | async-start | bytes 163840 | tf_op jit(solution)/shard_map/all_to_all | solution.py:340
  79.1 0.6 constant_dynamic-slice_fusion
  79.7 7.8 %all-to-all-done = f32[8,1,2560]{2,1,0:T(1,128)S(1)} async-done(((f32[8,1,2560]{2,1,0:T(1,128)}), f32[8,1,2560]{2,1,0:T(1,128)S(1)}, u32[]{:S(2)}, u32[]{:S(2)}) %all-to-all-start) | async-done | bytes 81952 | tf_op jit(solution)/shard_map/all_to_all | solution.py:340
  87.5 0.6 slice_reduce_fusion.1
  88.1 0.6 add.52.bias_ref
  88.7 0.6 fusion.10
  89.3 7.8 %reduce-scatter.2.cloned.1.call-done = bf16[1,256,1024]{2,1,0:T(8,128)(2,1)} async-done(((bf16[8,256,1024]{2,1,0:T(8,128)(2,1)}), bf16[1,256,1024]{2,1,0:T(8,128)(2,1)}) %reduce-scatter.2.cloned.1.call-update) | async-done | bytes 524304 | tf_op jit(solution)/shard_map/reduce_scatter | solution.py:304
  97.1 5.0 %shard_map.138 = (bf16[272,1024]{1,0:T(8,128)(2,1)}, f32[8,256]{1,0:T(8,128)}) custom-call(bf16[256,1024]{1,0:T(8,128)(2,1)} %bitcast.29, f32[8,256]{1,0:T(8,128)} %get-tuple-element.28.means_ref, f32[8,256]{1,0:T(8,128)} %get-tuple-element.27.squares_ref, f32[8,1024]{1,0:T(8,128)} %get-tuple-element.26.gains_ref, f32[1,1024]{1,0:T(1,128)} %add.52.bias_ref, ...), custom_call_target="tpu_custom_call" | custom-call | tf_op jit(solution)/shard_map/pallas_call | solution.py:181
  102.1 4.5 %all-gather.3.cloned.1.call-done = bf16[32,256,256]{2,1,0:T(8,128)(2,1)} async-done(((bf16[2,256,256]{2,1,0:T(8,128)(2,1)}), bf16[32,256,256]{2,1,0:T(8,128)(2,1)}) %all-gather.3.cloned.1.call-update) | async-done | bytes 4194320 | tf_op jit(solution)/shard_map/all_gather | solution.py:318
  106.5 5.0 %shard_map.139 = bf16[2,4,144,512]{3,2,1,0:T(8,128)(2,1)} custom-call(bf16[272,1024]{1,0:T(8,128)(2,1)} %get-tuple-element.22.rows_ref, f32[8,256]{1,0:T(8,128)} %get-tuple-element.23.sums_ref, bf16[16,2,256,256]{3,2,1,0:T(8,128)(2,1)} %bitcast.28), custom_call_target="tpu_custom_call" | custom-call | tf_op jit(solution)/shard_map/pallas_call | solution.py:222
  111.6 5.1 %all-to-all-start.1 = ((bf16[8,144,512]{2,1,0:T(8,128)(2,1)}), bf16[8,144,512]{2,1,0:T(8,128)(2,1)S(1)}, u32[]{:S(2)}, u32[]{:S(2)}) async-start(bf16[8,144,512]{2,1,0:T(8,128)(2,1)} %bitcast.27), calls=%async_computation.2 | async-start | bytes 2359296 | tf_op jit(solution)/shard_map/all_to_all | solution.py:381
  117.3 0.3 fusion
  117.6 0.1 copy.20
  117.7 0.1 copy.21.cosine_ref
  117.9 0.1 pad_maximum_fusion.1.sine_ref
  117.9 15.1 %all-to-all-done.1.pieces_ref = bf16[8,144,512]{2,1,0:T(8,128)(2,1)S(1)} async-done(((bf16[8,144,512]{2,1,0:T(8,128)(2,1)}), bf16[8,144,512]{2,1,0:T(8,128)(2,1)S(1)}, u32[]{:S(2)}, u32[]{:S(2)}) %all-to-all-start.1) | async-done | bytes 1179680 | tf_op jit(solution)/shard_map/all_to_all | solution.py:381
  133.0 0.1 broadcast_in_dim.42.valid_ref
  133.1 1.2 shard_map.140
  (45 shorter events, 0.4 us)
Async XLA Ops:
  7.4 24.2 %copy-start = (bf16[2,512,256]{2,1,0:T(8,128)(2,1)S(1)}, bf16[2,512,256]{2,1,0:T(8,128)(2,1)}, u32[]{:S(2)}) copy-start(bf16[2,512,256]{2,1,0:T(8,128)(2,1)} %param.26) | copy-start | bytes 1572868
  7.4 89.7 %reduce-scatter.2.cloned.1.call-start = ((), (), s32[]{:S(2)}) async-start(), calls=%async_computation.3 | async-start | bytes 4718592 | tf_op jit(solution)/shard_map/reduce_scatter | solution.py:304
  31.5 1.8 %copy-start.7 = (f32[2048]{0:T(1024)S(1)}, f32[2048]{0:T(1024)}, u32[]{:S(2)}) copy-start(f32[2048]{0:T(1024)} %param.20) | copy-start | bytes 24580
  31.5 2.4 %copy-start.3 = (f32[16,8192]{1,0:T(8,128)S(1)}, f32[16,8192]{1,0:T(8,128)}, u32[]{:S(2)}) copy-start(f32[16,8192]{1,0:T(8,128)} %param.21) | copy-start | bytes 1572868
  31.5 4.0 %copy-start.9 = (f32[384]{0:T(512)S(1)}, f32[384]{0:T(512)}, u32[]{:S(2)}) copy-start(f32[384]{0:T(512)} %param.18) | copy-start | bytes 4612
  31.5 4.0 %copy-start.6 = (f32[384]{0:T(512)S(1)}, f32[384]{0:T(512)}, u32[]{:S(2)}) copy-start(f32[384]{0:T(512)} %gain_ref.1) | copy-start | bytes 4612
  31.5 4.0 %copy-start.2 = (bf16[384,2048]{1,0:T(8,128)(2,1)S(1)}, bf16[384,2048]{1,0:T(8,128)(2,1)}, u32[]{:S(2)}) copy-start(bf16[384,2048]{1,0:T(8,128)(2,1)} %weight_ref.3) | copy-start | bytes 4718596
  31.5 75.0 %all-gather.3.cloned.1.call-start = ((), (), s32[]{:S(2)}) async-start(), calls=%async_computation.4 | async-start | bytes 4456448 | tf_op jit(solution)/shard_map/all_gather | solution.py:318
  31.6 4.3 %copy-start.4 = (f32[2,4,8,8,128]{4,3,2,1,0:T(8,128)S(1)}, f32[2,4,8,8,128]{4,3,2,1,0:T(8,128)}, u32[]{:S(2)}) copy-start(f32[2,4,8,8,128]{4,3,2,1,0:T(8,128)} %get-tuple-element.19) | copy-start | bytes 786436
  31.7 0.8 collective-permute-start
  32.5 0.7 copy-start.5
  33.9 45.1 %copy-start.8 = (f32[2048]{0:T(1024)S(1)}, f32[2048]{0:T(1024)}, u32[]{:S(2)}) copy-start(f32[2048]{0:T(1024)} %param.25) | copy-start | bytes 24580
  72.2 15.3 %all-to-all-start = ((f32[8,1,2560]{2,1,0:T(1,128)}), f32[8,1,2560]{2,1,0:T(1,128)S(1)}, u32[]{:S(2)}, u32[]{:S(2)}) async-start(f32[8,1,2560]{2,1,0:T(1,128)} %all_to_all.11), calls=%async_computation.1 | async-start | bytes 163840 | tf_op jit(solution)/shard_map/all_to_all | solution.py:340
  111.6 5.7 %copy-start.10 = (s32[1,128]{1,0:T(1,128)S(1)}, s32[1,128]{1,0:T(1,128)}, u32[]{:S(2)}) copy-start(s32[1,128]{1,0:T(1,128)} %param.24) | copy-start | bytes 1540
  111.6 21.5 %copy-start.1 = (f32[2,256]{1,0:T(2,128)S(1)}, f32[2,256]{1,0:T(2,128)}, u32[]{:S(2)}) copy-start(f32[2,256]{1,0:T(2,128)} %bias_ref.1) | copy-start | bytes 6148
  111.6 21.4 %all-to-all-start.1 = ((bf16[8,144,512]{2,1,0:T(8,128)(2,1)}), bf16[8,144,512]{2,1,0:T(8,128)(2,1)S(1)}, u32[]{:S(2)}, u32[]{:S(2)}) async-start(bf16[8,144,512]{2,1,0:T(8,128)(2,1)} %bitcast.27), calls=%async_computation.2 | async-start | bytes 2359296 | tf_op jit(solution)/shard_map/all_to_all | solution.py:381
Sparse Core Ops, SparseCore 0:
  31.7 65.3 reduce-scatter.1
Sparse Core Ops, SparseCore 1:
  34.1 72.3 all-gather.2

commit v7 on v6

--- a/solution.py
+++ b/solution.py
@@ -1,3 +1,5 @@
+import functools
+
 import jax
 import jax.numpy as jnp
 from jax import lax
@@ -189,48 +191,55 @@
     )(summed, means, squares, gains, bias, unit, scale)
 
 
-def kv_kernel(rows_ref, sums_ref, weight_ref, out_ref):
+def kv_kernel(pair, rows_ref, sums_ref, weight_ref, *refs):
+    out_ref = refs[-1]
     halves = out_ref.shape[0]
     features = rows_ref.shape[1]
     count = rows_ref.shape[0] - EXTRA
     own = count // halves
-    width = weight_ref.shape[3]
-    for pair in range(2):
-        there = slice(pair * width, (pair + 1) * width)
-        weight = weight_ref[:, pair].reshape(features, width)
-        total = jnp.dot(rows_ref[...], weight, preferred_element_type=jnp.float32)
-        vector = total[count : count + 1] + total[count + 1 : count + 2] + total[count + 2 : count + 3]
-        for half in range(halves):
-            mine = slice(half * own, (half + 1) * own)
-            out_ref[half, 0, :own, there] = total[mine].astype(out_ref.dtype)
-            line = jnp.concatenate([sums_ref[pair : pair + 1, mine], sums_ref[2:3, mine]], 1)
-            extra = jnp.concatenate(
-                [
-                    *three_parts(vector),
-                    *three_parts(line),
-                    jnp.zeros((EXTRA - 6, width), jnp.float32),
-                ],
-                0,
-            )
-            out_ref[half, 0, own:, there] = extra.astype(out_ref.dtype)
-
-
-def kv_partial(rows, sums, weight, halves):
-    towers, pairs, depth, width = weight.shape
+    width = weight_ref.shape[2]
+    weight = weight_ref[...].reshape(features, width)
+    total = jnp.dot(rows_ref[...], weight, preferred_element_type=jnp.float32)
+    vector = total[count : count + 1] + total[count + 1 : count + 2] + total[count + 2 : count + 3]
+    for half in range(halves):
+        mine = slice(half * own, (half + 1) * own)
+        out_ref[half, 0, :own, :] = total[mine].astype(out_ref.dtype)
+        line = jnp.concatenate([sums_ref[pair : pair + 1, mine], sums_ref[2:3, mine]], 1)
+        extra = jnp.concatenate(
+            [
+                *three_parts(vector),
+                *three_parts(line),
+                jnp.zeros((EXTRA - 6, width), jnp.float32),
+            ],
+            0,
+        )
+        out_ref[half, 0, own:, :] = extra.astype(out_ref.dtype)
+
+
+def kv_partial(rows, sums, weight, halves, pair, held=None):
+    towers, depth, width = weight.shape
     groups = towers // INNER
     rows_out = (rows.shape[0] - EXTRA) // halves + EXTRA
+    in_specs = [
+        pl.BlockSpec(rows.shape, lambda g: (0, 0)),
+        pl.BlockSpec(sums.shape, lambda g: (0, 0)),
+        pl.BlockSpec((INNER, depth, width), lambda g: (g, 0, 0)),
+    ]
+    operands = [rows, sums, weight]
+    aliases = {}
+    if held is not None:
+        in_specs.append(pl.BlockSpec(memory_space=pl.ANY))
+        operands.append(held)
+        aliases = {3: 0}
     return pl.pallas_call(
-        kv_kernel,
+        functools.partial(kv_kernel, pair),
         grid=(groups,),
-        in_specs=[
-            pl.BlockSpec(rows.shape, lambda g: (0, 0)),
-            pl.BlockSpec(sums.shape, lambda g: (0, 0)),
-            pl.BlockSpec((INNER, pairs, depth, width), lambda g: (g, 0, 0, 0)),
-        ],
-        out_specs=pl.BlockSpec((halves, 1, rows_out, pairs * width), lambda g: (0, g, 0, 0)),
-        out_shape=jax.ShapeDtypeStruct((halves, groups, rows_out, pairs * width), jnp.bfloat16),
+        in_specs=in_specs,
+        out_specs=pl.BlockSpec((halves, 1, rows_out, width), lambda g: (0, g, 0, pair)),
+        out_shape=jax.ShapeDtypeStruct((halves, groups, rows_out, 2 * width), jnp.bfloat16),
+        input_output_aliases=aliases,
         compiler_params=pltpu.CompilerParams(vmem_limit_bytes=60 * 2**20),
-    )(rows, sums, weight)
+    )(*operands)
 
 
 def end_kernel(pieces_ref, bias_ref, cosine_ref, sine_ref, valid_ref, out_ref):
@@ -311,11 +320,15 @@
         for x in range(n_mp)
     ]
     cut = lax.dynamic_slice_in_dim(kv_weight, half * depth, depth, 1)
-    cut = lax.ppermute(cut, ("tower", "mp"), swap)
-    cut, stats, block_gain, block_bias = lax.optimization_barrier(
-        (cut, stats, block_gain, block_bias)
-    )
-    kv_rows = lax.all_gather(cut, "tower", axis=0, tiled=False)
+    key_cut, value_cut = lax.optimization_barrier((cut[0], cut[1]))
+    key_cut = lax.ppermute(key_cut, ("tower", "mp"), swap)
+    key_cut, value_cut = lax.optimization_barrier((key_cut, value_cut))
+    key_weight = lax.all_gather(key_cut, "tower", axis=0, tiled=False)
+    value_cut = lax.ppermute(value_cut, ("tower", "mp"), swap)
+    value_cut, stats, block_gain, block_bias = lax.optimization_barrier(
+        (value_cut, stats, block_gain, block_bias)
+    )
+    value_weight = lax.all_gather(value_cut, "tower", axis=0, tiled=False)
 
     vectors = split_dot(jnp.stack([block_gain, block_bias]), proj_weight)
     column_count = vectors.shape[1]
@@ -376,7 +389,8 @@
         local_unit[None],
         own_half(rms_gain)[None],
     )
-    pieces = kv_partial(rows, sums, kv_rows, n_half)
+    pieces = kv_partial(rows, sums, key_weight, n_half, 0)
+    pieces = kv_partial(rows, sums, value_weight, n_half, 1, pieces)
     pieces = pieces.reshape(n_half * n_mp, *pieces.shape[2:])
     pieces = lax.all_to_all(pieces, ("half", "mp"), 0, 0, tiled=True)
     return end_rows(pieces, kv_bias, cosine, sine, row_valid)

time: 142 us -> 176 us (1.24)
  waiting for transfers between devices: 35.1 us -> 62.6 us
  Pallas kernels: 21.4 us -> 24.8 us
    all_gather x1 -> x2, waiting for transfers between devices: 4.49 us -> 34.3 us  [the longest x1 34.3 us: local(): value_weight = lax.all_gather(value_cut, 'tower', axis=0, tiled=False)]
    pallas_call x1 -> x2, Pallas kernels: 5.04 us -> 8.6 us  [kv_partial(): pl.pallas_call(functools.partial(kv_kernel, pair), grid=(groups,), in_spe...]
    reduce_scatter x1, waiting for transfers between devices: 7.77 us -> 5.34 us  [local(): lax.psum_scatter(partial, ('row', 'half'), scatter_dimension=0, tiled=True)]
  transfers between devices with their start and end apart: 5 -> 7, of which waited for: 4 -> 4; matrix products, arithmetic and copies ran while one was open for 3% -> 3% of each run, Pallas kernels for 4% -> 5%
where the time goes in v7:
time: 176 us; the launch traced here: 175 us
  waiting for transfers between devices  62.6 us (36%)
  blocking collectives  49.3 us (28%)
  Pallas kernels  24.8 us (14%)
  between operations  17.1 us (10%)
  starting transfers between devices  13.5 us (8%)
  local copies, waits for them, and re-layouts  4.84 us (3%)
  other arithmetic  2.5 us (1%)
    all_gather x1, blocking collectives, local(): stats = lax.all_gather(stats, 'mp', axis=1, tiled=True)  35.3 us
    all_gather x1, waiting for transfers between devices, local(): value_weight = lax.all_gather(value_cut, 'tower', axis=0, tiled=False)  34.3 us
    all_to_all x1, waiting for transfers between devices, local(): pieces = lax.all_to_all(pieces, ('half', 'mp'), 0, 0, tiled=True)  15.1 us
    all_gather x1, blocking collectives, local(): lax.all_gather(block_rows.reshape(-1, channels), 'mp', axis=0, tiled=True)  14 us
    pallas_call x2, Pallas kernels, kv_partial(): pl.pallas_call(functools.partial(kv_kernel, pair), grid=(groups,), in_spe...  8.6 us
    all_to_all x1, waiting for transfers between devices, local(): payload = lax.all_to_all(payload, ('row', 'half'), 0, 0, tiled=True)  7.79 us
    all_to_all x1, starting transfers between devices, local(): payload = lax.all_to_all(payload, ('row', 'half'), 0, 0, tiled=True)  6.83 us
    pallas_call x1, Pallas kernels, project(): pl.pallas_call(project_kernel, grid=(groups,), in_specs=[pl.BlockSpec((co...  5.98 us
  transfers between devices with their start and end apart: 7, of which 4 were waited for; matrix products, arithmetic and copies ran while one was open for 3% of the time, Pallas kernels for 5%

profile of v7, /device:TPU:1, one launch (start us, length us, event | category | flops | bytes accessed | tf_op | source)
XLA Modules:
  0.0 175.0 jit_solution(6855977767838511249)
XLA Ops:
  7.4 4.0 %shard_map.136 = (bf16[4,8,8,384]{3,2,1,0:T(8,128)(2,1)}, f32[2,4,8,8,128]{4,3,2,1,0:T(8,128)}) custom-call(bf16[4,8,8,384]{3,2,1,0:T(8,128)(2,1)} %tile_ref.1, f32[7,7,384]{2,1,0:T(8,128)} %weight_ref.2, f32[384]{0:T(512)} %shift_ref.1, f32[384]{0:T(512)} %gain_ref.1), custom_call_target="tpu_custom_call" | custom-call | tf_op jit(solution)/shard_map/pallas_call | solution.py:64
  11.4 14.0 %all_gather.18.rows_ref = bf16[1024,384]{1,0:T(8,128)(2,1)} all-gather(bf16[256,384]{1,0:T(8,128)(2,1)} %bitcast.39), channel_id=1, replica_groups=mesh['tower'=16,'row'=4,'half'=2,'mp'=4] {'mp'}, dimensions={0}, use_global_device_ids=true | all-gather | bytes 983040 | tf_op jit(solution)/shard_map/all_gather | solution.py:310
  25.4 6.0 %shard_map.137 = bf16[8,256,1024]{2,1,0:T(8,128)(2,1)} custom-call(bf16[1024,384]{1,0:T(8,128)(2,1)} %all_gather.18.rows_ref, bf16[384,2048]{1,0:T(8,128)(2,1)} %weight_ref.3), custom_call_target="tpu_custom_call" | custom-call | tf_op jit(solution)/shard_map/pallas_call | solution.py:126
  31.5 0.9 copy-done.4
  32.4 0.8 collective-permute-start
  33.3 0.6 copy-done.5
  34.0 0.7 collective-permute-start.1
  34.7 0.6 copy-done.6
  36.1 0.2 select_reduce_fusion
  36.2 0.6 multiply_reduce_fusion
  37.6 0.3 fusion.1
  38.0 0.1 slice_reduce_fusion
  38.1 0.1 reshape_squeeze.3
  38.2 35.3 %all_gather.19 = f32[2,1024]{1,0:T(2,128)S(1)} all-gather(f32[2,256]{1,0:T(2,128)S(1)} %reshape_squeeze.3), channel_id=1, replica_groups=mesh['tower'=16,'row'=4,'half'=2,'mp'=4] {'mp'}, dimensions={1}, use_global_device_ids=true | all-gather | bytes 10240 | tf_op jit(solution)/shard_map/all_gather | solution.py:342
  73.6 0.8 all_to_all.11
  74.4 6.8 %all-to-all-start = ((f32[8,1,2560]{2,1,0:T(1,128)}), f32[8,1,2560]{2,1,0:T(1,128)S(1)}, u32[]{:S(2)}, u32[]{:S(2)}) async-start(f32[8,1,2560]{2,1,0:T(1,128)} %all_to_all.11), calls=%async_computation.1 | async-start | bytes 163840 | tf_op jit(solution)/shard_map/all_to_all | solution.py:353
  81.3 0.6 constant_dynamic-slice_fusion
  81.9 7.8 %all-to-all-done = f32[8,1,2560]{2,1,0:T(1,128)S(1)} async-done(((f32[8,1,2560]{2,1,0:T(1,128)}), f32[8,1,2560]{2,1,0:T(1,128)S(1)}, u32[]{:S(2)}, u32[]{:S(2)}) %all-to-all-start) | async-done | bytes 81952 | tf_op jit(solution)/shard_map/all_to_all | solution.py:353
  89.7 0.6 slice_reduce_fusion.1
  90.3 0.6 add.52.bias_ref
  90.9 0.6 fusion.10
  91.5 5.3 %reduce-scatter.2.cloned.1.call-done = bf16[1,256,1024]{2,1,0:T(8,128)(2,1)} async-done(((bf16[8,256,1024]{2,1,0:T(8,128)(2,1)}), bf16[1,256,1024]{2,1,0:T(8,128)(2,1)}) %reduce-scatter.2.cloned.1.call-update) | async-done | bytes 524304 | tf_op jit(solution)/shard_map/reduce_scatter | solution.py:313
  96.8 5.0 %shard_map.138 = (bf16[272,1024]{1,0:T(8,128)(2,1)}, f32[8,256]{1,0:T(8,128)}) custom-call(bf16[256,1024]{1,0:T(8,128)(2,1)} %bitcast.35, f32[8,256]{1,0:T(8,128)} %get-tuple-element.38.means_ref, f32[8,256]{1,0:T(8,128)} %get-tuple-element.37.squares_ref, f32[8,1024]{1,0:T(8,128)} %get-tuple-element.36.gains_ref, f32[1,1024]{1,0:T(1,128)} %add.52.bias_ref, ...), custom_call_target="tpu_custom_call" | custom-call | tf_op jit(solution)/shard_map/pallas_call | solution.py:183
  101.9 4.3 %shard_map.139.refs_0_ = bf16[2,4,144,512]{3,2,1,0:T(8,128)(2,1)} custom-call(bf16[272,1024]{1,0:T(8,128)(2,1)} %get-tuple-element.29.rows_ref, f32[8,256]{1,0:T(8,128)} %get-tuple-element.30.sums_ref, bf16[16,256,256]{2,1,0:T(8,128)(2,1)} %bitcast.34), custom_call_target="tpu_custom_call" | custom-call | tf_op jit(solution)/shard_map/pallas_call | solution.py:234
  106.1 34.3 %all-gather.5.cloned.1.call-done = bf16[4096,256]{1,0:T(8,128)(2,1)} async-done(((bf16[256,256]{1,0:T(8,128)(2,1)}), bf16[4096,256]{1,0:T(8,128)(2,1)}) %all-gather.5.cloned.1.call-update) | async-done | bytes 2097168 | tf_op jit(solution)/shard_map/all_gather | solution.py:331
  140.4 4.3 %shard_map.140 = bf16[2,4,144,512]{3,2,1,0:T(8,128)(2,1)} custom-call(bf16[272,1024]{1,0:T(8,128)(2,1)} %get-tuple-element.29.rows_ref, f32[8,256]{1,0:T(8,128)} %get-tuple-element.30.sums_ref, bf16[16,256,256]{2,1,0:T(8,128)(2,1)} %bitcast.33, bf16[2,4,144,512]{3,2,1,0:T(8,128)(2,1)} %shard_map.139.refs_0_), custom_call_target="tpu_custom_call", output_to_operand_aliasing={{}: (3, {})} | custom-call | tf_op jit(solution)/shard_map/pallas_call | solution.py:234
  144.8 5.1 %all-to-all-start.1 = ((bf16[8,144,512]{2,1,0:T(8,128)(2,1)}), bf16[8,144,512]{2,1,0:T(8,128)(2,1)S(1)}, u32[]{:S(2)}, u32[]{:S(2)}) async-start(bf16[8,144,512]{2,1,0:T(8,128)(2,1)} %bitcast.32), calls=%async_computation.2 | async-start | bytes 2359296 | tf_op jit(solution)/shard_map/all_to_all | solution.py:395
  150.5 0.3 fusion
  151.0 0.1 copy.22.cosine_ref
  151.1 0.1 pad_maximum_fusion.1.sine_ref
  151.2 15.1 %all-to-all-done.1.pieces_ref = bf16[8,144,512]{2,1,0:T(8,128)(2,1)S(1)} async-done(((bf16[8,144,512]{2,1,0:T(8,128)(2,1)}), bf16[8,144,512]{2,1,0:T(8,128)(2,1)S(1)}, u32[]{:S(2)}, u32[]{:S(2)}) %all-to-all-start.1) | async-done | bytes 1179680 | tf_op jit(solution)/shard_map/all_to_all | solution.py:395
  166.3 1.2 shard_map.141
  (53 shorter events, 0.6 us)
Async XLA Ops:
  7.4 89.5 %reduce-scatter.2.cloned.1.call-start = ((), (), s32[]{:S(2)}) async-start(), calls=%async_computation.3 | async-start | bytes 4718592 | tf_op jit(solution)/shard_map/reduce_scatter | solution.py:313
  31.4 1.0 copy-start.4
  31.4 4.0 %copy-start.8 = (f32[2048]{0:T(1024)S(1)}, f32[2048]{0:T(1024)}, u32[]{:S(2)}) copy-start(f32[2048]{0:T(1024)} %param.20) | copy-start | bytes 24580
  31.4 4.7 %copy-start.2 = (f32[16,8192]{1,0:T(8,128)S(1)}, f32[16,8192]{1,0:T(8,128)}, u32[]{:S(2)}) copy-start(f32[16,8192]{1,0:T(8,128)} %param.21) | copy-start | bytes 1572868
  31.4 6.2 %copy-start.10 = (f32[384]{0:T(512)S(1)}, f32[384]{0:T(512)}, u32[]{:S(2)}) copy-start(f32[384]{0:T(512)} %param.18) | copy-start | bytes 4612
  31.4 6.2 %copy-start.7 = (f32[384]{0:T(512)S(1)}, f32[384]{0:T(512)}, u32[]{:S(2)}) copy-start(f32[384]{0:T(512)} %gain_ref.1) | copy-start | bytes 4612
  31.4 6.2 %copy-start.1 = (bf16[384,2048]{1,0:T(8,128)(2,1)S(1)}, bf16[384,2048]{1,0:T(8,128)(2,1)}, u32[]{:S(2)}) copy-start(bf16[384,2048]{1,0:T(8,128)(2,1)} %weight_ref.3) | copy-start | bytes 4718596
  31.4 70.4 %all-gather.7.cloned.1.call-start = ((), (), s32[]{:S(2)}) async-start(), calls=%async_computation.5 | async-start | bytes 2228224 | tf_op jit(solution)/shard_map/all_gather | solution.py:326
  32.4 5.6 %copy-start.3 = (f32[2,4,8,8,128]{4,3,2,1,0:T(8,128)S(1)}, f32[2,4,8,8,128]{4,3,2,1,0:T(8,128)}, u32[]{:S(2)}) copy-start(f32[2,4,8,8,128]{4,3,2,1,0:T(8,128)} %get-tuple-element.26) | copy-start | bytes 786436
  32.4 0.8 collective-permute-start
  33.3 0.7 copy-start.5
  33.9 106.5 %all-gather.5.cloned.1.call-start = ((), (), s32[]{:S(2)}) async-start(), calls=%async_computation.4 | async-start | bytes 2228224 | tf_op jit(solution)/shard_map/all_gather | solution.py:331
  34.0 0.7 collective-permute-start.1
  34.7 0.7 copy-start.6
  36.1 45.2 %copy-start.9 = (f32[2048]{0:T(1024)S(1)}, f32[2048]{0:T(1024)}, u32[]{:S(2)}) copy-start(f32[2048]{0:T(1024)} %param.25) | copy-start | bytes 24580
  74.4 15.3 %all-to-all-start = ((f32[8,1,2560]{2,1,0:T(1,128)}), f32[8,1,2560]{2,1,0:T(1,128)S(1)}, u32[]{:S(2)}, u32[]{:S(2)}) async-start(f32[8,1,2560]{2,1,0:T(1,128)} %all_to_all.11), calls=%async_computation.1 | async-start | bytes 163840 | tf_op jit(solution)/shard_map/all_to_all | solution.py:353
  144.7 5.8 %copy-start.11 = (s32[1,128]{1,0:T(1,128)S(1)}, s32[1,128]{1,0:T(1,128)}, u32[]{:S(2)}) copy-start(s32[1,128]{1,0:T(1,128)} %param.24) | copy-start | bytes 1540
  144.8 21.6 %copy-start = (f32[2,256]{1,0:T(2,128)S(1)}, f32[2,256]{1,0:T(2,128)}, u32[]{:S(2)}) copy-start(f32[2,256]{1,0:T(2,128)} %bias_ref.1) | copy-start | bytes 6148
  144.8 21.5 %all-to-all-start.1 = ((bf16[8,144,512]{2,1,0:T(8,128)(2,1)}), bf16[8,144,512]{2,1,0:T(8,128)(2,1)S(1)}, u32[]{:S(2)}, u32[]{:S(2)}) async-start(bf16[8,144,512]{2,1,0:T(8,128)(2,1)} %bitcast.32), calls=%async_computation.2 | async-start | bytes 2359296 | tf_op jit(solution)/shard_map/all_to_all | solution.py:395
Sparse Core Ops, SparseCore 0:
  31.6 65.2 reduce-scatter.1
Sparse Core Ops, SparseCore 1:
  34.0 63.2 all-gather.6
  99.2 41.1 all-gather.4

commit v8 on v6

--- a/solution.py
+++ b/solution.py
@@ -15,45 +15,49 @@
 epsilon = 1e-06
 
 
+TILES = 4
+
+
 def conv_kernel(tile_ref, weight_ref, shift_ref, gain_ref, rows_ref, stats_ref, held):
-    _, cells, width, channels = tile_ref.shape
+    count, cells, width, channels = tile_ref.shape
     side = weight_ref.shape[0]
     reach = side // 2
     lanes = 128
-    total = jnp.zeros((cells, width, 1), jnp.float32)
     column = lax.broadcasted_iota(jnp.int32, (cells, width, lanes), 1)
-    for group in range(channels // lanes):
-        part = slice(group * lanes, (group + 1) * lanes)
-        cell = tile_ref[0, :, :, part].astype(jnp.float32)
-        sums = [
-            jnp.broadcast_to(shift_ref[part][None], (width, lanes)) for _ in range(cells)
-        ]
-        for col_off in range(side):
-            move = col_off - reach
-            moved = cell
-            if move:
-                inside = (column + move >= 0) & (column + move < width)
-                moved = jnp.where(inside, pltpu.roll(cell, (-move) % width, 1), 0.0)
-            for row_off in range(side):
-                scale = jnp.broadcast_to(
-                    weight_ref[row_off, col_off : col_off + 1, part], (width, lanes)
-                )
-                for row in range(cells):
-                    source = row + row_off - reach
-                    if 0 <= source < cells:
-                        sums[row] = sums[row] + moved[source] * scale
-        out = jnp.stack(sums)
-        held[:, :, part] = out
-        total = total + jnp.sum(out, -1, keepdims=True)
-    average = total / channels
-    square = jnp.zeros((cells, width, 1), jnp.float32)
-    for group in range(channels // lanes):
-        part = slice(group * lanes, (group + 1) * lanes)
-        centered = held[:, :, part] - average
-        square = square + jnp.sum(centered * centered, -1, keepdims=True)
-        rows_ref[0, :, :, part] = (centered * gain_ref[part]).astype(rows_ref.dtype)
-    stats_ref[0, 0] = jnp.broadcast_to(average, (cells, width, lanes))
-    stats_ref[1, 0] = jnp.broadcast_to(square, (cells, width, lanes))
+    for tile in range(count):
+        total = jnp.zeros((cells, width, 1), jnp.float32)
+        for group in range(channels // lanes):
+            part = slice(group * lanes, (group + 1) * lanes)
+            cell = tile_ref[tile, :, :, part].astype(jnp.float32)
+            sums = [
+                jnp.broadcast_to(shift_ref[part][None], (width, lanes)) for _ in range(cells)
+            ]
+            for col_off in range(side):
+                move = col_off - reach
+                moved = cell
+                if move:
+                    inside = (column + move >= 0) & (column + move < width)
+                    moved = jnp.where(inside, pltpu.roll(cell, (-move) % width, 1), 0.0)
+                for row_off in range(side):
+                    scale = jnp.broadcast_to(
+                        weight_ref[row_off, col_off : col_off + 1, part], (width, lanes)
+                    )
+                    for row in range(cells):
+                        source = row + row_off - reach
+                        if 0 <= source < cells:
+                            sums[row] = sums[row] + moved[source] * scale
+            out = jnp.stack(sums)
+            held[:, :, part] = out
+            total = total + jnp.sum(out, -1, keepdims=True)
+        average = total / channels
+        square = jnp.zeros((cells, width, 1), jnp.float32)
+        for group in range(channels // lanes):
+            part = slice(group * lanes, (group + 1) * lanes)
+            centered = held[:, :, part] - average
+            square = square + jnp.sum(centered * centered, -1, keepdims=True)
+            rows_ref[tile, :, :, part] = (centered * gain_ref[part]).astype(rows_ref.dtype)
+        stats_ref[0, tile] = jnp.broadcast_to(average, (cells, width, lanes))
+        stats_ref[1, tile] = jnp.broadcast_to(square, (cells, width, lanes))
 
 
 def conv_rows(tiles, kernel, shift, gain):
@@ -61,16 +65,16 @@
     whole = pl.BlockSpec((channels,), lambda t: (0,))
     return pl.pallas_call(
         conv_kernel,
-        grid=(count,),
+        grid=(count // TILES,),
         in_specs=[
-            pl.BlockSpec((1, cells, width, channels), lambda t: (t, 0, 0, 0)),
+            pl.BlockSpec((TILES, cells, width, channels), lambda t: (t, 0, 0, 0)),
             pl.BlockSpec(kernel.shape, lambda t: (0, 0, 0)),
             whole,
             whole,
         ],
         out_specs=[
-            pl.BlockSpec((1, cells, width, channels), lambda t: (t, 0, 0, 0)),
-            pl.BlockSpec((2, 1, cells, width, 128), lambda t: (0, t, 0, 0, 0)),
+            pl.BlockSpec((TILES, cells, width, channels), lambda t: (t, 0, 0, 0)),
+            pl.BlockSpec((2, TILES, cells, width, 128), lambda t: (0, t, 0, 0, 0)),
         ],
         out_shape=[
             jax.ShapeDtypeStruct(tiles.shape, jnp.bfloat16),
@@ -106,29 +110,34 @@
 
 
 def project_kernel(rows_ref, weight_ref, out_ref):
-    halves, _, columns = out_ref.shape
+    chunks, count, columns = out_ref.shape
+    parts = rows_ref.shape[0] // count
+    halves = chunks // parts
     width = columns // INNER
-    for half in range(halves):
-        for block in range(INNER):
-            begin = (block * halves + half) * width
-            out_ref[half, :, block * width : (block + 1) * width] = jnp.dot(
-                rows_ref[...],
-                weight_ref[:, begin : begin + width],
-                preferred_element_type=jnp.float32,
-            ).astype(out_ref.dtype)
+    for part in range(parts):
+        for half in range(halves):
+            for block in range(INNER):
+                begin = (block * halves + half) * width
+                out_ref[part * halves + half, :, block * width : (block + 1) * width] = jnp.dot(
+                    rows_ref[part * count : (part + 1) * count, :],
+                    weight_ref[:, begin : begin + width],
+                    preferred_element_type=jnp.float32,
+                ).astype(out_ref.dtype)
 
 
 def project(rows, weight, groups, halves):
     count, depth = rows.shape
     columns = weight.shape[1]
+    parts = 2
+    chunks = parts * halves
     return pl.pallas_call(
         project_kernel,
-        grid=(groups,),
+        grid=(groups // parts,),
         in_specs=[
-            pl.BlockSpec((count // groups, depth), lambda g: (g, 0)),
+            pl.BlockSpec((count // groups * parts, depth), lambda g: (g, 0)),
             pl.BlockSpec(weight.shape, lambda g: (0, 0)),
         ],
-        out_specs=pl.BlockSpec((halves, count // groups, columns // halves), lambda g: (g, 0, 0)),
+        out_specs=pl.BlockSpec((chunks, count // groups, columns // halves), lambda g: (g, 0, 0)),
         out_shape=jax.ShapeDtypeStruct(
             (groups * halves, count // groups, columns // halves), jnp.bfloat16
         ),

time: 142 us -> 141 us (level)
  Pallas kernels: 21.4 us -> 19.9 us
    pallas_call x2, Pallas kernels: 10.1 us -> 8.64 us  [the longest x1 5.41 us: project(): pl.pallas_call(project_kernel, grid=(groups // parts,), in_specs=[pl.Bloc...]
where the time goes in v8:
time: 141 us; the launch traced here: 140 us
  blocking collectives  49.2 us (35%)
  waiting for transfers between devices  35.2 us (25%)
  Pallas kernels  19.9 us (14%)
  between operations  17.1 us (12%)
  starting transfers between devices  12.7 us (9%)
  local copies, waits for them, and re-layouts  3.37 us (2%)
  other arithmetic  2.48 us (2%)
    all_gather x1, blocking collectives, local(): stats = lax.all_gather(stats, 'mp', axis=1, tiled=True)  35.2 us
    all_to_all x1, waiting for transfers between devices, local(): pieces = lax.all_to_all(pieces, ('half', 'mp'), 0, 0, tiled=True)  15.1 us
    all_gather x1, blocking collectives, local(): lax.all_gather(block_rows.reshape(-1, channels), 'mp', axis=0, tiled=True)  14 us
    all_to_all x1, waiting for transfers between devices, local(): payload = lax.all_to_all(payload, ('row', 'half'), 0, 0, tiled=True)  7.79 us
    reduce_scatter x1, waiting for transfers between devices, local(): lax.psum_scatter(partial, ('row', 'half'), scatter_dimension=0, tiled=True)  7.77 us
    all_to_all x1, starting transfers between devices, local(): payload = lax.all_to_all(payload, ('row', 'half'), 0, 0, tiled=True)  6.81 us
    pallas_call x1, Pallas kernels, project(): pl.pallas_call(project_kernel, grid=(groups // parts,), in_specs=[pl.Bloc...  5.41 us
    pallas_call x1, Pallas kernels, kv_partial(): pl.pallas_call(kv_kernel, grid=(groups,), in_specs=[pl.BlockSpec(rows.sha...  5.04 us
  transfers between devices with their start and end apart: 5, of which 4 were waited for; matrix products, arithmetic and copies ran while one was open for 3% of the time, Pallas kernels for 4%

profile of v8, /device:TPU:1, one launch (start us, length us, event | category | flops | bytes accessed | tf_op | source)
XLA Modules:
  0.0 140.3 jit_solution(12624489942576248461)
XLA Ops:
  7.4 3.2 %shard_map.136 = (bf16[4,8,8,384]{3,2,1,0:T(8,128)(2,1)}, f32[2,4,8,8,128]{4,3,2,1,0:T(8,128)}) custom-call(bf16[4,8,8,384]{3,2,1,0:T(8,128)(2,1)} %tile_ref.1, f32[7,7,384]{2,1,0:T(8,128)} %weight_ref.2, f32[384]{0:T(512)} %shift_ref.1, f32[384]{0:T(512)} %gain_ref.1), custom_call_target="tpu_custom_call" | custom-call | tf_op jit(solution)/shard_map/pallas_call | solution.py:66
  10.6 14.0 %all_gather.12.rows_ref = bf16[1024,384]{1,0:T(8,128)(2,1)} all-gather(bf16[256,384]{1,0:T(8,128)(2,1)} %bitcast.33), channel_id=1, replica_groups=mesh['tower'=16,'row'=4,'half'=2,'mp'=4] {'mp'}, dimensions={0}, use_global_device_ids=true | all-gather | bytes 983040 | tf_op jit(solution)/shard_map/all_gather | solution.py:310
  24.6 5.4 %shard_map.137 = bf16[8,256,1024]{2,1,0:T(8,128)(2,1)} custom-call(bf16[1024,384]{1,0:T(8,128)(2,1)} %all_gather.12.rows_ref, bf16[384,2048]{1,0:T(8,128)(2,1)} %weight_ref.3), custom_call_target="tpu_custom_call" | custom-call | tf_op jit(solution)/shard_map/pallas_call | solution.py:133
  30.1 0.0 reduce-scatter.2.cloned.1.call-update
  30.1 0.0 all-gather.3.cloned.1.call-start
  30.2 0.8 collective-permute-start
  31.0 0.7 copy-done.5
  32.5 0.2 select_reduce_fusion
  32.7 0.6 multiply_reduce_fusion
  34.1 0.3 fusion.1
  34.4 0.1 slice_reduce_fusion
  34.6 0.1 reshape_squeeze.3
  34.7 35.2 %all_gather.13 = f32[2,1024]{1,0:T(2,128)S(1)} all-gather(f32[2,256]{1,0:T(2,128)S(1)} %reshape_squeeze.3), channel_id=1, replica_groups=mesh['tower'=16,'row'=4,'half'=2,'mp'=4] {'mp'}, dimensions={1}, use_global_device_ids=true | all-gather | bytes 10240 | tf_op jit(solution)/shard_map/all_gather | solution.py:338
  70.0 0.8 all_to_all.11
  70.8 6.8 %all-to-all-start = ((f32[8,1,2560]{2,1,0:T(1,128)}), f32[8,1,2560]{2,1,0:T(1,128)S(1)}, u32[]{:S(2)}, u32[]{:S(2)}) async-start(f32[8,1,2560]{2,1,0:T(1,128)} %all_to_all.11), calls=%async_computation.1 | async-start | bytes 163840 | tf_op jit(solution)/shard_map/all_to_all | solution.py:349
  77.6 0.6 constant_dynamic-slice_fusion
  78.2 7.8 %all-to-all-done = f32[8,1,2560]{2,1,0:T(1,128)S(1)} async-done(((f32[8,1,2560]{2,1,0:T(1,128)}), f32[8,1,2560]{2,1,0:T(1,128)S(1)}, u32[]{:S(2)}, u32[]{:S(2)}) %all-to-all-start) | async-done | bytes 81952 | tf_op jit(solution)/shard_map/all_to_all | solution.py:349
  86.0 0.6 slice_reduce_fusion.1
  86.6 0.6 add.52.bias_ref
  87.2 0.6 fusion.10
  87.8 7.8 %reduce-scatter.2.cloned.1.call-done = bf16[1,256,1024]{2,1,0:T(8,128)(2,1)} async-done(((bf16[8,256,1024]{2,1,0:T(8,128)(2,1)}), bf16[1,256,1024]{2,1,0:T(8,128)(2,1)}) %reduce-scatter.2.cloned.1.call-update) | async-done | bytes 524304 | tf_op jit(solution)/shard_map/reduce_scatter | solution.py:313
  95.6 5.0 %shard_map.138 = (bf16[272,1024]{1,0:T(8,128)(2,1)}, f32[8,256]{1,0:T(8,128)}) custom-call(bf16[256,1024]{1,0:T(8,128)(2,1)} %bitcast.29, f32[8,256]{1,0:T(8,128)} %get-tuple-element.28.means_ref, f32[8,256]{1,0:T(8,128)} %get-tuple-element.27.squares_ref, f32[8,1024]{1,0:T(8,128)} %get-tuple-element.26.gains_ref, f32[1,1024]{1,0:T(1,128)} %add.52.bias_ref, ...), custom_call_target="tpu_custom_call" | custom-call | tf_op jit(solution)/shard_map/pallas_call | solution.py:190
  100.6 4.5 %all-gather.3.cloned.1.call-done = bf16[32,256,256]{2,1,0:T(8,128)(2,1)} async-done(((bf16[2,256,256]{2,1,0:T(8,128)(2,1)}), bf16[32,256,256]{2,1,0:T(8,128)(2,1)}) %all-gather.3.cloned.1.call-update) | async-done | bytes 4194320 | tf_op jit(solution)/shard_map/all_gather | solution.py:327
  105.1 5.0 %shard_map.139 = bf16[2,4,144,512]{3,2,1,0:T(8,128)(2,1)} custom-call(bf16[272,1024]{1,0:T(8,128)(2,1)} %get-tuple-element.22.rows_ref, f32[8,256]{1,0:T(8,128)} %get-tuple-element.23.sums_ref, bf16[16,2,256,256]{3,2,1,0:T(8,128)(2,1)} %bitcast.28), custom_call_target="tpu_custom_call" | custom-call | tf_op jit(solution)/shard_map/pallas_call | solution.py:231
  110.1 5.0 %all-to-all-start.1 = ((bf16[8,144,512]{2,1,0:T(8,128)(2,1)}), bf16[8,144,512]{2,1,0:T(8,128)(2,1)S(1)}, u32[]{:S(2)}, u32[]{:S(2)}) async-start(bf16[8,144,512]{2,1,0:T(8,128)(2,1)} %bitcast.27), calls=%async_computation.2 | async-start | bytes 2359296 | tf_op jit(solution)/shard_map/all_to_all | solution.py:390
  115.8 0.3 fusion
  116.2 0.1 copy.20
  116.3 0.1 copy.21.cosine_ref
  116.4 0.1 pad_maximum_fusion.1.sine_ref
  116.5 15.1 %all-to-all-done.1.pieces_ref = bf16[8,144,512]{2,1,0:T(8,128)(2,1)S(1)} async-done(((bf16[8,144,512]{2,1,0:T(8,128)(2,1)}), bf16[8,144,512]{2,1,0:T(8,128)(2,1)S(1)}, u32[]{:S(2)}, u32[]{:S(2)}) %all-to-all-start.1) | async-done | bytes 1179680 | tf_op jit(solution)/shard_map/all_to_all | solution.py:390
  131.5 0.1 broadcast_in_dim.42.valid_ref
  131.6 1.2 shard_map.140
  (45 shorter events, 0.4 us)
Async XLA Ops:
  7.4 22.8 %copy-start = (bf16[2,512,256]{2,1,0:T(8,128)(2,1)S(1)}, bf16[2,512,256]{2,1,0:T(8,128)(2,1)}, u32[]{:S(2)}) copy-start(bf16[2,512,256]{2,1,0:T(8,128)(2,1)} %param.26) | copy-start | bytes 1572868
  7.4 88.2 %reduce-scatter.2.cloned.1.call-start = ((), (), s32[]{:S(2)}) async-start(), calls=%async_computation.3 | async-start | bytes 4718592 | tf_op jit(solution)/shard_map/reduce_scatter | solution.py:313
  30.0 1.8 %copy-start.7 = (f32[2048]{0:T(1024)S(1)}, f32[2048]{0:T(1024)}, u32[]{:S(2)}) copy-start(f32[2048]{0:T(1024)} %param.20) | copy-start | bytes 24580
  30.0 2.4 %copy-start.3 = (f32[16,8192]{1,0:T(8,128)S(1)}, f32[16,8192]{1,0:T(8,128)}, u32[]{:S(2)}) copy-start(f32[16,8192]{1,0:T(8,128)} %param.21) | copy-start | bytes 1572868
  30.0 4.0 %copy-start.9 = (f32[384]{0:T(512)S(1)}, f32[384]{0:T(512)}, u32[]{:S(2)}) copy-start(f32[384]{0:T(512)} %param.18) | copy-start | bytes 4612
  30.0 4.0 %copy-start.6 = (f32[384]{0:T(512)S(1)}, f32[384]{0:T(512)}, u32[]{:S(2)}) copy-start(f32[384]{0:T(512)} %gain_ref.1) | copy-start | bytes 4612
  30.1 4.0 %copy-start.2 = (bf16[384,2048]{1,0:T(8,128)(2,1)S(1)}, bf16[384,2048]{1,0:T(8,128)(2,1)}, u32[]{:S(2)}) copy-start(bf16[384,2048]{1,0:T(8,128)(2,1)} %weight_ref.3) | copy-start | bytes 4718596
  30.1 75.0 %all-gather.3.cloned.1.call-start = ((), (), s32[]{:S(2)}) async-start(), calls=%async_computation.4 | async-start | bytes 4456448 | tf_op jit(solution)/shard_map/all_gather | solution.py:327
  30.2 4.3 %copy-start.4 = (f32[2,4,8,8,128]{4,3,2,1,0:T(8,128)S(1)}, f32[2,4,8,8,128]{4,3,2,1,0:T(8,128)}, u32[]{:S(2)}) copy-start(f32[2,4,8,8,128]{4,3,2,1,0:T(8,128)} %get-tuple-element.19) | copy-start | bytes 786436
  30.2 0.8 collective-permute-start
  31.0 0.7 copy-start.5
  32.5 45.1 %copy-start.8 = (f32[2048]{0:T(1024)S(1)}, f32[2048]{0:T(1024)}, u32[]{:S(2)}) copy-start(f32[2048]{0:T(1024)} %param.25) | copy-start | bytes 24580
  70.8 15.3 %all-to-all-start = ((f32[8,1,2560]{2,1,0:T(1,128)}), f32[8,1,2560]{2,1,0:T(1,128)S(1)}, u32[]{:S(2)}, u32[]{:S(2)}) async-start(f32[8,1,2560]{2,1,0:T(1,128)} %all_to_all.11), calls=%async_computation.1 | async-start | bytes 163840 | tf_op jit(solution)/shard_map/all_to_all | solution.py:349
  110.1 5.7 %copy-start.10 = (s32[1,128]{1,0:T(1,128)S(1)}, s32[1,128]{1,0:T(1,128)}, u32[]{:S(2)}) copy-start(s32[1,128]{1,0:T(1,128)} %param.24) | copy-start | bytes 1540
  110.1 21.5 %copy-start.1 = (f32[2,256]{1,0:T(2,128)S(1)}, f32[2,256]{1,0:T(2,128)}, u32[]{:S(2)}) copy-start(f32[2,256]{1,0:T(2,128)} %bias_ref.1) | copy-start | bytes 6148
  110.1 21.4 %all-to-all-start.1 = ((bf16[8,144,512]{2,1,0:T(8,128)(2,1)}), bf16[8,144,512]{2,1,0:T(8,128)(2,1)S(1)}, u32[]{:S(2)}, u32[]{:S(2)}) async-start(bf16[8,144,512]{2,1,0:T(8,128)(2,1)} %bitcast.27), calls=%async_computation.2 | async-start | bytes 2359296 | tf_op jit(solution)/shard_map/all_to_all | solution.py:390
Sparse Core Ops, SparseCore 0:
  30.2 65.3 reduce-scatter.1
Sparse Core Ops, SparseCore 1:
  32.7 72.3 all-gather.2
